TPU v7x, 32 devices: a whole 2x2x4 slice. The times are simulated.
32 devices in a mesh: group: 8 (over z, y), expert: 4 (over x, core).
Axes of the slice: x: 2, y: 2, z: 4, core: 2. Of those that a mesh axis runs over, the one named last changes fastest.
Arguments:
- tokens: bfloat16 [2, 2560, 2048], P(None, ('group', 'expert')), may hold values from -6 to 6
- cotangent: bfloat16 [2, 2560, 2048], P(None, ('group', 'expert')), may hold values from -6 to 6
- gain_attn: float32 [2048], replicated, may hold values from 0.5 to 1.5
- gain_mlp: float32 [2048], replicated, may hold values from 0.5 to 1.5
- w_kv: bfloat16 [2048, 4096], P(('group', 'expert')), may hold values from -0.125 to 0.125
- w_query: bfloat16 [4, 2048, 2048], P('expert', 'group'), may hold values from -0.125 to 0.125
- w_out: bfloat16 [4, 2048, 2048], P('expert', 'group'), may hold values from -1 to 1
- w_gate_up: bfloat16 [4, 2048, 11264], P('expert', 'group'), may hold values from -0.125 to 0.125
- w_down: bfloat16 [4, 5632, 2048], P('expert', 'group'), may hold values from -0.078125 to 0.078125
- att_routes: int32 [2, 2560, 2], P(None, 'group'), may hold values from 0 to 3, all different within a row; in each aligned block of 80 rows (0 to 79, 80 to 159, ..., all dimensions but the last counted through in order) at most 50 rows name the same one
- att_gates: float32 [2, 2560, 2], P(None, ('group', 'expert')), may hold values from 0.25 to 0.75
- mlp_routes: int32 [2, 2560, 2], P(None, 'group'), may hold values from 0 to 3, all different within a row; in each aligned block of 80 rows (0 to 79, 80 to 159, ..., all dimensions but the last counted through in order) at most 50 rows name the same one
- mlp_gates: float32 [2, 2560, 2], P(None, ('group', 'expert')), may hold values from 0.25 to 0.75
- blocks: int32 [2, 8, 320], P(None, 'group'), may hold values from 0 to 2, never falling along the last dimension, each value on 1 to 256 neighbouring positions
Outputs:
- output: bfloat16 [2, 2560, 2048], P(None, ('group', 'expert'))
- grad_input: bfloat16 [2, 2560, 2048], P(None, ('group', 'expert'))
- grad_gain_attn: float32 [2048], P(('group', 'expert'))
- grad_gain_mlp: float32 [2048], P(('group', 'expert'))
- grad_kv: float32 [2048, 4096], P(('group', 'expert'))
- grad_query: float32 [4, 2048, 2048], P('expert', 'group')
- grad_out: float32 [4, 2048, 2048], P('expert', 'group')
- grad_gate_up: float32 [4, 2048, 11264], P('expert', 'group')
- grad_down: float32 [4, 5632, 2048], P('expert', 'group')
Inputs may be any that keep to these rules, and one draw needn't show every extreme that they name: `att_routes`: each row names 2 different experts; among the 80 rows of one device in one micro-batch no expert is named more than 50 times. `mlp_routes`: each row names 2 different experts; among the 80 rows of one device in one micro-batch no expert is named more than 50 times. `blocks`: block numbers never fall along a sequence; a block has at most 256 positions.
All inputs are finite; a program needn't handle non-finite values.
Results may differ from a plain program's by a relative error of at most 0.019.
Values may be sent and summed in bfloat16 or wider, within the bound.
A program may use at most 448 MiB of HBM per device.

v0:
```python
import jax
import jax.numpy as jnp
from jax import lax
from jax.sharding import PartitionSpec as P

HEADS = 16
HDIM = 128
CAP = 50


EPS = 1e-06
HIGH = lax.Precision.HIGHEST


def angles(positions):
    half = HDIM // 2
    freq = 10000.0 ** (-jnp.arange(half, dtype=jnp.float32) / half)
    turn = positions.astype(jnp.float32)[:, None] * freq[None, :]
    return (jnp.cos(turn), jnp.sin(turn))


def rotate(values, cosine, sine):
    count = values.shape[0]
    split = values.reshape(count, HEADS, 2, HDIM // 2)
    first = split[:, :, 0]
    second = split[:, :, 1]
    cosine = cosine[:, None, :]
    sine = sine[:, None, :]
    turned = jnp.stack([first * cosine - second * sine, second * cosine + first * sine], axis=2)
    return turned.reshape(count, HEADS * HDIM)


def routing(routes, gates, block_ids, owner, experts):
    local = routes.shape[0] // experts
    per = routes.reshape(experts, local, routes.shape[1])
    flat = per.reshape(experts, -1)
    ids = jnp.arange(experts, dtype=jnp.int32)
    onehot = (flat[:, :, None] == ids[None, None, :]).astype(jnp.int32)
    before = jnp.cumsum(onehot, axis=1) - onehot
    slots = jnp.sum(before * onehot, axis=2).reshape(per.shape)
    places = jnp.arange(CAP, dtype=jnp.int32)
    own_ids = lax.dynamic_index_in_dim(per, owner, 0, keepdims=False)
    own_slots = lax.dynamic_index_in_dim(slots, owner, 0, keepdims=False)
    sent = (
        (own_ids[None, None] == ids[:, None, None, None])
        & (own_slots[None, None] == places[None, :, None, None])
    ).astype(jnp.float32)
    pick = jnp.sum(sent, axis=3)
    weighted = jnp.sum(sent * gates[None, None], axis=3)
    arrived = ((per == owner)[:, None] & (slots[:, None] == places[None, :, None, None])).astype(
        jnp.int32
    )
    length = experts * local
    spots = jnp.arange(length, dtype=jnp.int32).reshape(experts, 1, local, 1)
    marks = block_ids.reshape(experts, 1, local, 1)
    valid = jnp.sum(arrived, axis=(2, 3)).reshape(-1)
    row_pos = jnp.sum(arrived * spots, axis=(2, 3)).reshape(-1)
    row_block = jnp.sum(arrived * marks, axis=(2, 3)).reshape(-1) + (1 - valid) * length
    return (pick, weighted, row_pos, row_block)


def score_block(queries, keys, row_block, key_block):
    count = queries.shape[0]
    raw = jnp.einsum(
        "rhd,khd->hrk",
        queries.reshape(count, HEADS, HDIM),
        keys.reshape(keys.shape[0], HEADS, HDIM),
        preferred_element_type=jnp.float32,
    )
    visible = key_block[None, None, :] <= row_block[None, :, None]
    return jnp.where(visible, raw * HDIM ** (-0.5), -1e30)


def spread(pick, normed):
    return jnp.einsum(
        "ect,td->ecd", pick.astype(jnp.bfloat16), normed, preferred_element_type=jnp.float32
    ).astype(jnp.bfloat16)


def collect(weights, arrived):
    return jnp.einsum("ect,ecd->td", weights, arrived.astype(jnp.float32), precision=HIGH)


def joined_rows(store, chosen, name):
    return jnp.concatenate([store[name][index] for index in chosen], axis=0)


def expert_reduce(store, chosen):
    pairs = (
        ("rows", "query_grad"),
        ("attended", "result_grad"),
        ("rows_two", "both_grad"),
        ("hidden", "down_grad"),
    )
    groups = lax.axis_size("group")
    results = []
    for left_name, right_name in pairs:
        left = joined_rows(store, chosen, left_name)
        right = joined_rows(store, chosen, right_name)

        def term(start, count, left=left, right=right):
            return jnp.einsum("rd,rf->df", left, right, preferred_element_type=jnp.float32)

        shard = lax.psum_scatter(
            term(jnp.int32(0), lax.axis_size("group") * (left.shape[1] // groups)).astype(
                jnp.bfloat16
            ),
            "group",
            scatter_dimension=0,
            tiled=True,
        ).astype(jnp.float32)
        results.append(shard[None])
    return tuple(results)


def reduce_all(store, chosen):
    expert_parts = expert_reduce(store, chosen)
    shared_term = jnp.einsum(
        "td,tf->df",
        joined_rows(store, chosen, "normed"),
        joined_rows(store, chosen, "mixed_grad"),
        preferred_element_type=jnp.float32,
    )
    gain_first = jnp.sum(joined_rows(store, chosen, "gain_first"), axis=0)
    gain_second = jnp.sum(joined_rows(store, chosen, "gain_second"), axis=0)
    shared_parts = (
        lax.psum_scatter(shared_term, ("group", "expert"), scatter_dimension=0, tiled=True),
        lax.psum_scatter(gain_first, ("group", "expert"), scatter_dimension=0, tiled=True),
        lax.psum_scatter(gain_second, ("group", "expert"), scatter_dimension=0, tiled=True),
    )
    return tuple(expert_parts) + tuple(shared_parts)


def on_device(
    tokens,
    cotangent,
    gain_attn,
    gain_mlp,
    w_kv,
    w_query,
    w_out,
    w_gate_up,
    w_down,
    att_routes,
    att_gates,
    mlp_routes,
    mlp_gates,
    blocks,
):
    experts = lax.axis_size("expert")
    owner = lax.axis_index("expert")
    shared_full = lax.all_gather(w_kv, ("group", "expert"), axis=0, tiled=True)
    gathered = (
        lax.all_gather(w_query, "group", axis=1, tiled=True),
        lax.all_gather(w_out, "group", axis=1, tiled=True),
        lax.all_gather(w_gate_up, "group", axis=1, tiled=True),
        lax.all_gather(w_down, "group", axis=1, tiled=True),
    )
    query_full = gathered[0][0]
    output_full = gathered[1][0]
    gate_up_full = gathered[2][0]
    down_full = gathered[3][0]
    micro = tokens.shape[0]
    local = tokens.shape[1]
    model = tokens.shape[2]
    length = local * experts
    width = HEADS * HDIM
    hidden_width = gate_up_full.shape[1] // 2
    own_cos, own_sin = angles(owner * local + jnp.arange(local, dtype=jnp.int32))
    names = (
        "rows",
        "query_grad",
        "attended",
        "result_grad",
        "rows_two",
        "both_grad",
        "hidden",
        "down_grad",
        "normed",
        "mixed_grad",
        "gain_first",
        "gain_second",
    )
    store = {name: [] for name in names}
    outputs = []
    input_grads = []
    for index in range(micro):
        inputs = tokens[index].astype(jnp.float32)
        block_ids = blocks[index, 0]
        att_pick, att_weight, row_pos, row_block = routing(
            att_routes[index], att_gates[index], block_ids, owner, experts
        )
        mlp_pick, mlp_weight, unused_pos, unused_block = routing(
            mlp_routes[index], mlp_gates[index], block_ids, owner, experts
        )
        scale = lax.rsqrt(jnp.mean(inputs * inputs, axis=1, keepdims=True) + EPS)
        normed = (inputs * scale * gain_attn).astype(jnp.bfloat16)
        mixed = jnp.dot(normed, shared_full, preferred_element_type=jnp.float32)
        keys_here = rotate(mixed[:, :width], own_cos, own_sin).astype(jnp.bfloat16)
        local_kv = jnp.concatenate([keys_here, mixed[:, width:].astype(jnp.bfloat16)], axis=1)
        sequence_kv = lax.all_gather(local_kv, "expert", axis=0, tiled=True)
        keys = sequence_kv[:, :width]
        values = sequence_kv[:, width:].reshape(length, HEADS, HDIM)
        rows = lax.all_to_all(
            spread(att_pick, normed), "expert", split_axis=0, concat_axis=0, tiled=True
        ).reshape(-1, model)
        row_cos, row_sin = angles(row_pos)
        queries = rotate(
            jnp.dot(rows, query_full, preferred_element_type=jnp.float32), row_cos, row_sin
        ).astype(jnp.bfloat16)
        scores = score_block(queries, keys, row_block, block_ids)
        top = jnp.max(scores, axis=2, keepdims=True)
        powers = jnp.exp(scores - top)
        total = jnp.sum(powers, axis=2, keepdims=True)
        log_total = top + jnp.log(total)
        probs = (powers / total).astype(jnp.bfloat16)
        attended = jnp.einsum("hrk,khd->rhd", probs, values, preferred_element_type=jnp.float32)
        attended = attended.reshape(-1, width).astype(jnp.bfloat16)
        result = jnp.dot(attended, output_full, preferred_element_type=jnp.float32).astype(
            jnp.bfloat16
        )
        back = lax.all_to_all(
            result.reshape(experts, CAP, model), "expert", split_axis=0, concat_axis=0, tiled=True
        )
        middle = inputs + collect(att_weight, back)
        scale_two = lax.rsqrt(jnp.mean(middle * middle, axis=1, keepdims=True) + EPS)
        normed_two = (middle * scale_two * gain_mlp).astype(jnp.bfloat16)
        rows_two = lax.all_to_all(
            spread(mlp_pick, normed_two), "expert", split_axis=0, concat_axis=0, tiled=True
        ).reshape(-1, model)
        both = jnp.dot(rows_two, gate_up_full, preferred_element_type=jnp.float32)
        gate = both[:, :hidden_width]
        up = both[:, hidden_width:]
        sigma = 1.0 / (1.0 + jnp.exp(-gate))
        hidden = (gate * sigma * up).astype(jnp.bfloat16)
        result_two = jnp.dot(hidden, down_full, preferred_element_type=jnp.float32).astype(
            jnp.bfloat16
        )
        back_two = lax.all_to_all(
            result_two.reshape(experts, CAP, model),
            "expert",
            split_axis=0,
            concat_axis=0,
            tiled=True,
        )
        final = middle + collect(mlp_weight, back_two)
        outputs.append(final.astype(jnp.bfloat16))
        upstream = cotangent[index].astype(jnp.float32)
        outgoing = jnp.einsum("ect,td->ecd", mlp_weight, upstream, precision=HIGH).astype(
            jnp.bfloat16
        )
        down_grad = lax.all_to_all(
            outgoing, "expert", split_axis=0, concat_axis=0, tiled=True
        ).reshape(-1, model)
        hidden_grad = jnp.einsum(
            "rd,fd->rf", down_grad, down_full, preferred_element_type=jnp.float32
        )
        slope = sigma * (1.0 + gate * (1.0 - sigma))
        both_grad = jnp.concatenate(
            [hidden_grad * up * slope, hidden_grad * gate * sigma], axis=1
        ).astype(jnp.bfloat16)
        row_grad_two = jnp.einsum(
            "rf,df->rd", both_grad, gate_up_full, preferred_element_type=jnp.float32
        ).astype(jnp.bfloat16)
        returned_two = lax.all_to_all(
            row_grad_two.reshape(experts, CAP, model),
            "expert",
            split_axis=0,
            concat_axis=0,
            tiled=True,
        )
        normed_two_grad = collect(mlp_pick, returned_two)
        scaled_two = normed_two_grad * gain_mlp
        gain_second = jnp.sum(normed_two_grad * middle * scale_two, axis=0, keepdims=True)
        middle_grad = (
            upstream
            + scale_two * scaled_two
            - middle * scale_two**3 * jnp.mean(scaled_two * middle, axis=1, keepdims=True)
        )
        outgoing_att = jnp.einsum("ect,td->ecd", att_weight, middle_grad, precision=HIGH).astype(
            jnp.bfloat16
        )
        result_grad = lax.all_to_all(
            outgoing_att, "expert", split_axis=0, concat_axis=0, tiled=True
        ).reshape(-1, model)
        attended_grad = jnp.einsum(
            "rd,fd->rf", result_grad, output_full, preferred_element_type=jnp.float32
        ).astype(jnp.bfloat16)
        again = jnp.exp(score_block(queries, keys, row_block, block_ids) - log_total)
        heads_grad = attended_grad.reshape(-1, HEADS, HDIM)
        value_grad = jnp.einsum(
            "hrk,rhd->khd",
            again.astype(jnp.bfloat16),
            heads_grad,
            preferred_element_type=jnp.float32,
        )
        prob_grad = jnp.einsum(
            "rhd,khd->hrk", heads_grad, values, preferred_element_type=jnp.float32
        )
        inner = jnp.sum(again * prob_grad, axis=2, keepdims=True)
        raw_grad = (again * (prob_grad - inner) * HDIM ** (-0.5)).astype(jnp.bfloat16)
        query_grad = jnp.einsum(
            "hrk,khd->rhd",
            raw_grad,
            keys.reshape(length, HEADS, HDIM),
            preferred_element_type=jnp.float32,
        ).reshape(-1, width)
        query_grad = rotate(query_grad, row_cos, -row_sin).astype(jnp.bfloat16)
        key_grad = jnp.einsum(
            "hrk,rhd->khd",
            raw_grad,
            queries.reshape(-1, HEADS, HDIM),
            preferred_element_type=jnp.float32,
        ).reshape(length, width)
        row_grad = jnp.einsum(
            "rf,df->rd", query_grad, query_full, preferred_element_type=jnp.float32
        ).astype(jnp.bfloat16)
        returned = lax.all_to_all(
            row_grad.reshape(experts, CAP, model), "expert", split_axis=0, concat_axis=0, tiled=True
        )
        kv_grad = lax.psum_scatter(
            jnp.concatenate([key_grad, value_grad.reshape(length, width)], axis=1).astype(
                jnp.bfloat16
            ),
            "expert",
            scatter_dimension=0,
            tiled=True,
        ).astype(jnp.float32)
        mixed_grad = jnp.concatenate(
            [rotate(kv_grad[:, :width], own_cos, -own_sin), kv_grad[:, width:]], axis=1
        ).astype(jnp.bfloat16)
        normed_grad = collect(att_pick, returned) + jnp.einsum(
            "tf,df->td", mixed_grad, shared_full, preferred_element_type=jnp.float32
        )
        scaled = normed_grad * gain_attn
        gain_first = jnp.sum(normed_grad * inputs * scale, axis=0, keepdims=True)
        input_grad = (
            middle_grad
            + scale * scaled
            - inputs * scale**3 * jnp.mean(scaled * inputs, axis=1, keepdims=True)
        )
        input_grads.append(input_grad.astype(jnp.bfloat16))
        kept = (
            rows,
            query_grad,
            attended,
            result_grad,
            rows_two,
            both_grad,
            hidden,
            down_grad,
            normed,
            mixed_grad,
            gain_first,
            gain_second,
        )
        for name, value in zip(names, kept):
            store[name].append(value)
    reduced = reduce_all(store, list(range(micro)))
    grad_query, grad_out, grad_gate_up, grad_down, grad_kv, grad_gain_attn, grad_gain_mlp = reduced
    return (
        jnp.stack(outputs, axis=0),
        jnp.stack(input_grads, axis=0),
        grad_gain_attn,
        grad_gain_mlp,
        grad_kv,
        grad_query,
        grad_out,
        grad_gate_up,
        grad_down,
    )


def solution(mesh):
    in_specs = (
        P(None, ("group", "expert"), None),
        P(None, ("group", "expert"), None),
        P(),
        P(),
        P(("group", "expert"), None),
        P("expert", "group", None),
        P("expert", "group", None),
        P("expert", "group", None),
        P("expert", "group", None),
        P(None, "group", None),
        P(None, ("group", "expert"), None),
        P(None, "group", None),
        P(None, ("group", "expert"), None),
        P(None, "group", None),
    )
    out_specs = (
        P(None, ("group", "expert"), None),
        P(None, ("group", "expert"), None),
        P(("group", "expert")),
        P(("group", "expert")),
        P(("group", "expert"), None),
        P("expert", "group", None),
        P("expert", "group", None),
        P("expert", "group", None),
        P("expert", "group", None),
    )
    return jax.shard_map(
        on_device, mesh=mesh, in_specs=in_specs, out_specs=out_specs, check_vma=False
    )
```

profile of v0, /device:TPU:0, one launch (start us, length us, event | category | flops | bytes accessed | tf_op | source)
XLA Modules:
  0.0 3856.1 jit_solution(10142143073186883707)
XLA Ops:
  12.8 115.7 %all-gather.8.cloned.1.call-done = bf16[2048,4096]{1,0:T(8,128)(2,1)} async-done(((bf16[64,4096]{1,0:T(8,128)(2,1)}), bf16[2048,4096]{1,0:T(8,128)(2,1)}) %all-gather.8.cloned.1.call-update) | async-done | bytes 16777232 | tf_op jit(solution)/shard_map/all_gather | solution.py:152
  128.5 8.9 fusion.346
  204.6 7.4 all-to-all-done
  217.1 36.6 all-gather.12.cloned.1.call-done
  253.7 12.4 copy.425
  266.2 6.1 fusion.224
  287.2 119.4 %all-gather.14.cloned.1.call-done = bf16[1,2048,2048]{2,1,0:T(8,128)(2,1)} async-done(((bf16[1,256,2048]{2,1,0:T(8,128)(2,1)}), bf16[1,2048,2048]{2,1,0:T(8,128)(2,1)}) %all-gather.14.cloned.1.call-update) | async-done | bytes 8388624 | tf_op jit(solution)/shard_map/all_gather | solution.py:155
  406.6 6.1 fusion.87
  415.1 17.3 all-gather.10.cloned.1.call-done
  449.5 8.7 all-to-all-done.8
  469.6 6.1 all-to-all-done.5
  483.3 9.0 all-to-all-done.1
  499.3 10.4 all-to-all-done.6
  527.6 779.9 %all-gather.16.cloned.1.call-done = bf16[1,2048,11264]{2,1,0:T(8,128)(2,1)} async-done(((bf16[1,256,11264]{2,1,0:T(8,128)(2,1)}), bf16[1,2048,11264]{2,1,0:T(8,128)(2,1)}) %all-gather.16.cloned.1.call-update) | async-done | bytes 46137360 | tf_op jit(solution)/shard_map/all_gather | solution.py:156
  1307.5 23.9 fusion.6
  1331.4 418.8 %all-gather.18.cloned.1.call-done = bf16[1,5632,2048]{2,1,0:T(8,128)(2,1)} async-done(((bf16[1,704,2048]{2,1,0:T(8,128)(2,1)}), bf16[1,5632,2048]{2,1,0:T(8,128)(2,1)}) %all-gather.18.cloned.1.call-update) | async-done | bytes 23068688 | tf_op jit(solution)/shard_map/all_gather | solution.py:157
  1750.1 16.9 multiply_convert_fusion.3
  1767.0 22.3 fusion.73
  1796.4 22.5 fusion.8
  1818.9 17.2 multiply_convert_fusion.5
  1836.1 22.3 fusion.68
  1866.8 11.3 all-to-all-done.9
  1890.3 12.3 all-to-all-done.10
  1905.0 6.6 fusion.209
  1918.6 27.5 fusion.174
  1957.3 13.9 all-to-all-done.14
  1971.4 6.6 fusion.206
  1985.4 26.4 fusion.177
  2017.8 25.4 fusion.162
  2046.0 25.1 fusion.165
  2076.9 7.8 convolution_convert_fusion.3
  2086.6 7.1 convolution_convert_fusion.2
  2095.1 17.7 convolution_convert_fusion.1
  2114.2 33.5 convolution_convert_fusion
  2155.8 14.7 fusion.192
  2172.2 10.4 fusion.99
  2187.4 13.8 fusion.96
  2208.6 10.7 all-to-all-done.3
  2222.7 6.6 fusion.78
  2234.0 7.5 fusion.81
  2243.8 11.9 fusion.254
  2262.7 12.3 fusion.250
  2278.7 43.0 %all-reduce.7 = (f32[2048]{0:T(1024)S(1)}, f32[2048]{0:T(1024)S(1)}) all-reduce(f32[2048]{0:T(1024)S(1)} %reduce_sum.352, f32[2048]{0:T(1024)S(1)} %reduce_sum.355), channel_id=4, replica_groups=mesh['group'=8,'expert'=4] {'group','expert'}, use_global_device_ids=true, to_apply=%region_44.45.clone | all-reduce | flops 4096 | bytes 32768
  2330.0 56.5 %reduce-scatter.18.cloned.1.call-done = bf16[256,2048]{1,0:T(8,128)(2,1)} async-done(((bf16[2048,2048]{1,0:T(8,128)(2,1)}), bf16[256,2048]{1,0:T(8,128)(2,1)}) %reduce-scatter.18.cloned.1.call-update) | async-done | bytes 1048592 | tf_op jit(solution)/shard_map/reduce_scatter | solution.py:104
  2389.3 373.5 %reduce-scatter.20.cloned.1.call-done = bf16[704,2048]{1,0:T(8,128)(2,1)} async-done(((bf16[5632,2048]{1,0:T(8,128)(2,1)}), bf16[704,2048]{1,0:T(8,128)(2,1)}) %reduce-scatter.20.cloned.1.call-update) | async-done | bytes 2883600 | tf_op jit(solution)/shard_map/reduce_scatter | solution.py:104
  2768.0 725.1 %reduce-scatter.22.cloned.1.call-done = bf16[256,11264]{1,0:T(8,128)(2,1)} async-done(((bf16[2048,11264]{1,0:T(8,128)(2,1)}), bf16[256,11264]{1,0:T(8,128)(2,1)}) %reduce-scatter.22.cloned.1.call-update) | async-done | bytes 5767184
  3493.1 8.5 bitcast_convert_fusion
  3501.7 347.7 %reduce-scatter.14.cloned.1.call-done = f32[64,4096]{1,0:T(8,128)} async-done(((f32[2048,4096]{1,0:T(8,128)}), f32[64,4096]{1,0:T(8,128)}) %reduce-scatter.14.cloned.1.call-update) | async-done | bytes 1048592 | tf_op jit(solution)/shard_map/reduce_scatter | solution.py:127
  (543 shorter events, 288.4 us)
Async XLA Ops:
  7.2 121.3 %all-gather.8.cloned.1.call-start = ((), (), s32[]{:S(2)}) async-start(), calls=%async_computation.23 | async-start | bytes 17301504 | tf_op jit(solution)/shard_map/all_gather | solution.py:152
  7.9 245.8 %all-gather.12.cloned.1.call-start = ((), (), s32[]{:S(2)}) async-start(), calls=%async_computation.25 | async-start | bytes 9437184 | tf_op jit(solution)/shard_map/all_gather | solution.py:154
  8.7 271.0 %all-gather.20.cloned.1.call-start = ((), (), s32[]{:S(2)}) async-start(), calls=%async_computation.29 | async-start | bytes 3276800 | tf_op jit(solution)/shard_map/all_gather | solution.py:201
  10.6 126.7 %copy-start.96 = (f32[80]{0:T(128)}, f32[80]{0:T(128)S(1)}, u32[]{:S(2)}) copy-start(f32[80]{0:T(128)S(1)} %get-tuple-element.118) | copy-start | bytes 964
  10.6 126.8 %copy-start.98 = (f32[80]{0:T(128)}, f32[80]{0:T(128)S(1)}, u32[]{:S(2)}) copy-start(f32[80]{0:T(128)S(1)} %get-tuple-element.100) | copy-start | bytes 964
  11.5 134.8 %copy-start.78 = (f32[80,64]{0,1:T(8,128)}, f32[80,64]{0,1:T(8,128)S(1)}, u32[]{:S(2)}) copy-start(f32[80,64]{0,1:T(8,128)S(1)} %get-tuple-element.96) | copy-start | bytes 61444
  12.8 153.6 %copy-start.17 = (bf16[80,2048]{1,0:T(8,128)(2,1)}, bf16[80,2048]{1,0:T(8,128)(2,1)S(1)}, u32[]{:S(2)}) copy-start(bf16[80,2048]{1,0:T(8,128)(2,1)S(1)} %get-tuple-element.69) | copy-start | bytes 983044
  12.8 181.4 %copy-start.15 = (bf16[80,2048]{1,0:T(8,128)(2,1)}, bf16[80,2048]{1,0:T(8,128)(2,1)S(1)}, u32[]{:S(2)}) copy-start(bf16[80,2048]{1,0:T(8,128)(2,1)S(1)} %get-tuple-element.68) | copy-start | bytes 983044
  149.5 257.1 %all-gather.14.cloned.1.call-start = ((), (), s32[]{:S(2)}) async-start(), calls=%async_computation.26 | async-start | bytes 9437184 | tf_op jit(solution)/shard_map/all_gather | solution.py:155
  150.1 282.3 %all-gather.10.cloned.1.call-start = ((), (), s32[]{:S(2)}) async-start(), calls=%async_computation.24 | async-start | bytes 3276800 | tf_op jit(solution)/shard_map/all_gather | solution.py:201
  152.6 1154.9 %all-gather.16.cloned.1.call-start = ((), (), s32[]{:S(2)}) async-start(), calls=%async_computation.27 | async-start | bytes 51904512 | tf_op jit(solution)/shard_map/all_gather | solution.py:156
  153.2 1596.9 %all-gather.18.cloned.1.call-start = ((), (), s32[]{:S(2)}) async-start(), calls=%async_computation.28 | async-start | bytes 25952256 | tf_op jit(solution)/shard_map/all_gather | solution.py:157
  167.7 27.8 all-to-all-start.4
  194.2 81.8 %copy-start.71 = (f32[200,64]{0,1:T(8,128)}, f32[200,64]{0,1:T(8,128)S(1)}, u32[]{:S(2)}) copy-start(f32[200,64]{0,1:T(8,128)S(1)} %get-tuple-element.90) | copy-start | bytes 153604
  195.5 16.6 all-to-all-start
  212.1 229.6 %all-to-all-start.12 = ((bf16[4,50,2048]{2,1,0:T(8,128)(2,1)}), bf16[4,50,2048]{2,1,0:T(8,128)(2,1)S(1)}, u32[]{:S(2)}, u32[]{:S(2)}) async-start(bf16[4,50,2048]{2,1,0:T(8,128)(2,1)} %convolution_convert_fusion.4), calls=%async_computation.13 | async-start | bytes 1835008 | tf_op jit(solution)/shard_map/all_to_all | solution.py:252
  276.5 157.8 %copy-start.33 = (bf16[200,16,2,64]{0,3,2,1:T(8,128)(2,1)}, bf16[200,16,2,64]{0,3,2,1:T(8,128)(2,1)S(1)}, u32[]{:S(2)}) copy-start(bf16[200,16,2,64]{0,3,2,1:T(8,128)(2,1)S(1)} %pad_maximum_fusion.2) | copy-start | bytes 2457604
  287.2 125.5 %copy-start.55 = (bf16[16,25,8,128]{3,2,1,0:T(8,128)(2,1)}, bf16[16,25,8,128]{3,2,1,0:T(8,128)(2,1)S(1)}, u32[]{:S(2)}) copy-start(bf16[16,25,8,128]{3,2,1,0:T(8,128)(2,1)S(1)} %fusion.203) | copy-start | bytes 2457604
  441.7 16.6 all-to-all-start.8
  459.2 16.5 all-to-all-start.5
  475.8 16.5 all-to-all-start.1
  481.2 1469.7 %copy-start.3 = (f32[80,2048]{1,0:T(8,128)}, f32[80,2048]{1,0:T(8,128)S(1)}, u32[]{:S(2)}) copy-start(f32[80,2048]{1,0:T(8,128)S(1)} %get-tuple-element.111) | copy-start | bytes 1966084
  481.9 1396.3 %copy-start.100 = (f32[80]{0:T(128)}, f32[80]{0:T(128)S(1)}, u32[]{:S(2)}) copy-start(f32[80]{0:T(128)S(1)} %get-tuple-element.107) | copy-start | bytes 964
  492.3 17.4 all-to-all-start.6
  497.3 1383.6 %copy-start.5 = (f32[80,2048]{1,0:T(8,128)}, f32[80,2048]{1,0:T(8,128)S(1)}, u32[]{:S(2)}) copy-start(f32[80,2048]{1,0:T(8,128)S(1)} %get-tuple-element.115) | copy-start | bytes 1966084
  497.9 1380.2 %copy-start.103 = (f32[80]{0:T(128)}, f32[80]{0:T(128)S(1)}, u32[]{:S(2)}) copy-start(f32[80]{0:T(128)S(1)} %get-tuple-element.105) | copy-start | bytes 964
  509.7 16.7 all-to-all-start.2
  527.6 1222.5 %copy-start.61 = (bf16[200,2048]{1,0:T(8,128)(2,1)S(1)}, bf16[200,2048]{1,0:T(8,128)(2,1)}, u32[]{:S(2)}) copy-start(bf16[200,2048]{1,0:T(8,128)(2,1)} %reshape.829) | copy-start | bytes 2457604
  1791.7 69.1 %all-to-all-start.13 = ((bf16[4,50,2048]{2,1,0:T(8,128)(2,1)}), bf16[4,50,2048]{2,1,0:T(8,128)(2,1)}, u32[]{:S(2)}, u32[]{:S(2)}) async-start(bf16[4,50,2048]{2,1,0:T(8,128)(2,1)} %reshape.830), calls=%async_computation.14 | async-start | bytes 1835008 | tf_op jit(solution)/shard_map/all_to_all | solution.py:265
  1860.8 17.4 all-to-all-start.9
  1866.8 84.1 %copy-start.9 = (f32[80,2048]{1,0:T(8,128)}, f32[80,2048]{1,0:T(8,128)S(1)}, u32[]{:S(2)}) copy-start(f32[80,2048]{1,0:T(8,128)S(1)} %convolution_bitcast_fusion.1) | copy-start | bytes 1966084
  1885.1 17.5 all-to-all-start.10
  1889.5 258.2 %reduce-scatter.10.cloned.1.call-start = ((), (), s32[]{:S(2)}) async-start(), calls=%async_computation.30 | async-start | bytes 3276800 | tf_op jit(solution)/shard_map/reduce_scatter | solution.py:321
  1953.6 17.5 all-to-all-start.14
  1957.2 192.1 %reduce-scatter.12.cloned.1.call-start = ((), (), s32[]{:S(2)}) async-start(), calls=%async_computation.31 | async-start | bytes 3276800 | tf_op jit(solution)/shard_map/reduce_scatter | solution.py:321
  2015.5 311.7 %reduce-scatter.16.cloned.1.call-start = ((), (), s32[]{:S(2)}) async-start(), calls=%async_computation.33 | async-start | bytes 9437184 | tf_op jit(solution)/shard_map/reduce_scatter | solution.py:104
  2084.7 301.8 %reduce-scatter.18.cloned.1.call-start = ((), (), s32[]{:S(2)}) async-start(), calls=%async_computation.34 | async-start | bytes 9437184 | tf_op jit(solution)/shard_map/reduce_scatter | solution.py:104
  2093.7 669.2 %reduce-scatter.20.cloned.1.call-start = ((), (), s32[]{:S(2)}) async-start(), calls=%async_computation.35 | async-start | bytes 25952256 | tf_op jit(solution)/shard_map/reduce_scatter | solution.py:104
  2112.8 1380.3 %reduce-scatter.22.cloned.1.call-start = ((), (), s32[]{:S(2)}) async-start(), calls=%async_computation.36 | async-start | bytes 51904512
  2147.7 1701.7 %reduce-scatter.14.cloned.1.call-start = ((), (), s32[]{:S(2)}) async-start(), calls=%async_computation.32 | async-start | bytes 34603008 | tf_op jit(solution)/shard_map/reduce_scatter | solution.py:127
  2183.8 18.6 all-to-all-start.7
  2202.4 16.9 all-to-all-start.3
  2230.5 25.2 all-to-all-start.15
  2255.6 19.4 all-to-all-start.11
  2262.6 60.2 %copy-start.10 = (f32[80,2048]{1,0:T(8,128)S(1)}, f32[80,2048]{1,0:T(8,128)}, u32[]{:S(2)}) copy-start(f32[80,2048]{1,0:T(8,128)} %copy-done.9) | copy-start | bytes 1966084
  2262.7 60.2 %copy-start.21 = (bf16[2,80,2048]{2,1,0:T(8,128)(2,1)S(1)}, bf16[2,80,2048]{2,1,0:T(8,128)(2,1)}, u32[]{:S(2)}) copy-start(bf16[2,80,2048]{2,1,0:T(8,128)(2,1)} %param.15) | copy-start | bytes 1966084
  2262.7 60.2 %copy-start.76 = (f32[2048]{0:T(1024)S(1)}, f32[2048]{0:T(1024)}, u32[]{:S(2)}) copy-start(f32[2048]{0:T(1024)} %param.17) | copy-start | bytes 24580
  2262.7 60.2 %copy-start.102 = (f32[80]{0:T(128)S(1)}, f32[80]{0:T(128)}, u32[]{:S(2)}) copy-start(f32[80]{0:T(128)} %copy-done.100) | copy-start | bytes 964
  (109 other events, 1397.8 us)
Sparse Core Ops, SparseCore 0:
  10.9 117.5 all-gather.7
  130.6 123.1 all-gather.11
  255.9 23.7 all-gather.19
  281.6 124.9 all-gather.13
  408.6 23.7 all-gather.9
  433.7 873.6 all-gather.15
  1309.0 441.0 all-gather.17
  1951.0 34.3 reduce-scatter.9
  2015.6 33.8 reduce-scatter.11
  2084.9 148.0 reduce-scatter.15
  2237.0 149.4 reduce-scatter.17
  2390.3 372.5 reduce-scatter.19
  2766.7 726.3 reduce-scatter.21
  3496.0 353.3 reduce-scatter.13
where the time goes:
time: 3870 us; the launch traced here: 3860 us
  waiting for transfers between devices  3090 us (80%)
  matrix products  472 us (12%)
  local copies, waits for them, and re-layouts  85.3 us (2%)
  other arithmetic  83.9 us (2%)
  starting transfers between devices  62.5 us (2%)
  blocking collectives  43 us (1%)
    all_gather x1, waiting for transfers between devices, on_device(): lax.all_gather(w_gate_up, 'group', axis=1, tiled=True)  780 us
    unnamed x15, waiting for transfers between devices  728 us
    reduce_scatter x3, waiting for transfers between devices, expert_reduce(): lax.psum_scatter(term(jnp.int32(0), lax.axis_size('group') * (left.shape[...  430 us
    all_gather x1, waiting for transfers between devices, on_device(): lax.all_gather(w_down, 'group', axis=1, tiled=True)  419 us
    reduce_scatter x1, waiting for transfers between devices, reduce_all(): lax.psum_scatter(shared_term, ('group', 'expert'), scatter_dimension=0, t...  348 us
    all_gather x1, waiting for transfers between devices, on_device(): lax.all_gather(w_out, 'group', axis=1, tiled=True)  119 us
    all_gather x1, waiting for transfers between devices, on_device(): shared_full = lax.all_gather(w_kv, ('group', 'expert'), axis=0, tiled=True)  116 us
  transfers between devices with their start and end apart: 30, of which 21 were waited for; matrix products, arithmetic and copies ran while one was open for 14% of the time, Pallas kernels for 0%

commit v1 on v0

--- a/solution.py
+++ b/solution.py
@@ -1,6 +1,10 @@
+import functools
+
 import jax
 import jax.numpy as jnp
 from jax import lax
+from jax.experimental import pallas as pl
+from jax.experimental.pallas import tpu as pltpu
 from jax.sharding import PartitionSpec as P
 
 HEADS = 16
@@ -371,6 +375,412 @@
     )
 
 
+ZS, YS, XS, CS = 4, 2, 2, 2
+SEQ = 320
+F32 = jnp.float32
+BF16 = jnp.bfloat16
+
+
+def fits(mesh):
+    return mesh.shape["group"] == ZS * YS and mesh.shape["expert"] == XS * CS
+
+
+def group_move(value, move):
+    pairs = []
+    for z in range(ZS):
+        for y in range(YS):
+            to_z, to_y = move(z, y)
+            pairs.append((z * YS + y, to_z * YS + to_y))
+    return lax.ppermute(value, "group", pairs)
+
+
+def z_move(value, step):
+    return group_move(value, lambda z, y: ((z + step) % ZS, y))
+
+
+def y_move(value):
+    return group_move(value, lambda z, y: (z, 1 - y))
+
+
+def x_move(value):
+    return lax.ppermute(value, "expert", [(x * CS + c, (1 - x) * CS + c) for x in range(XS) for c in range(CS)])
+
+
+def c_move(value):
+    return lax.ppermute(value, "expert", [(x * CS + c, x * CS + 1 - c) for x in range(XS) for c in range(CS)])
+
+
+def z_exchange(value):
+    columns = [[z * YS + y for z in range(ZS)] for y in range(YS)]
+    return lax.all_to_all(
+        value, "group", split_axis=0, concat_axis=0, tiled=True, axis_index_groups=columns
+    )
+
+
+def gather_tokens(own):
+    column = jnp.stack([own] + [z_move(own, -step) for step in range(1, ZS)], axis=0)
+    plane = jnp.stack([column, x_move(column)], axis=1)
+    plane = plane.reshape((ZS, XS * own.shape[0]) + own.shape[1:])
+    return jnp.stack([plane, c_move(plane)], axis=0)
+
+
+def reduce_tokens(other, mine):
+    local = mine.shape[1] // XS
+    total = mine.astype(F32) + c_move(other).astype(F32)
+    arrived = x_move(total[:, local:].astype(BF16))
+    total = total[:, :local] + arrived.astype(F32)
+    result = total[0]
+    for step in range(1, ZS):
+        result = result + z_move(total[step].astype(BF16), step).astype(F32)
+    return result
+
+
+def merge(index, own, other, axis):
+    return jnp.where(index == 0, jnp.stack([own, other], axis), jnp.stack([other, own], axis))
+
+
+def take(value, index, axis):
+    return lax.dynamic_index_in_dim(value, index, axis, keepdims=False)
+
+
+def dot(left, right):
+    return jnp.dot(left, right, preferred_element_type=F32)
+
+
+def dot_t(left, right):
+    return lax.dot_general(left, right, (((1,), (1,)), ((), ())), preferred_element_type=F32)
+
+
+def dot_l(left, right):
+    return lax.dot_general(left, right, (((0,), (0,)), ((), ())), preferred_element_type=F32)
+
+
+def turned(value, cosine, sine):
+    return value * cosine + pltpu.roll(value, HDIM // 2, 1) * sine
+
+
+def masked_probs(query, key, row_block, key_block):
+    scores = jnp.where(key_block <= row_block, dot_t(query, key) * HDIM ** (-0.5), -1e30)
+    powers = jnp.exp(scores - jnp.max(scores, axis=1, keepdims=True))
+    return powers / jnp.sum(powers, axis=1, keepdims=True)
+
+
+def attend_kernel(qkv_ref, cos_ref, sin_ref, row_ref, key_ref, turned_ref, out_ref):
+    cosine, sine = cos_ref[...], sin_ref[...]
+    rows, width = cosine.shape[0], out_ref.shape[3]
+    half = rows // 2
+    for head in range(width // HDIM):
+        parts = []
+        for kind in range(3):
+            span = slice(kind * width + head * HDIM, kind * width + (head + 1) * HDIM)
+            value = qkv_ref[:, 0, :, span].reshape(rows, HDIM)
+            if kind < 2:
+                value = turned(value, cosine, sine)
+            value = value.astype(BF16)
+            turned_ref[:, 0, :, span] = value.reshape(2, half, HDIM)
+            parts.append(value)
+        query, key, value = parts
+        probs = masked_probs(query, key, row_ref[0], key_ref[0]).astype(BF16)
+        span = slice(head * HDIM, (head + 1) * HDIM)
+        out_ref[:, 0, :, span] = dot(probs, value).astype(BF16).reshape(2, half, HDIM)
+
+
+def attend(qkv, cosine, sine, row_blocks, key_blocks):
+    cores, seqs, half, triple = qkv.shape
+    width = triple // 3
+    rows = cores * half
+    return pl.pallas_call(
+        attend_kernel,
+        grid=(seqs,),
+        in_specs=[
+            pl.BlockSpec((cores, 1, half, triple), lambda k: (0, k, 0, 0)),
+            pl.BlockSpec((rows, HDIM), lambda k: (0, 0)),
+            pl.BlockSpec((rows, HDIM), lambda k: (0, 0)),
+            pl.BlockSpec((1, rows, 1), lambda k: (k, 0, 0)),
+            pl.BlockSpec((1, 1, rows), lambda k: (k, 0, 0)),
+        ],
+        out_specs=[
+            pl.BlockSpec((cores, 1, half, triple), lambda k: (0, k, 0, 0)),
+            pl.BlockSpec((cores, 1, half, width), lambda k: (0, k, 0, 0)),
+        ],
+        out_shape=[
+            jax.ShapeDtypeStruct(qkv.shape, BF16),
+            jax.ShapeDtypeStruct((cores, seqs, half, width), BF16),
+        ],
+        compiler_params=pltpu.CompilerParams(vmem_limit_bytes=40 << 20),
+        cost_estimate=pl.CostEstimate(
+            flops=4 * seqs * rows * rows * width,
+            bytes_accessed=qkv.size * 6 + qkv.size,
+            transcendentals=seqs * rows * rows * width // HDIM,
+        ),
+    )(qkv, cosine, sine, row_blocks, key_blocks)
+
+
+def attend_back_kernel(turned_ref, grad_ref, cos_ref, sin_ref, row_ref, key_ref, out_ref):
+    cosine, sine = cos_ref[...], -sin_ref[...]
+    rows, width = cosine.shape[0], grad_ref.shape[3]
+    half = rows // 2
+    for head in range(width // HDIM):
+        spans = [slice(kind * width + head * HDIM, kind * width + (head + 1) * HDIM) for kind in range(3)]
+        query, key, value = [turned_ref[:, 0, :, span].reshape(rows, HDIM) for span in spans]
+        grad = grad_ref[:, 0, :, spans[0]].reshape(rows, HDIM)
+        probs = masked_probs(query, key, row_ref[0], key_ref[0])
+        prob_grad = dot_t(grad, value)
+        inner = jnp.sum(probs * prob_grad, axis=1, keepdims=True)
+        raw_grad = (probs * (prob_grad - inner) * HDIM ** (-0.5)).astype(BF16)
+        results = [
+            turned(dot(raw_grad, key), cosine, sine),
+            turned(dot_l(raw_grad, query), cosine, sine),
+            dot_l(probs.astype(BF16), grad),
+        ]
+        for span, result in zip(spans, results):
+            out_ref[:, 0, :, span] = result.astype(BF16).reshape(2, half, HDIM)
+
+
+def attend_back(kept, grad, cosine, sine, row_blocks, key_blocks):
+    cores, seqs, half, triple = kept.shape
+    width = triple // 3
+    rows = cores * half
+    return pl.pallas_call(
+        attend_back_kernel,
+        grid=(seqs,),
+        in_specs=[
+            pl.BlockSpec((cores, 1, half, triple), lambda k: (0, k, 0, 0)),
+            pl.BlockSpec((cores, 1, half, width), lambda k: (0, k, 0, 0)),
+            pl.BlockSpec((rows, HDIM), lambda k: (0, 0)),
+            pl.BlockSpec((rows, HDIM), lambda k: (0, 0)),
+            pl.BlockSpec((1, rows, 1), lambda k: (k, 0, 0)),
+            pl.BlockSpec((1, 1, rows), lambda k: (k, 0, 0)),
+        ],
+        out_specs=pl.BlockSpec((cores, 1, half, triple), lambda k: (0, k, 0, 0)),
+        out_shape=jax.ShapeDtypeStruct(kept.shape, BF16),
+        compiler_params=pltpu.CompilerParams(vmem_limit_bytes=40 << 20),
+        cost_estimate=pl.CostEstimate(
+            flops=10 * seqs * rows * rows * width,
+            bytes_accessed=kept.size * 4 + grad.size * 2,
+            transcendentals=seqs * rows * rows * width // HDIM,
+        ),
+    )(kept, grad, cosine, sine, row_blocks, key_blocks)
+
+
+def columns_of(parts, kinds):
+    width = parts.shape[2] // kinds
+    return jnp.concatenate(
+        [parts[z, :, kind * width : (kind + 1) * width] for kind in range(kinds) for z in range(ZS)], axis=1
+    )
+
+
+def fast_device(
+    tokens,
+    cotangent,
+    gain_attn,
+    gain_mlp,
+    w_kv,
+    w_query,
+    w_out,
+    w_gate_up,
+    w_down,
+    att_routes,
+    att_gates,
+    mlp_routes,
+    mlp_gates,
+    blocks,
+):
+    group, owner = lax.axis_index("group"), lax.axis_index("expert")
+    y = group % YS
+    x, core = owner // CS, owner % CS
+    micro, local, model = tokens.shape
+    wide = w_query.shape[2] // ZS
+    hidden_width = w_gate_up.shape[2] // (2 * ZS)
+    kv_rows = w_kv.shape[0]
+    model_rows = w_query.shape[1]
+
+    def own_rows(table):
+        return lax.dynamic_slice_in_dim(table, owner * local, local, 0).astype(F32)
+
+    columns = []
+    for index in range(micro):
+        columns += [own_rows(att_routes[index]), att_gates[index], own_rows(mlp_routes[index]), mlp_gates[index]]
+        columns += [own_rows(blocks[index, 0][:, None])]
+    table = gather_tokens(jnp.concatenate(columns, axis=1))
+    table = table.reshape(CS, ZS, XS * local, micro, 9)
+
+    positions = (
+        (x ^ jnp.arange(XS)[None, :, None]) * CS + (core ^ jnp.arange(CS)[:, None, None])
+    ) * local + jnp.arange(local)[None, None, :]
+    cosine, sine = angles(positions.reshape(-1))
+    cosine = jnp.concatenate([cosine, cosine], axis=1)
+    sine = jnp.concatenate([-sine, sine], axis=1)
+
+    kv_part = w_kv.reshape(kv_rows, 2, ZS, wide).transpose(2, 0, 1, 3).reshape(ZS, kv_rows, 2 * wide)
+    kv_part = z_exchange(kv_part)
+    kv_part = merge(y, kv_part, y_move(kv_part), 1)
+    kv_part = merge(x, kv_part, x_move(kv_part), 2)
+    kv_part = merge(core, kv_part, c_move(kv_part), 3)
+    kv_part = kv_part.reshape(model, 2 * wide)
+    query_part = z_exchange(w_query[0].reshape(model_rows, ZS, wide).transpose(1, 0, 2))
+    query_part = merge(y, query_part, y_move(query_part), 1).reshape(model, wide)
+    qkv_weight = jnp.concatenate([query_part, kv_part], axis=1)
+    out_weight = merge(y, w_out[0], y_move(w_out[0]), 0).reshape(wide, model)
+    down_weight = merge(y, w_down[0], y_move(w_down[0]), 0).reshape(hidden_width, model)
+    gate_up = w_gate_up[0].reshape(model_rows, 2, ZS, hidden_width).transpose(2, 0, 1, 3)
+    gate_up = z_exchange(gate_up.reshape(ZS, model_rows, 2 * hidden_width))
+    gate_up = merge(y, gate_up, y_move(gate_up), 1).reshape(model, 2 * hidden_width)
+
+    outputs, input_grads, kept = [], [], []
+    before_mask = jnp.arange(SEQ)[:, None] < jnp.arange(SEQ)[None, :]
+    for index in range(micro):
+        part = table[:, :, :, index]
+        att_weight = jnp.sum(jnp.where(part[..., 0:2] == owner, part[..., 2:4], 0.0), axis=-1)
+        mlp_hit = jnp.any(part[..., 4:6] == owner, axis=-1)
+        mlp_weight = jnp.sum(jnp.where(part[..., 4:6] == owner, part[..., 6:8], 0.0), axis=-1)
+        seq_blocks = part[..., 8].transpose(1, 0, 2).reshape(ZS, -1).astype(jnp.int32)
+        row_blocks, key_blocks = seq_blocks[:, :, None], seq_blocks[:, None, :]
+        hit = mlp_hit.transpose(1, 0, 2).reshape(ZS, -1)
+        before = jnp.einsum(
+            "kt,tu->ku", hit.astype(BF16), before_mask.astype(BF16), preferred_element_type=F32
+        ).astype(jnp.int32)
+        places = jnp.arange(owner_cap(local))
+        chosen = hit[:, None, :] & (before[:, None, :] == places[None, :, None])
+        row_gate = jnp.sum(
+            jnp.where(chosen, mlp_weight.transpose(1, 0, 2).reshape(ZS, 1, -1), 0.0), axis=2
+        )
+        select = chosen.astype(BF16).reshape(ZS, -1, CS, XS * local)
+        halves = [select[:, :, half] for half in range(CS)]
+
+        def to_rows(gathered, halves=halves):
+            return sum(
+                jnp.einsum("kru,kud->krd", halves[half], gathered[half], preferred_element_type=F32)
+                for half in range(CS)
+            )
+
+        def to_tokens(rows, halves=halves):
+            return [
+                jnp.einsum("kru,krd->kud", halves[half], rows, preferred_element_type=F32).astype(BF16)
+                for half in range(CS)
+            ]
+
+        inputs = tokens[index].astype(F32)
+        upstream = cotangent[index].astype(F32)
+        scale = lax.rsqrt(jnp.mean(inputs * inputs, axis=1, keepdims=True) + EPS)
+        normed = gather_tokens((inputs * scale * gain_attn).astype(BF16))
+        qkv = dot(normed.reshape(-1, model), qkv_weight).reshape(CS, ZS, XS * local, 3 * wide)
+        turned_qkv, attended = attend(qkv, cosine, sine, row_blocks, key_blocks)
+        result = [
+            (dot(attended[half].reshape(-1, wide), out_weight) * att_weight[half].reshape(-1, 1))
+            .astype(BF16)
+            .reshape(ZS, XS * local, model)
+            for half in range(CS)
+        ]
+        middle = inputs + reduce_tokens(result[1], result[0])
+        scale_two = lax.rsqrt(jnp.mean(middle * middle, axis=1, keepdims=True) + EPS)
+        normed_two = gather_tokens((middle * scale_two * gain_mlp).astype(BF16))
+        cotangents = gather_tokens(cotangent[index])
+        rows_two = to_rows(normed_two).astype(BF16).reshape(-1, model)
+        down_grad = (to_rows(cotangents) * row_gate[:, :, None]).astype(BF16).reshape(-1, model)
+        both = dot(rows_two, gate_up)
+        gate, up = both[:, :hidden_width], both[:, hidden_width:]
+        sigma = 1.0 / (1.0 + jnp.exp(-gate))
+        hidden = (gate * sigma * up).astype(BF16)
+        hidden_grad = dot_t(down_grad, down_weight)
+        slope = sigma * (1.0 + gate * (1.0 - sigma))
+        both_grad = jnp.concatenate(
+            [hidden_grad * up * slope, hidden_grad * gate * sigma], axis=1
+        ).astype(BF16)
+        row_grad = dot_t(both_grad, gate_up).astype(BF16).reshape(ZS, -1, model)
+        row_grad = to_tokens(row_grad)
+        normed_two_grad = reduce_tokens(row_grad[1], row_grad[0])
+        scaled_two = normed_two_grad * gain_mlp
+        gain_second = jnp.sum(normed_two_grad * middle * scale_two, axis=0, keepdims=True)
+        middle_grad = (
+            upstream
+            + scale_two * scaled_two
+            - middle * scale_two**3 * jnp.mean(scaled_two * middle, axis=1, keepdims=True)
+        )
+        middle_grads = gather_tokens(middle_grad.astype(BF16))
+
+        result_two = (dot(hidden, down_weight) * row_gate.reshape(-1, 1)).astype(BF16)
+        result_two = to_tokens(result_two.reshape(ZS, -1, model))
+        outputs.append((middle + reduce_tokens(result_two[1], result_two[0])).astype(BF16))
+
+        result_grad = (middle_grads.astype(F32) * att_weight[..., None]).astype(BF16).reshape(-1, model)
+        attended_grad = dot_t(result_grad, out_weight).astype(BF16).reshape(attended.shape)
+        qkv_grad = attend_back(turned_qkv, attended_grad, cosine, sine, row_blocks, key_blocks)
+        normed_part = [
+            dot_t(qkv_grad[half].reshape(-1, 3 * wide), qkv_weight)
+            .astype(BF16)
+            .reshape(ZS, XS * local, model)
+            for half in range(CS)
+        ]
+        normed_grad = reduce_tokens(normed_part[1], normed_part[0])
+        scaled = normed_grad * gain_attn
+        gain_first = jnp.sum(normed_grad * inputs * scale, axis=0, keepdims=True)
+        input_grad = (
+            middle_grad
+            + scale * scaled
+            - inputs * scale**3 * jnp.mean(scaled * inputs, axis=1, keepdims=True)
+        )
+        input_grads.append(input_grad.astype(BF16))
+        kept.append(
+            (
+                rows_two,
+                both_grad,
+                hidden,
+                down_grad,
+                attended.reshape(-1, wide),
+                result_grad,
+                normed.reshape(-1, model),
+                qkv_grad.reshape(-1, 3 * wide),
+                gain_first,
+                gain_second,
+            )
+        )
+
+    def joined(place):
+        return jnp.concatenate([entry[place] for entry in kept], axis=0)
+
+    def halve(value, index, axis, move):
+        return take(value, index, axis) + move(take(value, 1 - index, axis).astype(BF16)).astype(F32)
+
+    grad_gate_up = dot_l(joined(0), joined(1)).reshape(ZS, YS, model_rows, 2 * hidden_width)
+    grad_gate_up = z_exchange(halve(grad_gate_up, y, 1, y_move).astype(BF16)).astype(F32)
+    grad_gate_up = columns_of(grad_gate_up, 2)[None]
+    grad_down = dot_l(joined(2), joined(3)).reshape(YS, -1, model)
+    grad_down = halve(grad_down, y, 0, y_move)[None]
+    grad_out = dot_l(joined(4), joined(5)).reshape(YS, -1, model)
+    grad_out = halve(grad_out, y, 0, y_move)[None]
+    grad_qkv = dot_l(joined(6), joined(7))
+    grad_query = grad_qkv[:, :wide].reshape(ZS, YS, model_rows, wide)
+    grad_query = z_exchange(halve(grad_query, y, 1, y_move).astype(BF16)).astype(F32)
+    grad_query = columns_of(grad_query, 1)[None]
+    grad_kv = grad_qkv[:, wide:].reshape(ZS, YS, XS, CS, kv_rows, 2 * wide)
+    grad_kv = halve(grad_kv, core, 3, c_move)
+    grad_kv = halve(grad_kv, x, 2, x_move)
+    grad_kv = z_exchange(halve(grad_kv, y, 1, y_move).astype(BF16)).astype(F32)
+    grad_kv = columns_of(grad_kv, 2)
+    gains = jnp.stack([jnp.sum(joined(8), axis=0), jnp.sum(joined(9), axis=0)], axis=0)
+    for move in (c_move, x_move, y_move):
+        gains = gains + move(gains)
+    gains = gains + sum(z_move(gains, step) for step in range(1, ZS))
+    devices = ZS * YS * XS * CS
+    gains = take(gains.reshape(2, devices, model // devices), group * XS * CS + owner, 1)
+    return (
+        jnp.stack(outputs, axis=0),
+        jnp.stack(input_grads, axis=0),
+        gains[0],
+        gains[1],
+        grad_kv,
+        grad_query,
+        grad_out,
+        grad_gate_up,
+        grad_down,
+    )
+
+
+def owner_cap(local):
+    return XS * CS * CAP
+
+
 def solution(mesh):
     in_specs = (
         P(None, ("group", "expert"), None),
@@ -399,6 +809,7 @@
         P("expert", "group", None),
         P("expert", "group", None),
     )
+    body = fast_device if fits(mesh) else on_device
     return jax.shard_map(
-        on_device, mesh=mesh, in_specs=in_specs, out_specs=out_specs, check_vma=False
-    )
+        body, mesh=mesh, in_specs=in_specs, out_specs=out_specs, check_vma=False
+    )

time: 3870 us -> 1600 us (0.41)
  waiting for transfers between devices: 3090 us -> 694 us
  starting transfers between devices: 62.5 us -> 243 us
  matrix products: 472 us -> 299 us
  other arithmetic: 83.9 us -> 178 us
  Pallas kernels: 0 us -> 57.3 us
  blocking collectives: 43 us -> 0 us
    all_gather x7 -> x0, waiting for transfers between devices: 1490 us -> none  [the longest x1 780 us: on_device(): lax.all_gather(w_gate_up, 'group', axis=1, tiled=True)]
    reduce_scatter x6 -> x0, waiting for transfers between devices: 778 us -> none  [the longest x3 430 us: expert_reduce(): lax.psum_scatter(term(jnp.int32(0), lax.axis_size('group') * (left.shape[...]
    unnamed x15 -> x0, waiting for transfers between devices: 728 us -> none
    ppermute x0 -> x105, waiting for transfers between devices: none -> 679 us  [the longest x65 449 us: group_move(): return lax.ppermute(value, 'group', pairs)]
    ppermute x0 -> x105, starting transfers between devices: none -> 205 us  [the longest x65 173 us: group_move(): return lax.ppermute(value, 'group', pairs)]
    dot_general x53 -> x42, matrix products: 472 us -> 299 us  [the longest x10 93.4 us: dot_t(): lax.dot_general(left, right, (((1,), (1,)), ((), ())), preferred_element_...]
    all_to_all x16 -> x6, waiting for transfers between devices: 96 us -> 14.5 us  [z_exchange(): lax.all_to_all(value, 'group', split_axis=0, concat_axis=0, tiled=True, a...]
    pallas_call x0 -> x4, Pallas kernels: none -> 57.3 us  [the longest x2 30.5 us: attend_back(): pl.pallas_call(attend_back_kernel, grid=(seqs,), in_specs=[pl.BlockSpec((...]
  transfers between devices with their start and end apart: 30 -> 111, of which waited for: 21 -> 47; matrix products, arithmetic and copies ran while one was open for 14% -> 24% of each run, Pallas kernels for 0% -> 3%
where the time goes in v1:
time: 1600 us; the launch traced here: 1590 us
  waiting for transfers between devices  694 us (43%)
  matrix products  299 us (19%)
  starting transfers between devices  243 us (15%)
  other arithmetic  178 us (11%)
  local copies, waits for them, and re-layouts  112 us (7%)
  Pallas kernels  57.3 us (4%)
    ppermute x65, waiting for transfers between devices, group_move(): return lax.ppermute(value, 'group', pairs)  449 us
    ppermute x20, waiting for transfers between devices, x_move(): lax.ppermute(value, 'expert', [(x * CS + c, (1 - x) * CS + c) for x in ra...  228 us
    ppermute x65, starting transfers between devices, group_move(): return lax.ppermute(value, 'group', pairs)  173 us
    dot_general x10, matrix products, dot_t(): lax.dot_general(left, right, (((1,), (1,)), ((), ())), preferred_element_...  93.4 us
    dot_general x10, matrix products, dot(): return jnp.dot(left, right, preferred_element_type=F32)  80.4 us
    dot_general x4, matrix products, dot_l(): lax.dot_general(left, right, (((0,), (0,)), ((), ())), preferred_element_...  80.3 us
    all_to_all x6, starting transfers between devices, z_exchange(): lax.all_to_all(value, 'group', split_axis=0, concat_axis=0, tiled=True, a...  38.5 us
    select_n x9, other arithmetic, merge(): jnp.where(index == 0, jnp.stack([own, other], axis), jnp.stack([other, ow...  35 us
  transfers between devices with their start and end apart: 111, of which 47 were waited for; matrix products, arithmetic and copies ran while one was open for 24% of the time, Pallas kernels for 3%

profile of v1, /device:TPU:0, one launch (start us, length us, event | category | flops | bytes accessed | tf_op | source)
XLA Modules:
  0.0 1586.3 jit_solution(13402943176091341049)
XLA Ops:
  55.0 10.1 all-to-all-done.1
  95.3 15.9 %collective-permute-done.3 = bf16[4,80,2048]{2,1,0:T(8,128)(2,1)} collective-permute-done((bf16[4,80,2048]{2,1,0:T(8,128)(2,1)}, bf16[4,80,2048]{2,1,0:T(8,128)(2,1)}, u32[]{:S(2)}, u32[]{:S(2)}) %collective-permute-start.3) | collective-permute-done | bytes 1310752 | tf_op jit(solution)/shard_map/ppermute | solution.py:406
  114.5 19.1 %collective-permute-done.7 = bf16[4,2,64,1024]{3,2,1,0:T(8,128)(2,1)} collective-permute-done((bf16[4,2,64,1024]{3,2,1,0:T(8,128)(2,1)}, bf16[4,2,64,1024]{3,2,1,0:T(8,128)(2,1)}, u32[]{:S(2)}, u32[]{:S(2)}) %collective-permute-start.7) | collective-permute-done | bytes 1048608 | tf_op jit(solution)/shard_map/ppermute | solution.py:406
  158.9 10.0 collective-permute-done.5
  173.9 11.7 fusion.31.qkv_ref
  185.6 13.5 shard_map.205
  205.5 10.7 fusion.29.qkv_ref
  216.2 13.3 shard_map.206
  252.9 19.3 %collective-permute-done.16 = bf16[4,80,2048]{2,1,0:T(8,128)(2,1)S(1)} collective-permute-done((bf16[4,80,2048]{2,1,0:T(8,128)(2,1)S(1)}, bf16[4,80,2048]{2,1,0:T(8,128)(2,1)S(1)}, u32[]{:S(2)}, u32[]{:S(2)}) %collective-permute-start.16) | collective-permute-done | bytes 1310752 | tf_op jit(solution)/shard_map/ppermute | solution.py:406
  277.0 22.3 %collective-permute-done.38 = bf16[4,80,2048]{2,1,0:T(8,128)(2,1)S(1)} collective-permute-done((bf16[4,80,2048]{2,1,0:T(8,128)(2,1)S(1)}, bf16[4,80,2048]{2,1,0:T(8,128)(2,1)S(1)}, u32[]{:S(2)}, u32[]{:S(2)}) %collective-permute-start.38) | collective-permute-done | bytes 1310752 | tf_op jit(solution)/shard_map/ppermute | solution.py:406
  310.0 10.1 collective-permute-start.40
  323.3 18.2 %collective-permute-done.18 = bf16[80,2048]{1,0:T(8,128)(2,1)} collective-permute-done((bf16[80,2048]{1,0:T(8,128)(2,1)}, bf16[80,2048]{1,0:T(8,128)(2,1)}, u32[]{:S(2)}, u32[]{:S(2)}) %collective-permute-start.18) | collective-permute-done | bytes 327712 | tf_op jit(solution)/shard_map/ppermute | solution.py:394
  341.9 13.5 collective-permute-done.40
  361.6 15.0 collective-permute-done.21
  389.7 25.2 %collective-permute-done.23 = bf16[4,80,2048]{2,1,0:T(8,128)(2,1)} collective-permute-done((bf16[4,80,2048]{2,1,0:T(8,128)(2,1)}, bf16[4,80,2048]{2,1,0:T(8,128)(2,1)}, u32[]{:S(2)}, u32[]{:S(2)}) %collective-permute-start.23) | collective-permute-done | bytes 1310752 | tf_op jit(solution)/shard_map/ppermute | solution.py:406
  423.0 106.5 %collective-permute-done.26 = bf16[704,2048]{1,0:T(8,128)(2,1)} collective-permute-done((bf16[704,2048]{1,0:T(8,128)(2,1)}, bf16[704,2048]{1,0:T(8,128)(2,1)}, u32[]{:S(2)}, u32[]{:S(2)}) %collective-permute-start.26) | collective-permute-done | bytes 2883616 | tf_op jit(solution)/shard_map/ppermute | solution.py:394
  550.7 12.8 maximum_select_fusion
  563.5 15.2 copy.216
  578.7 16.3 %fusion.222 = f32[800,2816]{1,0:T(8,128)} fusion(bf16[800,2048]{1,0:T(8,128)(2,1)} %bitcast.693, bf16[2048,2816]{1,0:T(8,128)(2,1)} %bitcast.655), kind=kOutput, calls=%fused_computation.457 | convolution fusion | flops 9227468800 | bytes 23822336 | tf_op jit(solution)/shard_map/dot_general | solution.py:447
  595.0 12.5 multiply_convert_fusion.13
  618.9 13.1 fusion.49
  643.0 23.5 %collective-permute-done.28 = bf16[4,80,2048]{2,1,0:T(8,128)(2,1)S(1)} collective-permute-done((bf16[4,80,2048]{2,1,0:T(8,128)(2,1)S(1)}, bf16[4,80,2048]{2,1,0:T(8,128)(2,1)S(1)}, u32[]{:S(2)}, u32[]{:S(2)}) %collective-permute-start.28) | collective-permute-done | bytes 1310752 | tf_op jit(solution)/shard_map/ppermute | solution.py:406
  667.3 26.4 %collective-permute-done.58 = bf16[4,80,2048]{2,1,0:T(8,128)(2,1)S(1)} collective-permute-done((bf16[4,80,2048]{2,1,0:T(8,128)(2,1)S(1)}, bf16[4,80,2048]{2,1,0:T(8,128)(2,1)S(1)}, u32[]{:S(2)}, u32[]{:S(2)}) %collective-permute-start.58) | collective-permute-done | bytes 1310752 | tf_op jit(solution)/shard_map/ppermute | solution.py:406
  708.3 16.8 %collective-permute-done.30 = bf16[80,2048]{1,0:T(8,128)(2,1)S(1)} collective-permute-done((bf16[80,2048]{1,0:T(8,128)(2,1)S(1)}, bf16[80,2048]{1,0:T(8,128)(2,1)S(1)}, u32[]{:S(2)}, u32[]{:S(2)}) %collective-permute-start.30) | collective-permute-done | bytes 327712 | tf_op jit(solution)/shard_map/ppermute | solution.py:394
  725.0 17.6 %collective-permute-done.60 = bf16[80,2048]{1,0:T(8,128)(2,1)S(1)} collective-permute-done((bf16[80,2048]{1,0:T(8,128)(2,1)S(1)}, bf16[80,2048]{1,0:T(8,128)(2,1)S(1)}, u32[]{:S(2)}, u32[]{:S(2)}) %collective-permute-start.60) | collective-permute-done | bytes 327712 | tf_op jit(solution)/shard_map/ppermute | solution.py:394
  758.7 13.3 collective-permute-done.43
  775.8 27.1 %collective-permute-done.45 = bf16[4,80,2048]{2,1,0:T(8,128)(2,1)S(1)} collective-permute-done((bf16[4,80,2048]{2,1,0:T(8,128)(2,1)S(1)}, bf16[4,80,2048]{2,1,0:T(8,128)(2,1)S(1)}, u32[]{:S(2)}, u32[]{:S(2)}) %collective-permute-start.45) | collective-permute-done | bytes 1310752 | tf_op jit(solution)/shard_map/ppermute | solution.py:406
  821.7 13.4 fusion.223
  835.1 11.1 multiply_convert_fusion.11
  846.2 14.1 fusion.46
  872.9 32.3 %fusion.11 = f32[2048,2816]{1,0:T(8,128)} fusion(bf16[800,1408]{1,0:T(8,128)(2,1)} %get-tuple-element.68, bf16[800,1408]{1,0:T(8,128)(2,1)} %get-tuple-element.67, bf16[800,1408]{1,0:T(8,128)(2,1)} %get-tuple-element.66, bf16[800,1408]{1,0:T(8,128)(2,1)} %get-tuple-element.65, bf16[800,2048]{1,0:T(8,128)(2,1)} %bitcast.698, bf16[800,2048]{1,0:T(8,128)(2,1)} %bitcast.694), kind=kOutput, calls=%fused_computation.18 | convolution fusion | flops 18504089600 | bytes 38633472 | tf_op jit(solution)/shard_map/dot_general | solution.py:455
  913.3 15.9 %fusion.25 = f32[1408,2048]{1,0:T(8,128)} fusion(bf16[800,2048]{1,0:T(8,128)(2,1)S(1)} %bitcast.696, bf16[800,2048]{1,0:T(8,128)(2,1)S(1)} %bitcast.692, bf16[800,1408]{1,0:T(8,128)(2,1)} %get-tuple-element.70, bf16[800,1408]{1,0:T(8,128)(2,1)} %copy-done.77), kind=kOutput, calls=%fused_computation.32 | convolution fusion | flops 9249587200 | bytes 22593536 | tf_op jit(solution)/shard_map/dot_general | solution.py:455
  955.6 15.6 collective-permute-done.48
  994.7 14.0 collective-permute-done.50
  1023.2 12.9 collective-permute-done.63
  1038.9 17.4 %collective-permute-start.84 = (bf16[80,2048]{1,0:T(8,128)(2,1)}, bf16[80,2048]{1,0:T(8,128)(2,1)}, u32[]{:S(2)}, u32[]{:S(2)}) collective-permute-start(bf16[80,2048]{1,0:T(8,128)(2,1)} %get-tuple-element.129), channel_id=1, source_target_pairs={{0,8},{4,12},{8,16},{12,20},{16,24},{20,28},{24,0},{28,4},{1,9},{5... | collective-permute-start | bytes 983048 | tf_op jit(solution)/shard_map/ppermute | solution.py:394
  1091.7 35.0 %collective-permute-done.104 = bf16[704,2048]{1,0:T(8,128)(2,1)} collective-permute-done((bf16[704,2048]{1,0:T(8,128)(2,1)}, bf16[704,2048]{1,0:T(8,128)(2,1)}, u32[]{:S(2)}, u32[]{:S(2)}) %collective-permute-start.104) | collective-permute-done | bytes 2883616 | tf_op jit(solution)/shard_map/ppermute | solution.py:394
  1135.5 9.7 fusion
  1151.8 15.4 shard_map.207
  1181.1 15.1 shard_map.208
  1198.7 21.8 %fusion.1 = f32[2048,1536]{1,0:T(8,128)} fusion(bf16[1280,2048]{1,0:T(8,128)(2,1)} %bitcast.680, bf16[1280,2048]{1,0:T(8,128)(2,1)S(1)} %bitcast.679, bf16[1280,1536]{1,0:T(8,128)(2,1)S(1)} %bitcast.630, bf16[1280,1536]{1,0:T(8,128)(2,1)S(1)} %bitcast.629), kind=kOutput, calls=%fused_computation.4 | convolution fusion | flops 16142827520 | bytes 30932992 | tf_op jit(solution)/shard_map/dot_general | solution.py:455
  1223.1 9.8 slice.586
  1289.9 10.2 fusion.5
  1325.8 25.0 %collective-permute-done.100 = bf16[4,64,1024]{2,1,0:T(8,128)(2,1)S(1)} collective-permute-done((bf16[4,64,1024]{2,1,0:T(8,128)(2,1)S(1)}, bf16[4,64,1024]{2,1,0:T(8,128)(2,1)S(1)}, u32[]{:S(2)}, u32[]{:S(2)}) %collective-permute-start.100) | collective-permute-done | bytes 524320 | tf_op jit(solution)/shard_map/ppermute | solution.py:394
  1391.2 18.0 %collective-permute-done.88 = bf16[4,80,2048]{2,1,0:T(8,128)(2,1)S(1)} collective-permute-done((bf16[4,80,2048]{2,1,0:T(8,128)(2,1)S(1)}, bf16[4,80,2048]{2,1,0:T(8,128)(2,1)S(1)}, u32[]{:S(2)}, u32[]{:S(2)}) %collective-permute-start.88) | collective-permute-done | bytes 1310752 | tf_op jit(solution)/shard_map/ppermute | solution.py:406
  1413.7 67.1 %collective-permute-done.69 = bf16[80,2048]{1,0:T(8,128)(2,1)S(1)} collective-permute-done((bf16[80,2048]{1,0:T(8,128)(2,1)S(1)}, bf16[80,2048]{1,0:T(8,128)(2,1)S(1)}, u32[]{:S(2)}, u32[]{:S(2)}) %collective-permute-start.69) | collective-permute-done | bytes 327712 | tf_op jit(solution)/shard_map/ppermute | solution.py:394
  1480.8 55.2 %collective-permute-start.90 = (bf16[80,2048]{1,0:T(8,128)(2,1)S(1)}, bf16[80,2048]{1,0:T(8,128)(2,1)S(1)}, u32[]{:S(2)}, u32[]{:S(2)}) collective-permute-start(bf16[80,2048]{1,0:T(8,128)(2,1)S(1)} %get-tuple-element.83), channel_id=1, source_target_pairs={{0,16},{4,20},{8,24},{12,28},{16,0},{20,4},{24,8},{28,12},{1,17},{... | collective-permute-start | bytes 983048 | tf_op jit(solution)/shard_map/ppermute | solution.py:394
  1545.0 13.0 collective-permute-done.90
  (629 shorter events, 612.4 us)
Async XLA Ops:
  15.6 58.9 %collective-permute-start.1 = (bf16[80,2048]{1,0:T(8,128)(2,1)}, bf16[80,2048]{1,0:T(8,128)(2,1)}, u32[]{:S(2)}, u32[]{:S(2)}) collective-permute-start(bf16[80,2048]{1,0:T(8,128)(2,1)} %get-tuple-element.133), channel_id=1, source_target_pairs={{0,16},{4,20},{8,24},{12,28},{16,0},{20,4},{24,8},{28,12},{1,17},{... | collective-permute-start | bytes 983048 | tf_op jit(solution)/shard_map/ppermute | solution.py:394
  18.9 46.1 %all-to-all-start.1 = ((bf16[4,64,1024]{2,1,0:T(8,128)(2,1)}), bf16[4,64,1024]{2,1,0:T(8,128)(2,1)S(1)}, u32[]{:S(2)}, u32[]{:S(2)}) async-start(bf16[4,64,1024]{2,1,0:T(8,128)(2,1)} %reshape.835), calls=%async_computation.1 | async-start | bytes 1048576 | tf_op jit(solution)/shard_map/all_to_all | solution.py:415
  24.9 51.4 %collective-permute-start = (bf16[80,2048]{1,0:T(8,128)(2,1)}, bf16[80,2048]{1,0:T(8,128)(2,1)}, u32[]{:S(2)}, u32[]{:S(2)}) collective-permute-start(bf16[80,2048]{1,0:T(8,128)(2,1)} %get-tuple-element.133), channel_id=1, source_target_pairs={{0,24},{4,28},{8,0},{12,4},{16,8},{20,12},{24,16},{28,20},{1,25},{... | collective-permute-start | bytes 983048 | tf_op jit(solution)/shard_map/ppermute | solution.py:394
  28.8 60.8 %collective-permute-start.34 = (bf16[80,2048]{1,0:T(8,128)(2,1)}, bf16[80,2048]{1,0:T(8,128)(2,1)}, u32[]{:S(2)}, u32[]{:S(2)}) collective-permute-start(bf16[80,2048]{1,0:T(8,128)(2,1)} %get-tuple-element.134), channel_id=1, source_target_pairs={{0,8},{4,12},{8,16},{12,20},{16,24},{20,28},{24,0},{28,4},{1,9},{5... | collective-permute-start | bytes 983048 | tf_op jit(solution)/shard_map/ppermute | solution.py:394
  50.5 40.7 %collective-permute-start.33 = (bf16[80,2048]{1,0:T(8,128)(2,1)}, bf16[80,2048]{1,0:T(8,128)(2,1)}, u32[]{:S(2)}, u32[]{:S(2)}) collective-permute-start(bf16[80,2048]{1,0:T(8,128)(2,1)} %get-tuple-element.134), channel_id=1, source_target_pairs={{0,16},{4,20},{8,24},{12,28},{16,0},{20,4},{24,8},{28,12},{1,17},{... | collective-permute-start | bytes 983048 | tf_op jit(solution)/shard_map/ppermute | solution.py:394
  52.3 38.8 %collective-permute-start.32 = (bf16[80,2048]{1,0:T(8,128)(2,1)}, bf16[80,2048]{1,0:T(8,128)(2,1)}, u32[]{:S(2)}, u32[]{:S(2)}) collective-permute-start(bf16[80,2048]{1,0:T(8,128)(2,1)} %get-tuple-element.134), channel_id=1, source_target_pairs={{0,24},{4,28},{8,0},{12,4},{16,8},{20,12},{24,16},{28,20},{1,25},{... | collective-permute-start | bytes 983048 | tf_op jit(solution)/shard_map/ppermute | solution.py:394
  65.1 72.5 %all-to-all-start = ((bf16[4,256,512]{2,1,0:T(8,128)(2,1)}), bf16[4,256,512]{2,1,0:T(8,128)(2,1)}, u32[]{:S(2)}, u32[]{:S(2)}) async-start(bf16[4,256,512]{2,1,0:T(8,128)(2,1)} %bitcast.628), calls=%async_computation | async-start | bytes 2097152 | tf_op jit(solution)/shard_map/all_to_all | solution.py:415
  85.0 48.6 %collective-permute-start.7 = (bf16[4,2,64,1024]{3,2,1,0:T(8,128)(2,1)}, bf16[4,2,64,1024]{3,2,1,0:T(8,128)(2,1)}, u32[]{:S(2)}, u32[]{:S(2)}) collective-permute-start(bf16[4,2,64,1024]{3,2,1,0:T(8,128)(2,1)} %maximum_select_fusion.6), channel_id=1, source_target_pairs={{0,2},{1,3},{2,0},{3,1},{4,6},{5,7},{6,4},{7,5},{8,10},{9,11},{10,... | collective-permute-start | bytes 3145736 | tf_op jit(solution)/shard_map/ppermute | solution.py:406
  89.5 53.9 %collective-permute-start.14 = (bf16[256,2048]{1,0:T(8,128)(2,1)}, bf16[256,2048]{1,0:T(8,128)(2,1)}, u32[]{:S(2)}, u32[]{:S(2)}) collective-permute-start(bf16[256,2048]{1,0:T(8,128)(2,1)} %bitcast.729), channel_id=1, source_target_pairs={{0,4},{4,0},{8,12},{12,8},{16,20},{20,16},{24,28},{28,24},{1,5},{5... | collective-permute-start | bytes 3145736 | tf_op jit(solution)/shard_map/ppermute | solution.py:394
  94.1 59.8 %collective-permute-start.35 = (bf16[4,80,2048]{2,1,0:T(8,128)(2,1)}, bf16[4,80,2048]{2,1,0:T(8,128)(2,1)}, u32[]{:S(2)}, u32[]{:S(2)}) collective-permute-start(bf16[4,80,2048]{2,1,0:T(8,128)(2,1)} %get-tuple-element.124), channel_id=1, source_target_pairs={{0,2},{1,3},{2,0},{3,1},{4,6},{5,7},{6,4},{7,5},{8,10},{9,11},{10,... | collective-permute-start | bytes 3932168 | tf_op jit(solution)/shard_map/ppermute | solution.py:406
  114.5 59.4 %collective-permute-start.4 = (bf16[4,160,2048]{2,1,0:T(8,128)(2,1)}, bf16[4,160,2048]{2,1,0:T(8,128)(2,1)}, u32[]{:S(2)}, u32[]{:S(2)}) collective-permute-start(bf16[4,160,2048]{2,1,0:T(8,128)(2,1)} %bitcast.7), channel_id=1, source_target_pairs={{0,1},{1,0},{2,3},{3,2},{4,5},{5,4},{6,7},{7,6},{8,9},{9,8},{10,11... | collective-permute-start | bytes 7864328 | tf_op jit(solution)/shard_map/ppermute | solution.py:410
  137.6 185.7 %all-to-all-start.2 = ((bf16[4,256,2816]{1,2,0:T(8,128)(2,1)}), bf16[4,256,2816]{1,2,0:T(8,128)(2,1)}, u32[]{:S(2)}, u32[]{:S(2)}) async-start(bf16[4,256,2816]{1,2,0:T(8,128)(2,1)} %bitcast.639), calls=%async_computation.2 | async-start | bytes 11534336 | tf_op jit(solution)/shard_map/all_to_all | solution.py:415
  155.8 49.7 %collective-permute-start.36 = (bf16[4,160,2048]{2,1,0:T(8,128)(2,1)S(1)}, bf16[4,160,2048]{2,1,0:T(8,128)(2,1)}, u32[]{:S(2)}, u32[]{:S(2)}) collective-permute-start(bf16[4,160,2048]{2,1,0:T(8,128)(2,1)S(1)} %bitcast.661), channel_id=1, source_target_pairs={{0,1},{1,0},{2,3},{3,2},{4,5},{5,4},{6,7},{7,6},{8,9},{9,8},{10,11... | collective-permute-start | bytes 7864328 | tf_op jit(solution)/shard_map/ppermute | solution.py:410
  246.5 52.8 %collective-permute-start.38 = (bf16[4,80,2048]{2,1,0:T(8,128)(2,1)S(1)}, bf16[4,80,2048]{2,1,0:T(8,128)(2,1)S(1)}, u32[]{:S(2)}, u32[]{:S(2)}) collective-permute-start(bf16[4,80,2048]{2,1,0:T(8,128)(2,1)S(1)} %slice.863), channel_id=1, source_target_pairs={{0,2},{1,3},{2,0},{3,1},{4,6},{5,7},{6,4},{7,5},{8,10},{9,11},{10,... | collective-permute-start | bytes 3932168 | tf_op jit(solution)/shard_map/ppermute | solution.py:406
  248.0 58.1 %collective-permute-start.53 = (bf16[80,2048]{1,0:T(8,128)(2,1)S(1)}, bf16[80,2048]{1,0:T(8,128)(2,1)S(1)}, u32[]{:S(2)}, u32[]{:S(2)}) collective-permute-start(bf16[80,2048]{1,0:T(8,128)(2,1)S(1)} %get-tuple-element.138), channel_id=1, source_target_pairs={{0,16},{4,20},{8,24},{12,28},{16,0},{20,4},{24,8},{28,12},{1,17},{... | collective-permute-start | bytes 983048 | tf_op jit(solution)/shard_map/ppermute | solution.py:394
  250.9 55.3 %collective-permute-start.52 = (bf16[80,2048]{1,0:T(8,128)(2,1)S(1)}, bf16[80,2048]{1,0:T(8,128)(2,1)S(1)}, u32[]{:S(2)}, u32[]{:S(2)}) collective-permute-start(bf16[80,2048]{1,0:T(8,128)(2,1)S(1)} %get-tuple-element.138), channel_id=1, source_target_pairs={{0,24},{4,28},{8,0},{12,4},{16,8},{20,12},{24,16},{28,20},{1,25},{... | collective-permute-start | bytes 983048 | tf_op jit(solution)/shard_map/ppermute | solution.py:394
  252.4 54.8 %collective-permute-start.54 = (bf16[80,2048]{1,0:T(8,128)(2,1)S(1)}, bf16[80,2048]{1,0:T(8,128)(2,1)S(1)}, u32[]{:S(2)}, u32[]{:S(2)}) collective-permute-start(bf16[80,2048]{1,0:T(8,128)(2,1)S(1)} %get-tuple-element.138), channel_id=1, source_target_pairs={{0,8},{4,12},{8,16},{12,20},{16,24},{20,28},{24,0},{28,4},{1,9},{5... | collective-permute-start | bytes 983048 | tf_op jit(solution)/shard_map/ppermute | solution.py:394
  310.0 45.4 %collective-permute-start.40 = (bf16[80,2048]{1,0:T(8,128)(2,1)}, bf16[80,2048]{1,0:T(8,128)(2,1)}, u32[]{:S(2)}, u32[]{:S(2)}) collective-permute-start(bf16[80,2048]{1,0:T(8,128)(2,1)} %get-tuple-element.120), channel_id=1, source_target_pairs={{0,16},{4,20},{8,24},{12,28},{16,0},{20,4},{24,8},{28,12},{1,17},{... | collective-permute-start | bytes 983048 | tf_op jit(solution)/shard_map/ppermute | solution.py:394
  321.8 64.4 %collective-permute-start.55 = (bf16[4,80,2048]{2,1,0:T(8,128)(2,1)}, bf16[4,80,2048]{2,1,0:T(8,128)(2,1)}, u32[]{:S(2)}, u32[]{:S(2)}) collective-permute-start(bf16[4,80,2048]{2,1,0:T(8,128)(2,1)} %get-tuple-element.95), channel_id=1, source_target_pairs={{0,2},{1,3},{2,0},{3,1},{4,6},{5,7},{6,4},{7,5},{8,10},{9,11},{10,... | collective-permute-start | bytes 3932168 | tf_op jit(solution)/shard_map/ppermute | solution.py:406
  341.5 209.2 %collective-permute-start.25 = (bf16[4,256,2816]{1,2,0:T(8,128)(2,1)}, bf16[4,256,2816]{1,2,0:T(8,128)(2,1)}, u32[]{:S(2)}, u32[]{:S(2)}) collective-permute-start(bf16[4,256,2816]{1,2,0:T(8,128)(2,1)} %all-to-all-done.2), channel_id=1, source_target_pairs={{0,4},{4,0},{8,12},{12,8},{16,20},{20,16},{24,28},{28,24},{1,5},{5... | collective-permute-start | bytes 17301512 | tf_op jit(solution)/shard_map/ppermute | solution.py:394
  376.6 152.9 %collective-permute-start.26 = (bf16[704,2048]{1,0:T(8,128)(2,1)}, bf16[704,2048]{1,0:T(8,128)(2,1)}, u32[]{:S(2)}, u32[]{:S(2)}) collective-permute-start(bf16[704,2048]{1,0:T(8,128)(2,1)} %bitcast.74), channel_id=1, source_target_pairs={{0,4},{4,0},{8,12},{12,8},{16,20},{20,16},{24,28},{28,24},{1,5},{5... | collective-permute-start | bytes 8650760 | tf_op jit(solution)/shard_map/ppermute | solution.py:394
  389.6 148.6 %collective-permute-start.56 = (bf16[4,160,2048]{2,1,0:T(8,128)(2,1)}, bf16[4,160,2048]{2,1,0:T(8,128)(2,1)}, u32[]{:S(2)}, u32[]{:S(2)}) collective-permute-start(bf16[4,160,2048]{2,1,0:T(8,128)(2,1)} %bitcast.130), channel_id=1, source_target_pairs={{0,1},{1,0},{2,3},{3,2},{4,5},{5,4},{6,7},{7,6},{8,9},{9,8},{10,11... | collective-permute-start | bytes 7864328 | tf_op jit(solution)/shard_map/ppermute | solution.py:410
  418.6 127.4 %collective-permute-start.24 = (bf16[4,160,2048]{2,1,0:T(8,128)(2,1)}, bf16[4,160,2048]{2,1,0:T(8,128)(2,1)}, u32[]{:S(2)}, u32[]{:S(2)}) collective-permute-start(bf16[4,160,2048]{2,1,0:T(8,128)(2,1)} %bitcast.65), channel_id=1, source_target_pairs={{0,1},{1,0},{2,3},{3,2},{4,5},{5,4},{6,7},{7,6},{8,9},{9,8},{10,11... | collective-permute-start | bytes 7864328 | tf_op jit(solution)/shard_map/ppermute | solution.py:410
  639.3 54.3 %collective-permute-start.58 = (bf16[4,80,2048]{2,1,0:T(8,128)(2,1)S(1)}, bf16[4,80,2048]{2,1,0:T(8,128)(2,1)S(1)}, u32[]{:S(2)}, u32[]{:S(2)}) collective-permute-start(bf16[4,80,2048]{2,1,0:T(8,128)(2,1)S(1)} %slice.861), channel_id=1, source_target_pairs={{0,2},{1,3},{2,0},{3,1},{4,6},{5,7},{6,4},{7,5},{8,10},{9,11},{10,... | collective-permute-start | bytes 3932168 | tf_op jit(solution)/shard_map/ppermute | solution.py:406
  640.9 55.0 %collective-permute-start.73 = (bf16[80,2048]{1,0:T(8,128)(2,1)S(1)}, bf16[80,2048]{1,0:T(8,128)(2,1)S(1)}, u32[]{:S(2)}, u32[]{:S(2)}) collective-permute-start(bf16[80,2048]{1,0:T(8,128)(2,1)S(1)} %copy-done.49), channel_id=1, source_target_pairs={{0,16},{4,20},{8,24},{12,28},{16,0},{20,4},{24,8},{28,12},{1,17},{... | collective-permute-start | bytes 983048 | tf_op jit(solution)/shard_map/ppermute | solution.py:394
  640.9 55.1 %collective-permute-start.72 = (bf16[80,2048]{1,0:T(8,128)(2,1)S(1)}, bf16[80,2048]{1,0:T(8,128)(2,1)S(1)}, u32[]{:S(2)}, u32[]{:S(2)}) collective-permute-start(bf16[80,2048]{1,0:T(8,128)(2,1)S(1)} %copy-done.49), channel_id=1, source_target_pairs={{0,24},{4,28},{8,0},{12,4},{16,8},{20,12},{24,16},{28,20},{1,25},{... | collective-permute-start | bytes 983048 | tf_op jit(solution)/shard_map/ppermute | solution.py:394
  642.4 54.1 %collective-permute-start.74 = (bf16[80,2048]{1,0:T(8,128)(2,1)S(1)}, bf16[80,2048]{1,0:T(8,128)(2,1)S(1)}, u32[]{:S(2)}, u32[]{:S(2)}) collective-permute-start(bf16[80,2048]{1,0:T(8,128)(2,1)S(1)} %copy-done.49), channel_id=1, source_target_pairs={{0,8},{4,12},{8,16},{12,20},{16,24},{20,28},{24,0},{28,4},{1,9},{5... | collective-permute-start | bytes 983048 | tf_op jit(solution)/shard_map/ppermute | solution.py:394
  699.9 42.7 %collective-permute-start.60 = (bf16[80,2048]{1,0:T(8,128)(2,1)S(1)}, bf16[80,2048]{1,0:T(8,128)(2,1)S(1)}, u32[]{:S(2)}, u32[]{:S(2)}) collective-permute-start(bf16[80,2048]{1,0:T(8,128)(2,1)S(1)} %get-tuple-element.93), channel_id=1, source_target_pairs={{0,16},{4,20},{8,24},{12,28},{16,0},{20,4},{24,8},{28,12},{1,17},{... | collective-permute-start | bytes 983048 | tf_op jit(solution)/shard_map/ppermute | solution.py:394
  706.2 67.6 %collective-permute-start.75 = (bf16[4,80,2048]{2,1,0:T(8,128)(2,1)S(1)}, bf16[4,80,2048]{2,1,0:T(8,128)(2,1)S(1)}, u32[]{:S(2)}, u32[]{:S(2)}) collective-permute-start(bf16[4,80,2048]{2,1,0:T(8,128)(2,1)S(1)} %get-tuple-element.100), channel_id=1, source_target_pairs={{0,2},{1,3},{2,0},{3,1},{4,6},{5,7},{6,4},{7,5},{8,10},{9,11},{10,... | collective-permute-start | bytes 3932168 | tf_op jit(solution)/shard_map/ppermute | solution.py:406
  872.3 56.9 %collective-permute-start.47 = (bf16[4,160,2048]{2,1,0:T(8,128)(2,1)}, bf16[4,160,2048]{2,1,0:T(8,128)(2,1)S(1)}, u32[]{:S(2)}, u32[]{:S(2)}) collective-permute-start(bf16[4,160,2048]{2,1,0:T(8,128)(2,1)} %convolution_convert_fusion.8), channel_id=1, source_target_pairs={{0,1},{1,0},{2,3},{3,2},{4,5},{5,4},{6,7},{7,6},{8,9},{9,8},{10,11... | collective-permute-start | bytes 7864328 | tf_op jit(solution)/shard_map/ppermute | solution.py:410
  930.6 40.7 %collective-permute-start.48 = (bf16[4,80,2048]{2,1,0:T(8,128)(2,1)S(1)}, bf16[4,80,2048]{2,1,0:T(8,128)(2,1)S(1)}, u32[]{:S(2)}, u32[]{:S(2)}) collective-permute-start(bf16[4,80,2048]{2,1,0:T(8,128)(2,1)S(1)} %slice.862), channel_id=1, source_target_pairs={{0,2},{1,3},{2,0},{3,1},{4,6},{5,7},{6,4},{7,5},{8,10},{9,11},{10,... | collective-permute-start | bytes 3932168 | tf_op jit(solution)/shard_map/ppermute | solution.py:406
  938.5 196.9 %collective-permute-start.103 = (bf16[4,256,2816]{2,1,0:T(8,128)(2,1)}, bf16[4,256,2816]{2,1,0:T(8,128)(2,1)}, u32[]{:S(2)}, u32[]{:S(2)}) collective-permute-start(bf16[4,256,2816]{2,1,0:T(8,128)(2,1)} %fusion.33), channel_id=1, source_target_pairs={{0,4},{4,0},{8,12},{12,8},{16,20},{20,16},{24,28},{28,24},{1,5},{5... | collective-permute-start | bytes 17301512 | tf_op jit(solution)/shard_map/ppermute | solution.py:394
  1019.7 107.0 %collective-permute-start.104 = (bf16[704,2048]{1,0:T(8,128)(2,1)}, bf16[704,2048]{1,0:T(8,128)(2,1)}, u32[]{:S(2)}, u32[]{:S(2)}) collective-permute-start(bf16[704,2048]{1,0:T(8,128)(2,1)} %fusion.52), channel_id=1, source_target_pairs={{0,4},{4,0},{8,12},{12,8},{16,20},{20,16},{24,28},{28,24},{1,5},{5... | collective-permute-start | bytes 8650760 | tf_op jit(solution)/shard_map/ppermute | solution.py:394
  1037.4 40.3 %collective-permute-start.65 = (bf16[4,80,2048]{2,1,0:T(8,128)(2,1)}, bf16[4,80,2048]{2,1,0:T(8,128)(2,1)}, u32[]{:S(2)}, u32[]{:S(2)}) collective-permute-start(bf16[4,80,2048]{2,1,0:T(8,128)(2,1)} %get-tuple-element.90), channel_id=1, source_target_pairs={{0,2},{1,3},{2,0},{3,1},{4,6},{5,7},{6,4},{7,5},{8,10},{9,11},{10,... | collective-permute-start | bytes 3932168 | tf_op jit(solution)/shard_map/ppermute | solution.py:406
  1077.1 56.3 %collective-permute-start.85 = (bf16[4,80,2048]{2,1,0:T(8,128)(2,1)S(1)}, bf16[4,80,2048]{2,1,0:T(8,128)(2,1)S(1)}, u32[]{:S(2)}, u32[]{:S(2)}) collective-permute-start(bf16[4,80,2048]{2,1,0:T(8,128)(2,1)S(1)} %get-tuple-element.85), channel_id=1, source_target_pairs={{0,2},{1,3},{2,0},{3,1},{4,6},{5,7},{6,4},{7,5},{8,10},{9,11},{10,... | collective-permute-start | bytes 3932168 | tf_op jit(solution)/shard_map/ppermute | solution.py:406
  1081.1 64.1 %collective-permute-start.66 = (bf16[4,160,2048]{2,1,0:T(8,128)(2,1)}, bf16[4,160,2048]{2,1,0:T(8,128)(2,1)}, u32[]{:S(2)}, u32[]{:S(2)}) collective-permute-start(bf16[4,160,2048]{2,1,0:T(8,128)(2,1)} %bitcast.144), channel_id=1, source_target_pairs={{0,1},{1,0},{2,3},{3,2},{4,5},{5,4},{6,7},{7,6},{8,9},{9,8},{10,11... | collective-permute-start | bytes 7864328 | tf_op jit(solution)/shard_map/ppermute | solution.py:410
  1251.7 67.2 %collective-permute-start.67 = (bf16[4,160,2048]{2,1,0:T(8,128)(2,1)}, bf16[4,160,2048]{2,1,0:T(8,128)(2,1)}, u32[]{:S(2)}, u32[]{:S(2)}) collective-permute-start(bf16[4,160,2048]{2,1,0:T(8,128)(2,1)} %bitcast.770), channel_id=1, source_target_pairs={{0,1},{1,0},{2,3},{3,2},{4,5},{5,4},{6,7},{7,6},{8,9},{9,8},{10,11... | collective-permute-start | bytes 7864328 | tf_op jit(solution)/shard_map/ppermute | solution.py:410
  1260.2 115.3 %collective-permute-start.87 = (bf16[4,160,2048]{2,1,0:T(8,128)(2,1)}, bf16[4,160,2048]{2,1,0:T(8,128)(2,1)}, u32[]{:S(2)}, u32[]{:S(2)}) collective-permute-start(bf16[4,160,2048]{2,1,0:T(8,128)(2,1)} %bitcast.184), channel_id=1, source_target_pairs={{0,1},{1,0},{2,3},{3,2},{4,5},{5,4},{6,7},{7,6},{8,9},{9,8},{10,11... | collective-permute-start | bytes 7864328 | tf_op jit(solution)/shard_map/ppermute | solution.py:410
  1302.6 49.0 %all-to-all-start.4 = ((bf16[4,256,512]{2,1,0:T(8,128)(2,1)}), bf16[4,256,512]{2,1,0:T(8,128)(2,1)S(1)}, u32[]{:S(2)}, u32[]{:S(2)}) async-start(bf16[4,256,512]{2,1,0:T(8,128)(2,1)} %fusion.58), calls=%async_computation.4 | async-start | bytes 2097152 | tf_op jit(solution)/shard_map/all_to_all | solution.py:415
  1314.2 67.0 %collective-permute-start.102 = (bf16[256,2048]{1,0:T(8,128)(2,1)}, bf16[256,2048]{1,0:T(8,128)(2,1)}, u32[]{:S(2)}, u32[]{:S(2)}) collective-permute-start(bf16[256,2048]{1,0:T(8,128)(2,1)} %fusion.72), channel_id=1, source_target_pairs={{0,4},{4,0},{8,12},{12,8},{16,20},{20,16},{24,28},{28,24},{1,5},{5... | collective-permute-start | bytes 3145736 | tf_op jit(solution)/shard_map/ppermute | solution.py:394
  1324.1 60.2 %collective-permute-start.68 = (bf16[4,80,2048]{2,1,0:T(8,128)(2,1)S(1)}, bf16[4,80,2048]{2,1,0:T(8,128)(2,1)}, u32[]{:S(2)}, u32[]{:S(2)}) collective-permute-start(bf16[4,80,2048]{2,1,0:T(8,128)(2,1)S(1)} %slice.860), channel_id=1, source_target_pairs={{0,2},{1,3},{2,0},{3,1},{4,6},{5,7},{6,4},{7,5},{8,10},{9,11},{10,... | collective-permute-start | bytes 3932168 | tf_op jit(solution)/shard_map/ppermute | solution.py:406
  1370.1 205.9 %all-to-all-start.5 = ((bf16[4,256,2816]{2,1,0:T(8,128)(2,1)}), bf16[4,256,2816]{2,1,0:T(8,128)(2,1)}, u32[]{:S(2)}, u32[]{:S(2)}) async-start(bf16[4,256,2816]{2,1,0:T(8,128)(2,1)} %fusion), calls=%async_computation.5 | async-start | bytes 11534336 | tf_op jit(solution)/shard_map/all_to_all | solution.py:415
  1386.3 94.6 %collective-permute-start.69 = (bf16[80,2048]{1,0:T(8,128)(2,1)S(1)}, bf16[80,2048]{1,0:T(8,128)(2,1)S(1)}, u32[]{:S(2)}, u32[]{:S(2)}) collective-permute-start(bf16[80,2048]{1,0:T(8,128)(2,1)S(1)} %get-tuple-element.86), channel_id=1, source_target_pairs={{0,8},{4,12},{8,16},{12,20},{16,24},{20,28},{24,0},{28,4},{1,9},{5... | collective-permute-start | bytes 983048 | tf_op jit(solution)/shard_map/ppermute | solution.py:394
  1388.3 149.4 %collective-permute-start.71 = (bf16[80,2048]{1,0:T(8,128)(2,1)S(1)}, bf16[80,2048]{1,0:T(8,128)(2,1)S(1)}, u32[]{:S(2)}, u32[]{:S(2)}) collective-permute-start(bf16[80,2048]{1,0:T(8,128)(2,1)S(1)} %get-tuple-element.87), channel_id=1, source_target_pairs={{0,24},{4,28},{8,0},{12,4},{16,8},{20,12},{24,16},{28,20},{1,25},{... | collective-permute-start | bytes 983048 | tf_op jit(solution)/shard_map/ppermute | solution.py:394
  1390.2 154.8 %collective-permute-start.70 = (bf16[80,2048]{1,0:T(8,128)(2,1)S(1)}, bf16[80,2048]{1,0:T(8,128)(2,1)S(1)}, u32[]{:S(2)}, u32[]{:S(2)}) collective-permute-start(bf16[80,2048]{1,0:T(8,128)(2,1)S(1)} %get-tuple-element.88), channel_id=1, source_target_pairs={{0,16},{4,20},{8,24},{12,28},{16,0},{20,4},{24,8},{28,12},{1,17},{... | collective-permute-start | bytes 983048 | tf_op jit(solution)/shard_map/ppermute | solution.py:394
  1409.8 135.1 %collective-permute-start.89 = (bf16[80,2048]{1,0:T(8,128)(2,1)S(1)}, bf16[80,2048]{1,0:T(8,128)(2,1)S(1)}, u32[]{:S(2)}, u32[]{:S(2)}) collective-permute-start(bf16[80,2048]{1,0:T(8,128)(2,1)S(1)} %get-tuple-element.81), channel_id=1, source_target_pairs={{0,8},{4,12},{8,16},{12,20},{16,24},{20,28},{24,0},{28,4},{1,9},{5... | collective-permute-start | bytes 983048 | tf_op jit(solution)/shard_map/ppermute | solution.py:394
  1411.6 133.4 %collective-permute-start.91 = (bf16[80,2048]{1,0:T(8,128)(2,1)S(1)}, bf16[80,2048]{1,0:T(8,128)(2,1)S(1)}, u32[]{:S(2)}, u32[]{:S(2)}) collective-permute-start(bf16[80,2048]{1,0:T(8,128)(2,1)S(1)} %get-tuple-element.82), channel_id=1, source_target_pairs={{0,24},{4,28},{8,0},{12,4},{16,8},{20,12},{24,16},{28,20},{1,25},{... | collective-permute-start | bytes 983048 | tf_op jit(solution)/shard_map/ppermute | solution.py:394
  1480.8 77.1 %collective-permute-start.90 = (bf16[80,2048]{1,0:T(8,128)(2,1)S(1)}, bf16[80,2048]{1,0:T(8,128)(2,1)S(1)}, u32[]{:S(2)}, u32[]{:S(2)}) collective-permute-start(bf16[80,2048]{1,0:T(8,128)(2,1)S(1)} %get-tuple-element.83), channel_id=1, source_target_pairs={{0,16},{4,20},{8,24},{12,28},{16,0},{20,4},{24,8},{28,12},{1,17},{... | collective-permute-start | bytes 983048 | tf_op jit(solution)/shard_map/ppermute | solution.py:394
  (159 other events, 4201.0 us)

commit v2 on v0

--- a/solution.py
+++ b/solution.py
@@ -1,6 +1,10 @@
+import functools
+
 import jax
 import jax.numpy as jnp
 from jax import lax
+from jax.experimental import pallas as pl
+from jax.experimental.pallas import tpu as pltpu
 from jax.sharding import PartitionSpec as P
 
 HEADS = 16
@@ -371,6 +375,1174 @@
     )
 
 
+ZS, YS, XS, CS = 4, 2, 2, 2
+SEQ = 320
+F32 = jnp.float32
+BF16 = jnp.bfloat16
+
+
+def fits(mesh):
+    return mesh.shape["group"] == ZS * YS and mesh.shape["expert"] == XS * CS
+
+
+def group_move(value, move):
+    pairs = []
+    for z in range(ZS):
+        for y in range(YS):
+            to_z, to_y = move(z, y)
+            pairs.append((z * YS + y, to_z * YS + to_y))
+    return lax.ppermute(value, "group", pairs)
+
+
+def z_move(value, step):
+    return group_move(value, lambda z, y: ((z + step) % ZS, y))
+
+
+def y_move(value):
+    return group_move(value, lambda z, y: (z, 1 - y))
+
+
+def x_move(value):
+    return lax.ppermute(value, "expert", [(x * CS + c, (1 - x) * CS + c) for x in range(XS) for c in range(CS)])
+
+
+def c_move(value):
+    return lax.ppermute(value, "expert", [(x * CS + c, x * CS + 1 - c) for x in range(XS) for c in range(CS)])
+
+
+def z_exchange(value):
+    columns = [[z * YS + y for z in range(ZS)] for y in range(YS)]
+    return lax.all_to_all(
+        value, "group", split_axis=0, concat_axis=0, tiled=True, axis_index_groups=columns
+    )
+
+
+def gather_tokens(own):
+    column = jnp.stack([own] + [z_move(own, -step) for step in range(1, ZS)], axis=0)
+    plane = jnp.stack([column, x_move(column)], axis=1)
+    plane = plane.reshape((ZS, XS * own.shape[0]) + own.shape[1:])
+    return jnp.stack([plane, c_move(plane)], axis=0)
+
+
+def reduce_tokens(other, mine):
+    local = mine.shape[1] // XS
+    total = mine.astype(F32) + c_move(other).astype(F32)
+    arrived = x_move(total[:, local:].astype(BF16))
+    total = total[:, :local] + arrived.astype(F32)
+    result = total[0]
+    for step in range(1, ZS):
+        result = result + z_move(total[step].astype(BF16), step).astype(F32)
+    return result
+
+
+def merge(index, own, other, axis):
+    return jnp.where(index == 0, jnp.stack([own, other], axis), jnp.stack([other, own], axis))
+
+
+def take(value, index, axis):
+    return lax.dynamic_index_in_dim(value, index, axis, keepdims=False)
+
+
+def dot(left, right):
+    return jnp.dot(left, right, preferred_element_type=F32)
+
+
+def dot_t(left, right):
+    return lax.dot_general(left, right, (((1,), (1,)), ((), ())), preferred_element_type=F32)
+
+
+def dot_l(left, right):
+    return lax.dot_general(left, right, (((0,), (0,)), ((), ())), preferred_element_type=F32)
+
+
+def turned(value, cosine, sine):
+    return value * cosine + pltpu.roll(value, HDIM // 2, 1) * sine
+
+
+def masked_probs(query, key, row_block, key_block):
+    scores = jnp.where(key_block <= row_block, dot_t(query, key) * HDIM ** (-0.5), -1e30)
+    powers = jnp.exp(scores - jnp.max(scores, axis=1, keepdims=True))
+    return powers / jnp.sum(powers, axis=1, keepdims=True)
+
+
+MESH = pl.DeviceIdType.MESH
+ORDER = (3, 1, 2, 0)
+STEP = 16
+DMA = pltpu.SemaphoreType.DMA
+ANY = pl.BlockSpec(memory_space=pl.ANY)
+VMEM = pl.BlockSpec(memory_space=pltpu.VMEM)
+
+
+def by_rows(rows, body):
+    def step(index, carry):
+        body(pl.ds(pl.multiple_of(index * STEP, STEP), STEP))
+        return carry
+
+    lax.fori_loop(0, rows // STEP, step, 0)
+
+
+class Place:
+    def __init__(self):
+        group, owner = lax.axis_index("group"), lax.axis_index("expert")
+        self.z, self.y = lax.div(group, YS), lax.rem(group, YS)
+        self.x, self.core = lax.div(owner, CS), lax.rem(owner, CS)
+        self.group, self.owner = group, owner
+
+        def device(z, y, x, core):
+            return (z * YS + y, x * CS + core)
+
+        self.x_peer = device(self.z, self.y, 1 - self.x, self.core)
+        self.y_peer = device(self.z, 1 - self.y, self.x, self.core)
+        self.core_peer = device(self.z, self.y, self.x, 1 - self.core)
+        self.z_peers = [device(lax.rem(self.z + step, ZS), self.y, self.x, self.core) for step in range(ZS)]
+
+    def enter(self, with_y):
+        peers = [self.x_peer, self.core_peer] + self.z_peers[1:] + ([self.y_peer] if with_y else [])
+        barrier = pltpu.get_barrier_semaphore()
+        for peer in peers:
+            pl.semaphore_signal(barrier, inc=1, device_id=peer, device_id_type=MESH)
+        pl.semaphore_wait(barrier, len(peers))
+
+
+def remote(src, dst, send, arrive, peer):
+    return pltpu.make_async_remote_copy(
+        src_ref=src, dst_ref=dst, send_sem=send, recv_sem=arrive, device_id=peer, device_id_type=MESH
+    )
+
+
+class Reduce:
+    @staticmethod
+    def scratch(micro, rows, model):
+        return [
+            pltpu.VMEM((micro, ZS, XS, rows, model), BF16),
+            pltpu.VMEM((micro, ZS, XS, rows, model), BF16),
+            pltpu.VMEM((micro, ZS, rows, model), BF16),
+            pltpu.VMEM((micro, 2, ZS - 1, rows, model), BF16),
+            pltpu.VMEM((micro, rows, model), F32),
+            DMA((micro, ZS, XS)),
+            DMA((micro, ZS, XS)),
+            DMA((micro, ZS, XS)),
+            DMA((micro, ZS)),
+            DMA((micro, ZS)),
+            DMA((micro, 2, ZS)),
+            DMA((micro, 2, ZS)),
+        ]
+
+    def __init__(self, place, part, refs):
+        self.place, self.part = place, part
+        self.core_in, self.kept, self.x_in, self.z_in, self.total = [refs.pop(0) for _ in range(5)]
+        self.sems = [refs.pop(0) for _ in range(7)]
+        self.micro, self.rows = part.shape[0], part.shape[4]
+
+    def core_copy(self, m, k, dx):
+        send, arrive = self.sems[:2]
+        return remote(
+            self.part.at[m, k, 1, dx],
+            self.core_in.at[m, k, dx],
+            send.at[m, k, dx],
+            arrive.at[m, k, dx],
+            self.place.core_peer,
+        )
+
+    def kept_copy(self, m, k, dx):
+        return pltpu.make_async_copy(
+            self.part.at[m, k, 0, dx], self.kept.at[m, k, dx], self.sems[2].at[m, k, dx]
+        )
+
+    def x_copy(self, m, k):
+        send, arrive = self.sems[3:5]
+        return remote(
+            self.core_in.at[m, k, 1], self.x_in.at[m, k], send.at[m, k], arrive.at[m, k], self.place.x_peer
+        )
+
+    def z_copy(self, m, down, far):
+        send, arrive = self.sems[5:7]
+        return remote(
+            self.x_in.at[m, ZS - far if down else far],
+            self.z_in.at[m, down, far - 1],
+            send.at[m, down, far - 1],
+            arrive.at[m, down, far - 1],
+            self.place.z_peers[ZS - 1 if down else 1],
+        )
+
+    def begin(self):
+        for m in range(self.micro):
+            for dx in (1, 0):
+                for k in ORDER:
+                    self.core_copy(m, k, dx).start()
+                    self.kept_copy(m, k, dx).start()
+
+    def pass_x(self, m):
+        for k in ORDER:
+            self.core_copy(m, k, 1).wait_recv()
+            self.kept_copy(m, k, 1).wait()
+
+            def add(span, k=k):
+                value = self.core_in[m, k, 1, span, :].astype(F32) + self.kept[m, k, 1, span, :].astype(F32)
+                self.core_in[m, k, 1, span, :] = value.astype(BF16)
+
+            by_rows(self.rows, add)
+            self.x_copy(m, k).start()
+
+    def z_unit(self, m, k):
+        self.x_copy(m, k).wait_recv()
+        self.core_copy(m, k, 0).wait_recv()
+        self.kept_copy(m, k, 0).wait()
+
+        def add(span):
+            value = (
+                self.x_in[m, k, span, :].astype(F32)
+                + self.core_in[m, k, 0, span, :].astype(F32)
+                + self.kept[m, k, 0, span, :].astype(F32)
+            )
+            if k:
+                self.x_in[m, k, span, :] = value.astype(BF16)
+            else:
+                self.total[m, span, :] = value
+
+        by_rows(self.rows, add)
+
+    def beyond(self, down, far):
+        return self.place.z >= far if down else self.place.z + far < ZS
+
+    def chain(self, m, far):
+        for down in (0, 1):
+
+            def send(down=down):
+                if far < ZS - 1:
+                    pl.when(self.beyond(1 - down, 1))(functools.partial(self.join, m, down, far))
+                self.z_copy(m, down, far).start()
+
+            pl.when(self.beyond(down, far))(send)
+
+    def join(self, m, down, far):
+        self.z_copy(m, down, far + 1).wait_recv()
+        place = ZS - far if down else far
+
+        def add(span):
+            value = self.x_in[m, place, span, :].astype(F32) + self.z_in[m, down, far, span, :].astype(F32)
+            self.x_in[m, place, span, :] = value.astype(BF16)
+
+        by_rows(self.rows, add)
+
+    def finish(self, m):
+        for down in (0, 1):
+
+            def last(down=down):
+                self.z_copy(m, down, 1).wait_recv()
+
+                def add(span):
+                    self.total[m, span, :] += self.z_in[m, down, 0, span, :].astype(F32)
+
+                by_rows(self.rows, add)
+
+            pl.when(self.beyond(1 - down, 1))(last)
+
+    def sums(self, m):
+        for turn, k in enumerate(ORDER):
+            self.z_unit(m, k)
+            if m and turn < 2:
+                self.chain(m - 1, 2 - turn)
+        self.chain(m, ZS - 1)
+
+    def end_chain(self):
+        for far in range(ZS - 2, 0, -1):
+            self.chain(self.micro - 1, far)
+
+    def run(self):
+        self.begin()
+        for m in range(self.micro):
+            self.pass_x(m)
+        for m in range(self.micro):
+            self.sums(m)
+        self.end_chain()
+
+    def drain(self):
+        for m in range(self.micro):
+            for k in ORDER:
+                for dx in range(XS):
+                    self.core_copy(m, k, dx).wait_send()
+                self.x_copy(m, k).wait_send()
+            for down in (0, 1):
+                for far in range(1, ZS):
+                    pl.when(self.beyond(down, far))(self.z_copy(m, down, far).wait_send)
+
+
+class Gather:
+    @staticmethod
+    def scratch(micro):
+        return [
+            DMA((micro,)),
+            DMA((micro, ZS)),
+            DMA((micro, ZS)),
+            DMA((micro, ZS)),
+            DMA((micro, ZS, XS)),
+            DMA((micro, ZS, CS, XS)),
+        ]
+
+    def __init__(self, place, own, out, refs):
+        self.place, self.own, self.out = place, own, out
+        self.sems = [refs.pop(0) for _ in range(6)]
+        self.micro = out.shape[0]
+
+    def slot(self, m, k, dc, dx):
+        return self.out.at[m, k, dc, dx]
+
+    def local(self, m):
+        return pltpu.make_async_copy(self.own.at[m], self.slot(m, 0, 0, 0), self.sems[0].at[m])
+
+    def up(self, m, source, k):
+        return remote(
+            source, self.slot(m, k, 0, 0), self.sems[1].at[m, k], self.sems[5].at[m, k, 0, 0], self.place.z_peers[1]
+        )
+
+    def down(self, m, source, k):
+        return remote(
+            source,
+            self.slot(m, k, 0, 0),
+            self.sems[2].at[m, k],
+            self.sems[5].at[m, k, 0, 0],
+            self.place.z_peers[ZS - 1],
+        )
+
+    def over_x(self, m, source, k):
+        return remote(
+            source, self.slot(m, k, 0, 1), self.sems[3].at[m, k], self.sems[5].at[m, k, 0, 1], self.place.x_peer
+        )
+
+    def over_core(self, m, source, k, dx):
+        return remote(
+            source,
+            self.slot(m, k, 1, dx),
+            self.sems[4].at[m, k, dx],
+            self.sems[5].at[m, k, 1, dx],
+            self.place.core_peer,
+        )
+
+    def send_own(self, m):
+        source, z = self.own.at[m], self.place.z
+        pl.when(z < ZS - 1)(lambda: self.up(m, source, ZS - 1).start())
+        pl.when(z > 0)(lambda: self.down(m, source, 1).start())
+        self.over_x(m, source, 0).start()
+        self.over_core(m, source, 0, 0).start()
+        self.local(m).start()
+
+    def pass_on(self, m, k):
+        self.over_x(m, self.slot(m, k, 0, 0), k).start()
+        self.over_core(m, self.slot(m, k, 0, 0), k, 0).start()
+
+    def from_above(self, m, far):
+        self.up(m, self.own.at[m], far).wait_recv()
+        pl.when(self.place.z > 0)(lambda: self.down(m, self.slot(m, far, 0, 0), far + 1).start())
+        self.pass_on(m, far)
+
+    def from_below(self, m, far):
+        self.up(m, self.own.at[m], ZS - far).wait_recv()
+        source = self.slot(m, ZS - far, 0, 0)
+        pl.when(self.place.z < ZS - 1)(lambda: self.up(m, source, ZS - far - 1).start())
+        self.pass_on(m, ZS - far)
+
+    def z_arrival(self, m, far):
+        pl.when(self.place.z + far < ZS)(lambda: self.from_above(m, far))
+        pl.when(self.place.z - far >= 0)(lambda: self.from_below(m, far))
+
+    def x_arrival(self, m, k):
+        self.over_x(m, self.own.at[m], k).wait_recv()
+        self.over_core(m, self.slot(m, k, 0, 1), k, 1).start()
+
+    def z_round(self, far):
+        for m in range(self.micro):
+            self.z_arrival(m, far)
+
+    def x_round(self, far):
+        for m in range(self.micro):
+            if far == 0:
+                self.x_arrival(m, 0)
+            else:
+                pl.when(self.place.z + far < ZS)(lambda: self.x_arrival(m, far))
+                pl.when(self.place.z - far >= 0)(lambda: self.x_arrival(m, ZS - far))
+
+    def run(self):
+        self.z_round(1)
+        self.x_round(0)
+        self.z_round(2)
+        self.x_round(1)
+        self.z_round(3)
+        self.x_round(2)
+        self.x_round(3)
+
+    def drain(self):
+        z = self.place.z
+        for m in range(self.micro):
+            own = self.own.at[m]
+            for k in range(ZS):
+                for dx in range(XS):
+                    self.over_core(m, own, k, dx).wait_recv()
+            self.local(m).wait()
+            pl.when(z < ZS - 1)(lambda: self.up(m, own, ZS - 1).wait_send())
+            pl.when(z > 0)(lambda: self.down(m, own, 1).wait_send())
+            for far in range(1, ZS - 1):
+                pl.when((z + far < ZS) & (z > 0))(lambda: self.down(m, own, far + 1).wait_send())
+                pl.when((z - far >= 0) & (z < ZS - 1))(lambda: self.up(m, own, ZS - far - 1).wait_send())
+            for k in range(ZS):
+                self.over_x(m, own, k).wait_send()
+                for dx in range(XS):
+                    self.over_core(m, own, k, dx).wait_send()
+
+
+class Spread:
+    @staticmethod
+    def scratch(pieces, depth):
+        return [DMA((pieces,)), DMA((ZS, pieces)), DMA((ZS, pieces))] + [
+            DMA((ZS << step,)) for step in range(depth) for _ in range(2)
+        ]
+
+    def __init__(self, place, sources, targets, view, depth, refs):
+        self.place, self.sources, self.targets, self.view, self.depth = place, sources, targets, view, depth
+        self.local_sem, self.z_send, self.z_recv = [refs.pop(0) for _ in range(3)]
+        self.sems = [(refs.pop(0), refs.pop(0)) for _ in range(depth)]
+        self.pieces = self.local_sem.shape[0]
+
+    def z_copy(self, step, piece):
+        place = self.place
+        mine = self.targets(self.view(place.z, place.y, place.x, place.core))
+        return remote(
+            self.sources(lax.rem(place.z + step, ZS))[piece],
+            mine[piece],
+            self.z_send.at[step, piece],
+            self.z_recv.at[step, piece],
+            place.z_peers[step],
+        )
+
+    def local(self, piece):
+        place = self.place
+        mine = self.targets(self.view(place.z, place.y, place.x, place.core))
+        return pltpu.make_async_copy(self.sources(place.z)[piece], mine[piece], self.local_sem.at[piece])
+
+    def hop(self, axis, index):
+        place = self.place
+        z = lax.rem(place.z - (index >> axis) + ZS, ZS)
+        y = place.y if axis < 1 else (place.y + ((index >> (axis - 1)) & 1)) % 2
+        x = place.x if axis < 2 else (place.x + (index & 1)) % 2
+        block = self.view(z, y, x, place.core)
+        peer = (place.y_peer, place.x_peer, place.core_peer)[axis]
+        send, arrive = self.sems[axis]
+        return remote(block, block, send.at[index], arrive.at[index], peer)
+
+    def begin(self):
+        for piece in range(self.pieces):
+            self.local(piece).start()
+        for step in (1, 3, 2):
+            for piece in range(self.pieces):
+                self.z_copy(step, piece).start()
+
+    def forward(self, axis, index):
+        for later in range(axis, self.depth):
+            self.hop(later, index << (later - axis)).start()
+
+    def z_round(self, step):
+        for piece in range(self.pieces):
+            if step:
+                self.z_copy(step, piece).wait_recv()
+            else:
+                self.local(piece).wait()
+        self.forward(0, step)
+
+    def hop_round(self, axis, index):
+        self.hop(axis, index).wait_recv()
+        self.forward(axis + 1, index * 2 + 1)
+
+    def drain(self):
+        for step in range(1, ZS):
+            for piece in range(self.pieces):
+                self.z_copy(step, piece).wait_send()
+        for axis in range(self.depth):
+            for index in range(ZS << axis):
+                self.hop(axis, index).wait_send()
+
+
+class Share:
+    @staticmethod
+    def scratch(pieces):
+        return [DMA((pieces,)), DMA((pieces,)), DMA((pieces,))]
+
+    def __init__(self, place, blocks, refs):
+        local, send, arrive = [refs.pop(0) for _ in range(3)]
+        self.copies = []
+        for index, (source, target) in enumerate(blocks):
+            self.copies.append(pltpu.make_async_copy(source, target, local.at[index]))
+            self.copies.append(remote(source, target, send.at[index], arrive.at[index], place.y_peer))
+
+    def begin(self):
+        for copy in self.copies:
+            copy.start()
+
+    def drain(self):
+        for copy in self.copies:
+            copy.wait()
+
+
+def normed_rows(rows, gain):
+    return rows * lax.rsqrt(jnp.mean(rows * rows, axis=1, keepdims=True) + EPS) * gain
+
+
+def norm_back(grad, rows, upstream, gain):
+    scale = lax.rsqrt(jnp.mean(rows * rows, axis=1, keepdims=True) + EPS)
+    scaled = grad * gain
+    inner = jnp.mean(scaled * rows, axis=1, keepdims=True)
+    return upstream + scale * scaled - rows * (scale * scale * scale) * inner, grad * rows * scale
+
+
+def start_kernel(sizes, tokens, cotangent, gain, table, w_kv, w_query, w_out, w_down, *refs):
+    refs = list(refs)
+    normed_out, cotangent_out, table_out, qkv_weight, out_weight, down_weight = [refs.pop(0) for _ in range(6)]
+    wide, kv_rows, model_rows, out_rows, down_rows = sizes
+    place = Place()
+    normed_own = refs.pop(0)
+    normed = Gather(place, normed_own, normed_out, refs)
+    upstream = Gather(place, cotangent, cotangent_out, refs)
+    tables = Gather(place, table, table_out, refs)
+
+    def lanes(start):
+        return pl.ds(pl.multiple_of(start, HDIM), wide)
+
+    def kv_view(z, y, x, core):
+        row = ((z * YS + y) * (XS * CS) + x * CS + core) * kv_rows
+        return qkv_weight.at[pl.ds(pl.multiple_of(row, kv_rows), kv_rows), pl.ds(wide, 2 * wide)]
+
+    def query_view(z, y, x, core):
+        row = (z * YS + y) * model_rows
+        return qkv_weight.at[pl.ds(pl.multiple_of(row, model_rows), model_rows), pl.ds(0, wide)]
+
+    kv = Spread(
+        place,
+        lambda z: [w_kv.at[:, lanes(z * wide)], w_kv.at[:, lanes((ZS + z) * wide)]],
+        lambda block: [block.at[:, pl.ds(0, wide)], block.at[:, pl.ds(wide, wide)]],
+        kv_view,
+        3,
+        refs,
+    )
+    query = Spread(
+        place, lambda z: [w_query.at[0, :, lanes(z * wide)]], lambda block: [block], query_view, 1, refs
+    )
+
+    def half(target, rows):
+        return target.at[pl.ds(pl.multiple_of(place.y * rows, rows), rows)]
+
+    shared = Share(
+        place,
+        [(w_out.at[0], half(out_weight, out_rows)), (w_down.at[0], half(down_weight, down_rows))],
+        refs,
+    )
+    place.enter(True)
+    kv.begin()
+    tables.send_own(0)
+    for m in range(normed.micro):
+
+        def body(span, m=m):
+            normed_own[m, span, :] = normed_rows(tokens[m, span, :].astype(F32), gain[...]).astype(BF16)
+
+        by_rows(tokens.shape[1], body)
+        normed.send_own(m)
+    query.begin()
+    shared.begin()
+    kv.z_round(0)
+    tables.z_round(1)
+    kv.z_round(1)
+    kv.z_round(3)
+    normed.z_round(1)
+    for m in range(upstream.micro):
+        upstream.send_own(m)
+    kv.z_round(2)
+    for index in (0, 1, 3, 2):
+        kv.hop_round(0, index)
+    normed.x_round(0)
+    tables.z_round(2)
+    normed.z_round(2)
+    for step in (0, 1, 3, 2):
+        query.z_round(step)
+    for index in (0, 2, 6, 4, 1, 3, 7, 5):
+        kv.hop_round(1, index)
+    normed.z_round(3)
+    normed.x_round(1)
+    tables.z_round(3)
+    for far in range(ZS):
+        tables.x_round(far)
+    upstream.z_round(1)
+    normed.x_round(2)
+    upstream.x_round(0)
+    upstream.z_round(2)
+    normed.x_round(3)
+    upstream.x_round(1)
+    upstream.z_round(3)
+    upstream.x_round(2)
+    upstream.x_round(3)
+    for index in range(ZS << 2):
+        kv.hop_round(2, index)
+    for index in range(ZS):
+        query.hop_round(0, index)
+    for part in (tables, normed, kv, query, shared, upstream):
+        part.drain()
+
+
+def first_kernel(sizes, part, tokens, gain, w_gate_up, gate_part, *refs):
+    refs = list(refs)
+    rows_out, weight, middle_out, own = [refs.pop(0) for _ in range(4)]
+    model_rows, hidden_width = sizes
+    place = Place()
+    reduce = Reduce(place, part, refs)
+    gather = Gather(place, own, rows_out, refs)
+
+    def view(z, y, column):
+        row = pl.multiple_of((z * YS + y) * model_rows, model_rows)
+        return weight.at[pl.ds(row, model_rows), pl.ds(column, hidden_width)]
+
+    shared = Share(place, [(gate_part.at[z], view(z, place.y, 0)) for z in range(ZS)], refs)
+    up = Spread(
+        place,
+        lambda z: [w_gate_up.at[0, :, pl.ds(pl.multiple_of((ZS + z) * hidden_width, HDIM), hidden_width)]],
+        lambda block: [block],
+        lambda z, y, x, core: view(z, y, hidden_width),
+        1,
+        refs,
+    )
+    place.enter(True)
+    reduce.begin()
+    up.begin()
+    shared.begin()
+    reduce.pass_x(0)
+    up.z_round(0)
+    reduce.pass_x(1)
+    reduce.sums(0)
+    up.z_round(1)
+    up.z_round(3)
+    reduce.sums(1)
+    up.z_round(2)
+    reduce.end_chain()
+    for m in range(gather.micro):
+        reduce.finish(m)
+
+        def body(span, m=m):
+            middle = tokens[m, span, :].astype(F32) + reduce.total[m, span, :]
+            middle_out[m, span, :] = middle
+            own[m, span, :] = normed_rows(middle, gain[...]).astype(BF16)
+
+        by_rows(reduce.rows, body)
+        gather.send_own(m)
+    gather.run()
+    for index in range(ZS):
+        up.hop_round(0, index)
+    for part in (gather, shared, up, reduce):
+        part.drain()
+
+
+def second_kernel(part, middle, cotangent, gain, gate_grad, up_grad, down_grad, *refs):
+    refs = list(refs)
+    rows_out, grad_out, terms_out, gate_out, up_out, down_out, own = [refs.pop(0) for _ in range(7)]
+    place = Place()
+    reduce = Reduce(place, part, refs)
+    gather = Gather(place, own, rows_out, refs)
+    local, send, arrive, y_send, y_recv = [refs.pop(0) for _ in range(5)]
+    width = gate_grad.shape[2]
+    columns = gate_out.at[:, pl.ds(pl.multiple_of(place.z * width, HDIM), width)]
+    kept = pltpu.make_async_copy(gate_grad.at[place.z], columns, local)
+
+    def give(step):
+        return remote(
+            gate_grad.at[lax.rem(place.z + step, ZS)],
+            columns,
+            send.at[step],
+            arrive.at[step],
+            place.z_peers[step],
+        )
+
+    halves = [
+        remote(up_grad.at[:, 1 - place.y], up_out, y_send.at[0], y_recv.at[0], place.y_peer),
+        remote(down_grad.at[1 - place.y], down_out, y_send.at[1], y_recv.at[1], place.y_peer),
+    ]
+    place.enter(True)
+    kept.start()
+    reduce.begin()
+    for copy in halves:
+        copy.start()
+    for step in (1, 3, 2):
+        give(step).start()
+    for m in range(reduce.micro):
+        reduce.pass_x(m)
+    for m in range(reduce.micro):
+        reduce.sums(m)
+    reduce.end_chain()
+    terms_out[...] = jnp.zeros_like(terms_out)
+    for m in range(gather.micro):
+        reduce.finish(m)
+
+        def body(span, m=m):
+            result, terms = norm_back(
+                reduce.total[m, span, :], middle[m, span, :], cotangent[m, span, :].astype(F32), gain[...]
+            )
+            grad_out[m, span, :] = result
+            own[m, span, :] = result.astype(BF16)
+            terms_out[...] += terms
+
+        by_rows(reduce.rows, body)
+        gather.send_own(m)
+    gather.run()
+    gather.drain()
+    reduce.drain()
+    kept.wait()
+    for copy in halves:
+        copy.wait()
+    for step in (1, 3, 2):
+        give(step).wait()
+
+
+class Halves:
+    def __init__(self, own, other, copies):
+        self.own, self.other, self.copies = own, other, copies
+
+    def begin(self):
+        for copy in self.copies:
+            copy.start()
+
+    def add(self):
+        for copy in self.copies:
+            copy.wait()
+
+        def body(index, carry):
+            value = self.own[index].astype(F32) + self.other[index].astype(F32)
+            self.other[index] = value.astype(BF16)
+            return carry
+
+        lax.fori_loop(0, self.other.shape[0], body, 0)
+
+
+def last_kernel(part, other, tokens, middle, middle_grad, gain, terms_in, query_grad, kv_grad, out_grad, *refs):
+    refs = list(refs)
+    input_out, output, gains_out, query_out, kv_out, out_out = [refs.pop(0) for _ in range(6)]
+    place = Place()
+    first = Reduce(place, part, refs)
+    second = Reduce(place, other, refs)
+    query_own, query_in, kv_own, core_in, x_in, y_in = [refs.pop(0) for _ in range(6)]
+    hop_send, hop_recv, hop_local, z_send, z_recv, z_local = [refs.pop(0) for _ in range(6)]
+    terms, gain_in, gain_send, gain_recv = [refs.pop(0) for _ in range(4)]
+    wide, kv_rows = query_out.shape[1] // ZS, kv_out.shape[0]
+
+    def swap(number, source, target, peer):
+        return remote(source, target, hop_send.at[number], hop_recv.at[number], peer)
+
+    query = Halves(
+        query_own,
+        query_in,
+        [
+            pltpu.make_async_copy(query_grad.at[:, place.y], query_own, hop_local.at[0]),
+            swap(0, query_grad.at[:, 1 - place.y], query_in, place.y_peer),
+        ],
+    )
+    over_core = Halves(
+        kv_own,
+        core_in,
+        [
+            pltpu.make_async_copy(kv_grad.at[:, place.core], kv_own, hop_local.at[1]),
+            swap(1, kv_grad.at[:, 1 - place.core], core_in, place.core_peer),
+        ],
+    )
+    by_x = core_in.reshape(ZS * YS, XS, kv_rows, 2 * wide)
+    over_x = Halves(by_x.at[:, place.x], x_in, [swap(2, by_x.at[:, 1 - place.x], x_in, place.x_peer)])
+    by_y = x_in.reshape(ZS, YS, kv_rows, 2 * wide)
+    over_y = Halves(by_y.at[:, place.y], y_in, [swap(3, by_y.at[:, 1 - place.y], y_in, place.y_peer)])
+    over_out = swap(4, out_grad.at[1 - place.y], out_out, place.y_peer)
+
+    def lanes(start):
+        return pl.ds(pl.multiple_of(start, HDIM), wide)
+
+    def z_parts(step):
+        to = lax.rem(place.z + step, ZS)
+        pairs = [(query_in.at[to], query_out.at[:, lanes(place.z * wide)])]
+        for kind in range(2):
+            pairs.append(
+                (y_in.at[to, :, pl.ds(kind * wide, wide)], kv_out.at[:, lanes((kind * ZS + place.z) * wide)])
+            )
+        return pairs
+
+    def z_copy(step, piece):
+        source, target = z_parts(step)[piece]
+        if step == 0:
+            return pltpu.make_async_copy(source, target, z_local.at[piece])
+        return remote(source, target, z_send.at[step, piece], z_recv.at[step, piece], place.z_peers[step])
+
+    def add_gains(number, peers):
+        copies = [
+            remote(terms, gain_in.at[number + i], gain_send.at[number + i], gain_recv.at[number + i], peer)
+            for i, peer in enumerate(peers)
+        ]
+        for copy in copies:
+            copy.start()
+        for copy in copies:
+            copy.wait()
+        for i in range(len(peers)):
+            terms[...] += gain_in[number + i]
+
+    place.enter(True)
+    first.begin()
+    over_core.begin()
+    query.begin()
+    over_out.start()
+    second.begin()
+    for m in range(first.micro):
+        first.pass_x(m)
+    over_core.add()
+    over_x.begin()
+    first.sums(0)
+    query.add()
+    for step in (1, 3, 2, 0):
+        z_copy(step, 0).start()
+    for m in range(second.micro):
+        second.pass_x(m)
+    first.sums(1)
+    over_x.add()
+    over_y.begin()
+    first.end_chain()
+    second.sums(0)
+    over_y.add()
+    for step in (1, 3, 2, 0):
+        for piece in (1, 2):
+            z_copy(step, piece).start()
+    terms[...] = jnp.zeros_like(terms)
+    for m in range(first.micro):
+        first.finish(m)
+
+        def body(span, m=m):
+            result, found = norm_back(
+                first.total[m, span, :], tokens[m, span, :].astype(F32), middle_grad[m, span, :], gain[...]
+            )
+            input_out[m, span, :] = result.astype(BF16)
+            terms[0:1, :] += jnp.sum(found, axis=0, keepdims=True)
+
+        by_rows(first.rows, body)
+    terms[1:2, :] = jnp.sum(terms_in[...], axis=0, keepdims=True)
+    add_gains(0, [place.core_peer])
+    second.sums(1)
+    add_gains(1, [place.x_peer])
+    second.end_chain()
+    add_gains(2, [place.y_peer])
+    for m in range(second.micro):
+        second.finish(m)
+
+        def finish(span, m=m):
+            output[m, span, :] = (middle[m, span, :] + second.total[m, span, :]).astype(BF16)
+
+        by_rows(second.rows, finish)
+    add_gains(3, place.z_peers[1:])
+    gains_out[...] = terms[...]
+    first.drain()
+    second.drain()
+    over_out.wait()
+    for step in range(ZS):
+        for piece in range(3):
+            z_copy(step, piece).wait()
+
+
+def connect(kernel, operands, spaces, out_shapes, out_spaces, scratch, number, seconds):
+    return pl.pallas_call(
+        kernel,
+        in_specs=spaces,
+        out_specs=out_spaces,
+        out_shape=out_shapes,
+        scratch_shapes=scratch,
+        compiler_params=pltpu.CompilerParams(
+            collective_id=number, has_side_effects=True, vmem_limit_bytes=60 << 20
+        ),
+        cost_estimate=pl.CostEstimate(flops=0, bytes_accessed=int(seconds * 3e12), transcendentals=0),
+    )(*operands)
+
+
+def attend_kernel(qkv_ref, cos_ref, sin_ref, row_ref, key_ref, turned_ref, out_ref):
+    cosine, sine = cos_ref[...], sin_ref[...]
+    width = out_ref.shape[2]
+    for head in range(width // HDIM):
+        parts = []
+        for kind in range(3):
+            span = slice(kind * width + head * HDIM, kind * width + (head + 1) * HDIM)
+            value = qkv_ref[0, :, span]
+            if kind < 2:
+                value = turned(value, cosine, sine)
+            value = value.astype(BF16)
+            turned_ref[0, :, span] = value
+            parts.append(value)
+        query, key, value = parts
+        probs = masked_probs(query, key, row_ref[0], key_ref[0]).astype(BF16)
+        out_ref[0, :, head * HDIM : (head + 1) * HDIM] = dot(probs, value).astype(BF16)
+
+
+def attend_back_kernel(turned_ref, grad_ref, cos_ref, sin_ref, row_ref, key_ref, out_ref):
+    cosine, sine = cos_ref[...], -sin_ref[...]
+    width = grad_ref.shape[2]
+    for head in range(width // HDIM):
+        spans = [slice(kind * width + head * HDIM, kind * width + (head + 1) * HDIM) for kind in range(3)]
+        query, key, value = [turned_ref[0, :, span] for span in spans]
+        grad = grad_ref[0, :, spans[0]]
+        probs = masked_probs(query, key, row_ref[0], key_ref[0])
+        prob_grad = dot_t(grad, value)
+        inner = jnp.sum(probs * prob_grad, axis=1, keepdims=True)
+        raw_grad = (probs * (prob_grad - inner) * HDIM ** (-0.5)).astype(BF16)
+        results = [
+            turned(dot(raw_grad, key), cosine, sine),
+            turned(dot_l(raw_grad, query), cosine, sine),
+            dot_l(probs.astype(BF16), grad),
+        ]
+        for span, result in zip(spans, results):
+            out_ref[0, :, span] = result.astype(BF16)
+
+
+def per_sequence(kernel, operands, tables, out_widths, matmuls):
+    seqs, rows = operands[0].shape[:2]
+    own = [pl.BlockSpec((1,) + value.shape[1:], lambda k: (k, 0, 0)) for value in operands]
+    shared = [pl.BlockSpec(value.shape, lambda k: (0, 0)) for value in tables[:2]]
+    blocks = [pl.BlockSpec((1,) + value.shape[1:], lambda k: (k, 0, 0)) for value in tables[2:]]
+    width = out_widths[-1] if len(out_widths) > 1 else out_widths[0] // 3
+    moved = sum(value.size * value.dtype.itemsize for value in operands) + 2 * seqs * rows * sum(out_widths)
+    return pl.pallas_call(
+        kernel,
+        grid=(seqs,),
+        in_specs=own + shared + blocks,
+        out_specs=[pl.BlockSpec((1, rows, out), lambda k: (k, 0, 0)) for out in out_widths],
+        out_shape=[jax.ShapeDtypeStruct((seqs, rows, out), BF16) for out in out_widths],
+        compiler_params=pltpu.CompilerParams(vmem_limit_bytes=40 << 20),
+        cost_estimate=pl.CostEstimate(
+            flops=2 * matmuls * seqs * rows * rows * width,
+            bytes_accessed=moved,
+            transcendentals=seqs * rows * rows * width // HDIM,
+        ),
+    )(*operands, *tables)
+
+
+def fast_device(
+    tokens,
+    cotangent,
+    gain_attn,
+    gain_mlp,
+    w_kv,
+    w_query,
+    w_out,
+    w_gate_up,
+    w_down,
+    att_routes,
+    att_gates,
+    mlp_routes,
+    mlp_gates,
+    blocks,
+):
+    group, owner = lax.axis_index("group"), lax.axis_index("expert")
+    y = group % YS
+    x, core = owner // CS, owner % CS
+    micro, local, model = tokens.shape
+    wide = w_query.shape[2] // ZS
+    hidden_width = w_gate_up.shape[2] // (2 * ZS)
+    kv_rows = w_kv.shape[0]
+    model_rows = w_query.shape[1]
+
+    def own_rows(table):
+        return lax.dynamic_slice_in_dim(table, owner * local, local, 0).astype(F32)
+
+    lines = []
+    for m in range(micro):
+        lines += [own_rows(att_routes[m]).T, att_gates[m].T, own_rows(mlp_routes[m]).T, mlp_gates[m].T]
+        lines += [own_rows(blocks[m, 0][:, None]).T]
+    table = jnp.concatenate(lines, axis=0)
+    table = jnp.pad(table, ((0, -table.shape[0] % 8), (0, -local % HDIM)))[None]
+
+    positions = (
+        (x ^ jnp.arange(XS)[None, :, None]) * CS + (core ^ jnp.arange(CS)[:, None, None])
+    ) * local + jnp.arange(local)[None, None, :]
+    cosine, sine = angles(positions.reshape(-1))
+    cosine = jnp.concatenate([cosine, cosine], axis=1)
+    sine = jnp.concatenate([-sine, sine], axis=1)
+
+    shape = (micro, local, model)
+    everyone = (micro, ZS, CS, XS, local, model)
+    seqs = micro * ZS
+    first_gain, second_gain = gain_attn[None], gain_mlp[None]
+    tall = jax.ShapeDtypeStruct(shape, F32)
+    short = jax.ShapeDtypeStruct(shape, BF16)
+    gathered = jax.ShapeDtypeStruct(everyone, BF16)
+    terms = jax.ShapeDtypeStruct((STEP, model), F32)
+    own_buffer = pltpu.VMEM(shape, BF16)
+    normed, cotangents, table, qkv_weight, out_weight, down_weight = connect(
+        functools.partial(
+            start_kernel, (wide, kv_rows, model_rows, w_out.shape[1], w_down.shape[1])
+        ),
+        [tokens, cotangent, first_gain, table, w_kv, w_query, w_out, w_down],
+        [VMEM, VMEM, VMEM, VMEM, ANY, ANY, ANY, ANY],
+        [
+            gathered,
+            gathered,
+            jax.ShapeDtypeStruct((1, ZS, CS, XS) + table.shape[1:], F32),
+            jax.ShapeDtypeStruct((model, 3 * wide), BF16),
+            jax.ShapeDtypeStruct((wide, model), BF16),
+            jax.ShapeDtypeStruct((hidden_width, model), BF16),
+        ],
+        [ANY] * 6,
+        [own_buffer]
+        + Gather.scratch(micro)
+        + Gather.scratch(micro)
+        + Gather.scratch(1)
+        + Spread.scratch(2, 3)
+        + Spread.scratch(1, 1)
+        + Share.scratch(2),
+        1,
+        140e-6,
+    )
+    cotangents = cotangents.reshape(seqs, SEQ, model)
+    normed = normed.reshape(-1, model)
+    gate_part = w_gate_up[0, :, : ZS * hidden_width]
+    gate_part, normed = lax.optimization_barrier((gate_part, normed))
+    gate_part = z_exchange(gate_part.reshape(model_rows, ZS, hidden_width).transpose(1, 0, 2))
+
+    part = table[0, ..., : 9 * micro, :local].reshape(ZS, CS, XS, micro, 9, local)
+    part = part.transpose(3, 0, 1, 2, 5, 4).reshape(seqs, SEQ, 9)
+    att_weight = jnp.sum(jnp.where(part[..., 0:2] == owner, part[..., 2:4], 0.0), axis=-1).reshape(-1, 1)
+    hit = jnp.any(part[..., 4:6] == owner, axis=-1)
+    mlp_weight = jnp.sum(jnp.where(part[..., 4:6] == owner, part[..., 6:8], 0.0), axis=-1)
+    seq_blocks = part[..., 8].astype(jnp.int32)
+    tables = [cosine, sine, seq_blocks[:, :, None], seq_blocks[:, None, :]]
+    before_mask = jnp.arange(SEQ)[:, None] < jnp.arange(SEQ)[None, :]
+    before = dot(hit.astype(BF16), before_mask.astype(BF16)).astype(jnp.int32)
+    slots = jnp.arange(XS * CS * CAP)
+    chosen = hit[:, None, :] & (before[:, None, :] == slots[None, :, None])
+    row_gate = jnp.sum(jnp.where(chosen, mlp_weight[:, None, :], 0.0), axis=2)
+    select = chosen.astype(BF16)
+
+    def to_rows(gathered):
+        return jnp.einsum("gru,gud->grd", select, gathered, preferred_element_type=F32)
+
+    def to_tokens(rows):
+        rows = rows.reshape(seqs, -1, model)
+        rows = jnp.einsum("gru,grd->gud", select, rows, preferred_element_type=F32).astype(BF16)
+        return rows.reshape(everyone)
+
+    qkv = dot(normed, qkv_weight).reshape(seqs, SEQ, 3 * wide)
+    turned_qkv, attended = per_sequence(attend_kernel, [qkv], tables, [3 * wide, wide], 2)
+    attended = attended.reshape(-1, wide)
+    result = (dot(attended, out_weight) * att_weight).astype(BF16).reshape(everyone)
+    normed_two, gate_up, middle = connect(
+        functools.partial(first_kernel, (model_rows, hidden_width)),
+        [result, tokens, second_gain, w_gate_up, gate_part],
+        [ANY, VMEM, VMEM, ANY, ANY],
+        [gathered, jax.ShapeDtypeStruct((model, 2 * hidden_width), BF16), tall],
+        [ANY, ANY, VMEM],
+        [own_buffer]
+        + Reduce.scratch(*shape)
+        + Gather.scratch(micro)
+        + Share.scratch(ZS)
+        + Spread.scratch(1, 1),
+        2,
+        150e-6,
+    )
+    rows_two = to_rows(normed_two.reshape(seqs, SEQ, model)).astype(BF16).reshape(-1, model)
+    down_grad = (to_rows(cotangents) * row_gate[:, :, None]).astype(BF16).reshape(-1, model)
+    both = dot(rows_two, gate_up)
+    gate, up = both[:, :hidden_width], both[:, hidden_width:]
+    sigma = 1.0 / (1.0 + jnp.exp(-gate))
+    hidden = (gate * sigma * up).astype(BF16)
+    hidden_grad = dot_t(down_grad, down_weight)
+    slope = sigma * (1.0 + gate * (1.0 - sigma))
+    both_grad = jnp.concatenate(
+        [hidden_grad * up * slope, hidden_grad * gate * sigma], axis=1
+    ).astype(BF16)
+    row_grad = to_tokens(dot_t(both_grad, gate_up).astype(BF16))
+    result_two = to_tokens((dot(hidden, down_weight) * row_gate.reshape(-1, 1)).astype(BF16))
+
+    def halved(value, other):
+        return (take(value, y, 1).astype(F32) + other.astype(F32)).astype(BF16)
+
+    def by_y(value):
+        return value.astype(BF16).reshape(ZS, YS, model_rows, hidden_width)
+
+    gate_grad = by_y(dot_l(rows_two, both_grad[:, :hidden_width]))
+    gate_grad = halved(gate_grad, y_move(take(gate_grad, 1 - y, 1)))
+    up_grad = by_y(dot_l(rows_two, both_grad[:, hidden_width:]))
+    grad_down = dot_l(hidden, down_grad).reshape(YS, -1, model)
+    middle_grads, middle_grad, gain_second, gate_grad, up_other, down_other = connect(
+        second_kernel,
+        [row_grad, middle, cotangent, second_gain, gate_grad, up_grad, grad_down.astype(BF16)],
+        [ANY, VMEM, VMEM, VMEM, ANY, ANY, ANY],
+        [
+            gathered,
+            tall,
+            terms,
+            jax.ShapeDtypeStruct((model_rows, ZS * hidden_width), BF16),
+            jax.ShapeDtypeStruct((ZS, model_rows, hidden_width), BF16),
+            jax.ShapeDtypeStruct(w_down.shape[1:], BF16),
+        ],
+        [ANY, VMEM, VMEM, ANY, ANY, ANY],
+        [own_buffer]
+        + Reduce.scratch(*shape)
+        + Gather.scratch(micro)
+        + [DMA, DMA((ZS,)), DMA((ZS,)), DMA((2,)), DMA((2,))],
+        3,
+        130e-6,
+    )
+    up_grad = z_exchange(halved(up_grad, up_other))
+    grad_down = (take(grad_down, y, 0) + down_other.astype(F32))[None]
+    result_grad = (middle_grads.reshape(-1, model).astype(F32) * att_weight).astype(BF16)
+    attended_grad = dot_t(result_grad, out_weight).astype(BF16).reshape(seqs, SEQ, wide)
+    qkv_grad = per_sequence(attend_back_kernel, [turned_qkv, attended_grad], tables, [3 * wide], 5)[0]
+    qkv_grad = qkv_grad.reshape(-1, 3 * wide)
+    normed_part = dot_t(qkv_grad, qkv_weight).astype(BF16).reshape(everyone)
+    grad_out = dot_l(attended, result_grad).reshape(YS, -1, model)
+    query_grad = dot_l(normed, qkv_grad[:, :wide]).astype(BF16).reshape(ZS, YS, model_rows, wide)
+    kv_grad = dot_l(normed, qkv_grad[:, wide:]).astype(BF16).reshape(-1, CS, kv_rows, 2 * wide)
+    normed_part, up_grad = lax.optimization_barrier((normed_part, up_grad))
+    input_grad, output, gains, query_grad, kv_grad, out_other = connect(
+        last_kernel,
+        [
+            normed_part,
+            result_two,
+            tokens,
+            middle,
+            middle_grad,
+            first_gain,
+            gain_second,
+            query_grad,
+            kv_grad,
+            grad_out.astype(BF16),
+        ],
+        [ANY, ANY, VMEM, VMEM, VMEM, VMEM, VMEM, ANY, ANY, ANY],
+        [
+            short,
+            short,
+            jax.ShapeDtypeStruct((8, model), F32),
+            jax.ShapeDtypeStruct((model_rows, ZS * wide), BF16),
+            jax.ShapeDtypeStruct((kv_rows, 2 * ZS * wide), BF16),
+            jax.ShapeDtypeStruct(w_out.shape[1:], BF16),
+        ],
+        [VMEM, VMEM, VMEM, ANY, ANY, ANY],
+        Reduce.scratch(*shape)
+        + Reduce.scratch(*shape)
+        + [pltpu.VMEM((ZS, model_rows, wide), BF16) for _ in range(2)]
+        + [pltpu.VMEM((ZS * YS * XS, kv_rows, 2 * wide), BF16) for _ in range(2)]
+        + [pltpu.VMEM((ZS * YS, kv_rows, 2 * wide), BF16), pltpu.VMEM((ZS, kv_rows, 2 * wide), BF16)]
+        + [DMA((5,)), DMA((5,)), DMA((2,)), DMA((ZS, 3)), DMA((ZS, 3)), DMA((3,))]
+        + [pltpu.VMEM((8, model), F32), pltpu.VMEM((6, 8, model), F32), DMA((6,)), DMA((6,))],
+        4,
+        130e-6,
+    )
+    devices = ZS * YS * XS * CS
+    gains = take(gains[:2].reshape(2, devices, model // devices), group * XS * CS + owner, 1)
+    gate_up_grad = [gate_grad.astype(F32)] + [up_grad[z].astype(F32) for z in range(ZS)]
+    return (
+        output,
+        input_grad,
+        gains[0],
+        gains[1],
+        kv_grad.astype(F32),
+        query_grad.astype(F32)[None],
+        (take(grad_out, y, 0) + out_other.astype(F32))[None],
+        jnp.concatenate(gate_up_grad, axis=1)[None],
+        grad_down,
+    )
+
+
 def solution(mesh):
     in_specs = (
         P(None, ("group", "expert"), None),
@@ -399,6 +1571,7 @@
         P("expert", "group", None),
         P("expert", "group", None),
     )
+    body = fast_device if fits(mesh) else on_device
     return jax.shard_map(
-        on_device, mesh=mesh, in_specs=in_specs, out_specs=out_specs, check_vma=False
-    )
+        body, mesh=mesh, in_specs=in_specs, out_specs=out_specs, check_vma=False
+    )

time: 3870 us -> 1120 us (0.29)
  waiting for transfers between devices: 3090 us -> 21.8 us
  Pallas kernels: 0 us -> 728 us
  matrix products: 472 us -> 269 us
  starting transfers between devices: 62.5 us -> 9.9 us
  local copies, waits for them, and re-layouts: 85.3 us -> 40.2 us
  blocking collectives: 43 us -> 0 us
  other arithmetic: 83.9 us -> 43 us
    all_gather x7 -> x0, waiting for transfers between devices: 1490 us -> none  [the longest x1 780 us: on_device(): lax.all_gather(w_gate_up, 'group', axis=1, tiled=True)]
    reduce_scatter x6 -> x0, waiting for transfers between devices: 778 us -> none  [the longest x3 430 us: expert_reduce(): lax.psum_scatter(term(jnp.int32(0), lax.axis_size('group') * (left.shape[...]
    pallas_call x0 -> x6, Pallas kernels: none -> 728 us  [the longest x4 672 us: connect(): pl.pallas_call(kernel, in_specs=spaces, out_specs=out_spaces, out_shape=o...]
    unnamed x15 -> x0, waiting for transfers between devices: 728 us -> none
    dot_general x53 -> x19, matrix products: 472 us -> 269 us  [the longest x6 84.9 us: dot_l(): lax.dot_general(left, right, (((0,), (0,)), ((), ())), preferred_element_...]
    all_to_all x16 -> x2, waiting for transfers between devices: 96 us -> 21.8 us  [z_exchange(): lax.all_to_all(value, 'group', split_axis=0, concat_axis=0, tiled=True, a...]
    all_to_all x16 -> x2, starting transfers between devices: 62 us -> 8.65 us  [z_exchange(): lax.all_to_all(value, 'group', split_axis=0, concat_axis=0, tiled=True, a...]
    unnamed x1 -> x0, blocking collectives: 43 us -> none
  transfers between devices with their start and end apart: 30 -> 3, of which waited for: 21 -> 1; matrix products, arithmetic and copies ran while one was open for 14% -> 15% of each run, Pallas kernels for 0% -> 2%
where the time goes in v2:
time: 1120 us; the launch traced here: 1110 us
  Pallas kernels  728 us (65%)
  matrix products  269 us (24%)
  other arithmetic  43 us (4%)
  local copies, waits for them, and re-layouts  40.2 us (4%)
  waiting for transfers between devices  21.8 us (2%)
    pallas_call x4, Pallas kernels, connect(): pl.pallas_call(kernel, in_specs=spaces, out_specs=out_spaces, out_shape=o...  672 us
    dot_general x6, matrix products, dot_l(): lax.dot_general(left, right, (((0,), (0,)), ((), ())), preferred_element_...  84.9 us
    dot_general x4, matrix products, dot_t(): lax.dot_general(left, right, (((1,), (1,)), ((), ())), preferred_element_...  75.7 us
    dot_general x5, matrix products, dot(): return jnp.dot(left, right, preferred_element_type=F32)  74.2 us
    pallas_call x2, Pallas kernels, per_sequence(): pl.pallas_call(kernel, grid=(seqs,), in_specs=own + shared + blocks, out_...  56.5 us
  transfers between devices with their start and end apart: 3, of which 1 were waited for; matrix products, arithmetic and copies ran while one was open for 15% of the time, Pallas kernels for 2%

profile of v2, /device:TPU:0, one launch (start us, length us, event | category | flops | bytes accessed | tf_op | source)
XLA Modules:
  0.0 1113.7 jit_solution(9141577818331370236)
XLA Ops:
  0.7 1.8 slice-done.6
  2.5 2.7 copy.37
  6.3 186.3 %shard_map.205 = (bf16[2,4,2,2,80,2048]{5,4,3,2,1,0:T(8,128)(2,1)}, bf16[2,4,2,2,80,2048]{5,4,3,2,1,0:T(8,128)(2,1)}, f32[1,4,2,2,24,128]{5,4,3,2,1,0:T(8,128)},...) custom-call(bf16[2,80,2048]{2,1,0:T(8,128)(2,1)} %tokens.5, ...), custom_call_target="tpu_custom_call" | custom-call | bytes 420000000 | tf_op jit(solution)/shard_map/pallas_call | solution.py:1246
  192.6 2.7 copy.32
  195.3 4.8 all-to-all-start
  200.4 22.3 %fusion.56 = f32[2560,1536]{1,0:T(8,128)} fusion(bf16[2560,2048]{1,0:T(8,128)(2,1)} %bitcast.198, bf16[2048,1536]{1,0:T(8,128)(2,1)} %get-tuple-element.38), kind=kOutput, calls=%fused_computation.107 | convolution fusion | flops 16106127360 | bytes 32505856 | tf_op jit(solution)/shard_map/dot_general | solution.py:447
  226.8 26.2 %shard_map.206 = (bf16[8,320,1536]{2,1,0:T(8,128)(2,1)S(1)}, bf16[8,320,512]{2,1,0:T(8,128)(2,1)S(1)}) custom-call(f32[8,320,1536]{2,1,0:T(8,128)} %bitcast.169, f32[320,128]{1,0:T(8,128)S(1)} %pad_maximum_fusion.cos_ref, f32[320,128]{1,0:T(8,128)S(1)} %pad_maximum_fusion.1.sin_ref, s32[8,320,1]{2,1,0:T(8,128)S(1)} %copy.31.row_ref, ...), custom_call_target="tpu_custom_call" | custom-call | flops 1677721600 | bytes 26214400 | tf_op jit(solution)/shard_map/pallas_call | solution.py:1304
  253.0 3.1 copy-done
  256.1 1.5 copy-done.2
  257.6 4.4 copy.36
  262.0 10.5 multiply_convert_fusion.3
  272.5 8.5 multiply_convert_fusion.1
  281.0 154.6 %shard_map.207 = (bf16[2,4,2,2,80,2048]{5,4,3,2,1,0:T(8,128)(2,1)}, bf16[2048,2816]{1,0:T(8,128)(2,1)}, f32[2,80,2048]{2,1,0:T(8,128)}) custom-call(bf16[2,4,2,2,80,2048]{5,4,3,2,1,0:T(8,128)(2,1)} %bitcast.181, bf16[2,80,2048]{2,1,0:T(8,128)(2,1)} %tokens.5, f32[1,2048]{1,0:T(1,128)} %bitcast.194, bf16[1,256,11264]{2,1,0:T(8,128)(2,1)} %w_gate_up.1, ...), custom_call_target="tpu_custom_call" | custom-call | bytes 450000000 | tf_op jit(solution)/shard_map/pallas_call | solution.py:1246
  435.6 7.5 convolution_convert_fusion.5
  443.2 27.6 %fusion.57 = f32[1600,2816]{1,0:T(8,128)} fusion(bf16[1600,2048]{1,0:T(8,128)(2,1)S(1)} %bitcast.170, bf16[2048,2816]{1,0:T(8,128)(2,1)} %get-tuple-element.47), kind=kOutput, calls=%fused_computation.108 | convolution fusion | flops 18454937600 | bytes 36110336 | tf_op jit(solution)/shard_map/dot_general | solution.py:447
  470.8 24.3 %multiply_convert_fusion.6 = (bf16[1600,1408]{1,0:T(8,128)(2,1)}, bf16[1600,1408]{1,0:T(8,128)(2,1)}, bf16[1600,1408]{1,0:T(8,128)(2,1)}) fusion(f32[1600,2816]{1,0:T(8,128)} %fusion.57, bf16[1600,2048]{1,0:T(8,128)(2,1)} %bitcast.204, bf16[1408,2048]{1,0:T(8,128)(2,1)} %get-tuple-element.42), kind=kOutput, calls=%fused_computation.13 | convolution fusion | flops 9263513600 | bytes 43859968 | tf_op jit(solution)/shard_map/dot_general | solution.py:451
  495.1 16.7 %convolution_convert_fusion.2 = bf16[2048,1408]{1,0:T(8,128)(2,1)} fusion(bf16[1600,2048]{1,0:T(8,128)(2,1)} %bitcast.171, bf16[1600,1408]{1,0:T(8,128)(2,1)} %get-tuple-element.65), kind=kOutput, calls=%fused_computation.17 | convolution fusion | flops 9230352384 | bytes 16826368 | tf_op jit(solution)/shard_map/dot_general | solution.py:455
  511.7 25.7 %fusion.5 = bf16[1600,2048]{1,0:T(8,128)(2,1)} fusion(bf16[2048,2816]{1,0:T(8,128)(2,1)} %get-tuple-element.47, bf16[1600,1408]{1,0:T(8,128)(2,1)} %get-tuple-element.66, bf16[1600,1408]{1,0:T(8,128)(2,1)} %get-tuple-element.65), kind=kOutput, calls=%fused_computation.15 | convolution fusion | flops 18476236800 | bytes 27099136 | tf_op jit(solution)/shard_map/dot_general | solution.py:451
  537.5 3.6 dynamic-slice_bitcast_fusion
  541.1 1.3 collective-permute-start
  542.3 7.3 copy.34
  549.6 15.6 %multiply_convert_fusion.2 = bf16[1600,2048]{1,0:T(8,128)(2,1)} fusion(bf16[1600,1408]{1,0:T(8,128)(2,1)} %get-tuple-element.67, bf16[1408,2048]{1,0:T(8,128)(2,1)} %get-tuple-element.42, f32[1600]{0:T(1024)S(1)} %copy-done.27), kind=kOutput, calls=%fused_computation.4 | convolution fusion | flops 9234022400 | bytes 16832768 | tf_op jit(solution)/shard_map/dot_general | solution.py:447
  565.2 16.4 %fusion.54 = (bf16[2,704,2048]{2,1,0:T(8,128)(2,1)}, f32[2,704,2048]{2,1,0:T(8,128)}) fusion(bf16[2,704,1600]{2,1,0:T(8,128)(2,1)S(1)} %bitcast.187, bf16[1600,2048,1]{1,0,2:T(8,128)(2,1)} %bitcast.205), kind=kOutput, calls=%fused_computation.105 | convolution fusion | flops 9230352384 | bytes 28360704 | tf_op jit(solution)/shard_map/dot_general | solution.py:455
  581.7 5.9 convolution_convert_fusion.4
  587.6 10.0 convolution_convert_fusion.3
  597.6 15.0 %convolution_convert_fusion.1 = bf16[2048,1408]{1,0:T(8,128)(2,1)} fusion(bf16[1600,2048]{1,0:T(8,128)(2,1)S(1)} %bitcast.174, bf16[1600,1408]{1,0:T(8,128)(2,1)} %get-tuple-element.66), kind=kOutput, calls=%fused_computation.16 | convolution fusion | flops 9230352384 | bytes 16826368 | tf_op jit(solution)/shard_map/dot_general | solution.py:455
  612.6 4.1 fusion.9.gate_grad
  616.6 152.2 %shard_map.208 = (bf16[2,4,2,2,80,2048]{5,4,3,2,1,0:T(8,128)(2,1)}, f32[2,80,2048]{2,1,0:T(8,128)}, f32[16,2048]{1,0:T(8,128)}, bf16[256,5632]{1,0:T(8,128)(2,1)...) custom-call(bf16[2,4,2,2,80,2048]{5,4,3,2,1,0:T(8,128)(2,1)} %bitcast.163, ...), custom_call_target="tpu_custom_call" | custom-call | bytes 390000000 | tf_op jit(solution)/shard_map/pallas_call | solution.py:1246
  768.9 5.8 fusion
  774.7 5.9 convolution_convert_fusion.6
  780.7 30.3 %shard_map.209 = bf16[8,320,1536]{2,1,0:T(8,128)(2,1)S(1)} custom-call(bf16[8,320,1536]{2,1,0:T(8,128)(2,1)} %copy-done, bf16[8,320,512]{2,1,0:T(8,128)(2,1)S(1)} %bitcast.159, f32[320,128]{1,0:T(8,128)S(1)} %copy-done.5, f32[320,128]{1,0:T(8,128)S(1)} %copy-done.7, s32[8,320,1]{2,1,0:T(8,128)S(1)} %copy.31.row_ref, s32[8,1,320]{2,1,0:T(1,128)S(1)} %get-tuple-element.68.key_ref), custom_call_target="tpu_custom_call" | custom-call | flops 4194304000 | bytes 18350080 | tf_op jit(solution)/shard_map/pallas_call | solution.py:1304
  811.0 14.1 %convolution_convert_fusion.7 = bf16[2048,512]{1,0:T(8,128)(2,1)} fusion(bf16[2560,2048]{1,0:T(8,128)(2,1)} %bitcast.199, bf16[2560,1536]{1,0:T(8,128)(2,1)S(1)} %bitcast.154), kind=kOutput, calls=%fused_computation.32 | convolution fusion | flops 5369757696 | bytes 15204352 | tf_op jit(solution)/shard_map/dot_general | solution.py:455
  825.1 15.3 %fusion.13 = bf16[2048,1024]{1,0:T(8,128)(2,1)} fusion(bf16[2560,2048]{1,0:T(8,128)(2,1)} %bitcast.200, bf16[2560,1536]{1,0:T(8,128)(2,1)S(1)} %bitcast.155), kind=kOutput, calls=%fused_computation.31 | convolution fusion | flops 10739515392 | bytes 19922944 | tf_op jit(solution)/shard_map/dot_general | solution.py:455
  840.5 2.2 fusion.8
  842.7 3.9 all-to-all-start.1
  846.7 7.1 multiply_convert_fusion
  853.8 7.4 fusion.55
  861.2 1.8 constant_dynamic-update-slice_fusion
  863.0 1.1 copy-done.13
  864.1 6.8 fusion.10
  870.9 19.8 %convolution_convert_fusion = bf16[2560,2048]{1,0:T(8,128)(2,1)} fusion(bf16[2560,1536]{1,0:T(8,128)(2,1)S(1)} %bitcast.158, bf16[2048,1536]{1,0:T(8,128)(2,1)S(1)} %bitcast.203), kind=kOutput, calls=%fused_computation.6 | convolution fusion | flops 16111370240 | bytes 24641536 | tf_op jit(solution)/shard_map/dot_general | solution.py:451
  890.7 21.8 %all-to-all-done.1 = bf16[4,256,1408]{2,1,0:T(8,128)(2,1)S(1)} async-done(((bf16[4,256,1408]{2,1,0:T(8,128)(2,1)}), bf16[4,256,1408]{2,1,0:T(8,128)(2,1)S(1)}, u32[]{:S(2)}, u32[]{:S(2)}) %all-to-all-start.1) | async-done | bytes 2883616 | tf_op jit(solution)/shard_map/all_to_all | solution.py:415
  912.5 178.9 %shard_map.210 = (bf16[2,80,2048]{2,1,0:T(8,128)(2,1)}, bf16[2,80,2048]{2,1,0:T(8,128)(2,1)}, f32[8,2048]{1,0:T(8,128)}, bf16[256,2048]{1,0:T(8,128)(2,1)}, bf16...) custom-call(bf16[2,4,2,2,80,2048]{5,4,3,2,1,0:T(8,128)(2,1)} %bitcast.180, bf16[2,4,2,2,80,2048]{5,4,3,2,1,0:T(8,128)(2,1)} %bitcast.162, ...), custom_call_target="tpu_custom_call" | custom-call | bytes 390000000 | tf_op jit(solution)/shard_map/pallas_call | solution.py:1246
  1092.3 2.1 convert_element_type.256
  1094.4 2.8 bitcast_convert_fusion.1
  1099.1 1.0 bitcast_dynamic-update-slice_fusion.1
  1101.1 8.6 bitcast_convert_fusion
  1109.6 1.6 fusion.22
  (137 shorter events, 11.4 us)
Async XLA Ops:
  0.7 4.5 copy-start.28
  0.7 4.5 copy-start.29
  0.7 4.5 copy-start.30
  0.7 4.5 copy-start.31
  0.7 4.5 copy-start.32
  5.2 187.4 %copy-start.9 = (bf16[1,256,5632]{1,2,0:T(8,128)(2,1)S(1)}, bf16[1,256,5632]{1,2,0:T(8,128)(2,1)}, u32[]{:S(2)}) copy-start(bf16[1,256,5632]{1,2,0:T(8,128)(2,1)} %copy.37) | copy-start | bytes 8650756
  192.6 7.5 copy-start.23
  195.3 85.7 %all-to-all-start = ((bf16[4,256,1408]{2,1,0:T(8,128)(2,1)}), bf16[4,256,1408]{2,1,0:T(8,128)(2,1)}, u32[]{:S(2)}, u32[]{:S(2)}) async-start(bf16[4,256,1408]{2,1,0:T(8,128)(2,1)} %bitcast.32), calls=%async_computation | async-start | bytes 5767168 | tf_op jit(solution)/shard_map/all_to_all | solution.py:415
  222.9 49.6 %copy-start.25 = (f32[2560]{0:T(1024)}, f32[2560]{0:T(1024)S(1)}, u32[]{:S(2)}) copy-start(f32[2560]{0:T(1024)S(1)} %mul.114) | copy-start | bytes 30724
  224.4 211.2 %copy-start.21 = (pred[8,320]{1,0:T(8,128)(4,1)}, pred[8,320]{1,0:T(8,128)(4,1)S(1)}, u32[]{:S(2)}) copy-start(pred[8,320]{1,0:T(8,128)(4,1)S(1)} %fusion.50) | copy-start | bytes 7684
  224.5 211.1 %copy-start.15 = (s32[8,320]{1,0:T(8,128)}, s32[8,320]{1,0:T(8,128)S(1)}, u32[]{:S(2)}) copy-start(s32[8,320]{1,0:T(8,128)S(1)} %convolution_convert_fusion.8) | copy-start | bytes 30724
  226.7 26.3 %copy-start.4 = (f32[320,128]{1,0:T(8,128)}, f32[320,128]{1,0:T(8,128)S(1)}, u32[]{:S(2)}) copy-start(f32[320,128]{1,0:T(8,128)S(1)} %pad_maximum_fusion.cos_ref) | copy-start | bytes 491524
  226.8 26.2 %copy-start.6 = (f32[320,128]{1,0:T(8,128)}, f32[320,128]{1,0:T(8,128)S(1)}, u32[]{:S(2)}) copy-start(f32[320,128]{1,0:T(8,128)S(1)} %pad_maximum_fusion.1.sin_ref) | copy-start | bytes 491524
  253.0 3.1 copy-start
  262.0 10.5 copy-start.3
  262.0 10.5 copy-start.33
  443.1 27.6 %copy-start.8 = (bf16[8,200,2048]{2,1,0:T(8,128)(2,1)}, bf16[8,200,2048]{2,1,0:T(8,128)(2,1)S(1)}, u32[]{:S(2)}) copy-start(bf16[8,200,2048]{2,1,0:T(8,128)(2,1)S(1)} %convolution_convert_fusion.5) | copy-start | bytes 19660804
  537.5 12.1 %copy-start.27 = (f32[1600]{0:T(1024)S(1)}, f32[1600]{0:T(1024)}, u32[]{:S(2)}) copy-start(f32[1600]{0:T(1024)} %mul.126) | copy-start | bytes 19204
  541.1 71.5 %collective-permute-start = (bf16[4,256,1408]{2,1,0:T(8,128)(2,1)}, bf16[4,256,1408]{2,1,0:T(8,128)(2,1)}, u32[]{:S(2)}, u32[]{:S(2)}) collective-permute-start(bf16[4,256,1408]{2,1,0:T(8,128)(2,1)} %dynamic-slice_bitcast_fusion), channel_id=1, source_target_pairs={{0,4},{4,0},{8,12},{12,8},{16,20},{20,16},{24,28},{28,24},{1,5},{5... | collective-permute-start | bytes 8650760 | tf_op jit(solution)/shard_map/ppermute | solution.py:394
  549.6 15.6 %copy-start.10 = (bf16[1408,1600]{1,0:T(8,128)(2,1)S(1)}, bf16[1408,1600]{1,0:T(8,128)(2,1)}, u32[]{:S(2)}) copy-start(bf16[1408,1600]{1,0:T(8,128)(2,1)} %copy.34) | copy-start | bytes 13516804
  549.6 32.0 %slice-start.2 = ((s8[6553600]{0:T(1024)(128)(4,1)}), s8[4194304]{0:T(1024)(128)(4,1)S(1)}, s32[]{:S(2)}) async-start(s8[6553600]{0:T(1024)(128)(4,1)} %bitcast.165), calls=%async_computation.4 | async-start | bytes 8388608
  565.2 16.4 %slice-start.3 = ((s8[6553600]{0:T(1024)(128)(4,1)}), s8[2359296]{0:T(1024)(128)(4,1)S(1)}, s32[]{:S(2)}) async-start(s8[6553600]{0:T(1024)(128)(4,1)} %bitcast.165), calls=%async_computation.5 | async-start | bytes 4718592
  565.2 16.4 %copy-start.16 = (s32[8,320]{1,0:T(8,128)S(1)}, s32[8,320]{1,0:T(8,128)}, u32[]{:S(2)}) copy-start(s32[8,320]{1,0:T(8,128)} %copy-done.15) | copy-start | bytes 30724
  565.2 16.4 %copy-start.22 = (pred[8,320]{1,0:T(8,128)(4,1)S(1)}, pred[8,320]{1,0:T(8,128)(4,1)}, u32[]{:S(2)}) copy-start(pred[8,320]{1,0:T(8,128)(4,1)} %copy-done.21) | copy-start | bytes 7684
  581.7 15.9 %slice-start.4 = ((s8[6553600]{0:T(1024)(128)(4,1)}), s8[2359296]{0:T(1024)(128)(4,1)S(1)}, s32[]{:S(2)}) async-start(s8[6553600]{0:T(1024)(128)(4,1)} %bitcast.172), calls=%async_computation.6 | async-start | bytes 4718592
  587.6 10.0 slice-start.5
  587.6 25.0 %slice-start.9 = ((s8[5767168]{0:T(1024)(128)(4,1)}), s8[1572864]{0:T(1024)(128)(4,1)S(1)}, s32[]{:S(2)}) async-start(s8[5767168]{0:T(1024)(128)(4,1)} %bitcast.184), calls=%async_computation.11 | async-start | bytes 3145728
  597.6 15.0 %slice-start.10 = ((s8[5767168]{0:T(1024)(128)(4,1)}), s8[4194304]{0:T(1024)(128)(4,1)S(1)}, s32[]{:S(2)}) async-start(s8[5767168]{0:T(1024)(128)(4,1)} %bitcast.184), calls=%async_computation.12 | async-start | bytes 8388608
  616.6 152.2 %copy-start.26 = (f32[2560]{0:T(1024)S(1)}, f32[2560]{0:T(1024)}, u32[]{:S(2)}) copy-start(f32[2560]{0:T(1024)} %copy-done.25) | copy-start | bytes 30724
  768.9 5.8 copy-start.34
  774.7 6.0 copy-start.5
  774.7 6.0 copy-start.7
  811.0 14.1 %copy-start.1 = (bf16[8,320,1536]{2,1,0:T(8,128)(2,1)}, bf16[8,320,1536]{2,1,0:T(8,128)(2,1)S(1)}, u32[]{:S(2)}) copy-start(bf16[8,320,1536]{2,1,0:T(8,128)(2,1)S(1)} %shard_map.209) | copy-start | bytes 23592964
  811.0 29.5 %slice-start.7 = ((s8[5767168]{0:T(1024)(128)(4,1)}), s8[4194304]{0:T(1024)(128)(4,1)S(1)}, s32[]{:S(2)}) async-start(s8[5767168]{0:T(1024)(128)(4,1)} %bitcast.176), calls=%async_computation.9 | async-start | bytes 8388608
  825.1 15.3 %slice-start.8 = ((s8[5767168]{0:T(1024)(128)(4,1)}), s8[1572864]{0:T(1024)(128)(4,1)S(1)}, s32[]{:S(2)}) async-start(s8[5767168]{0:T(1024)(128)(4,1)} %bitcast.176), calls=%async_computation.10 | async-start | bytes 3145728
  825.1 15.3 %copy-start.12 = (bf16[4,256,1408]{2,1,0:T(8,128)(2,1)S(1)}, bf16[4,256,1408]{2,1,0:T(8,128)(2,1)}, u32[]{:S(2)}) copy-start(bf16[4,256,1408]{2,1,0:T(8,128)(2,1)} %get-tuple-element.50) | copy-start | bytes 8650756
  840.5 6.1 copy-start.24
  842.7 69.7 %all-to-all-start.1 = ((bf16[4,256,1408]{2,1,0:T(8,128)(2,1)}), bf16[4,256,1408]{2,1,0:T(8,128)(2,1)S(1)}, u32[]{:S(2)}, u32[]{:S(2)}) async-start(bf16[4,256,1408]{2,1,0:T(8,128)(2,1)} %fusion.8), calls=%async_computation.1 | async-start | bytes 5767168 | tf_op jit(solution)/shard_map/all_to_all | solution.py:415
  846.6 7.1 copy-start.14
  846.7 24.2 %slice-start.11 = ((s8[6291456]{0:T(1024)(128)(4,1)}), s8[4194304]{0:T(1024)(128)(4,1)S(1)}, s32[]{:S(2)}) async-start(s8[6291456]{0:T(1024)(128)(4,1)} %bitcast.202), calls=%async_computation.13 | async-start | bytes 8388608
  853.7 7.5 copy-start.11
  853.8 17.1 %slice-start.12 = ((s8[6291456]{0:T(1024)(128)(4,1)}), s8[2097152]{0:T(1024)(128)(4,1)S(1)}, s32[]{:S(2)}) async-start(s8[6291456]{0:T(1024)(128)(4,1)} %bitcast.202), calls=%async_computation.14 | async-start | bytes 4194304
  861.2 9.6 slice-start
  864.1 6.8 slice-start.1
  1101.1 8.6 copy-start.17
  1101.1 8.6 copy-start.18
  1101.1 10.7 copy-start.20
  1109.6 2.9 copy-start.19
  (3 other events, 6.2 us)

commit v3 on v2

--- a/solution.py
+++ b/solution.py
@@ -750,12 +750,16 @@
         self.over_x(m, self.own.at[m], k).wait_recv()
         self.over_core(m, self.slot(m, k, 0, 1), k, 1).start()
 
-    def z_round(self, far):
-        for m in range(self.micro):
+    def piece_arrival(self, m, k):
+        for dx in range(XS):
+            self.over_core(m, self.own.at[m], k, dx).wait_recv()
+
+    def z_round(self, far, chosen=None):
+        for m in range(self.micro) if chosen is None else [chosen]:
             self.z_arrival(m, far)
 
-    def x_round(self, far):
-        for m in range(self.micro):
+    def x_round(self, far, chosen=None):
+        for m in range(self.micro) if chosen is None else [chosen]:
             if far == 0:
                 self.x_arrival(m, 0)
             else:
@@ -771,14 +775,14 @@
         self.x_round(2)
         self.x_round(3)
 
-    def drain(self):
+    def drain(self, waited=False):
         z = self.place.z
         for m in range(self.micro):
             own = self.own.at[m]
-            for k in range(ZS):
-                for dx in range(XS):
-                    self.over_core(m, own, k, dx).wait_recv()
-            self.local(m).wait()
+            if not waited:
+                for k in range(ZS):
+                    self.piece_arrival(m, k)
+                self.local(m).wait()
             pl.when(z < ZS - 1)(lambda: self.up(m, own, ZS - 1).wait_send())
             pl.when(z > 0)(lambda: self.down(m, own, 1).wait_send())
             for far in range(1, ZS - 1):
@@ -790,6 +794,164 @@
                     self.over_core(m, own, k, dx).wait_send()
 
 
+class PieceReduce(Reduce):
+    @staticmethod
+    def scratch(micro, rows, model):
+        return [
+            pltpu.VMEM((micro, ZS, CS * XS * rows, model), BF16),
+            pltpu.VMEM((micro, ZS, XS, rows, model), BF16),
+            pltpu.VMEM((micro, ZS, rows, model), BF16),
+            pltpu.VMEM((micro, 2, ZS - 1, rows, model), BF16),
+            pltpu.VMEM((micro, rows, model), F32),
+            DMA((micro, ZS, XS)),
+            DMA((micro, ZS, XS)),
+            DMA((micro, ZS)),
+            DMA((micro, ZS)),
+            DMA((micro, 2, ZS)),
+            DMA((micro, 2, ZS)),
+        ]
+
+    def __init__(self, place, refs):
+        self.place = place
+        self.part, self.core_in, self.x_in, self.z_in, self.total = [refs.pop(0) for _ in range(5)]
+        core_send, core_recv, x_send, x_recv, z_send, z_recv = [refs.pop(0) for _ in range(6)]
+        self.sems = [core_send, core_recv, None, x_send, x_recv, z_send, z_recv]
+        self.micro, self.rows = self.total.shape[0], self.total.shape[1]
+
+    def unit(self, m, k, dc, dx):
+        return self.part.at[m, k, pl.ds((dc * XS + dx) * self.rows, self.rows)]
+
+    def core_copy(self, m, k, dx):
+        send, arrive = self.sems[:2]
+        return remote(
+            self.unit(m, k, 1, dx),
+            self.core_in.at[m, k, dx],
+            send.at[m, k, dx],
+            arrive.at[m, k, dx],
+            self.place.core_peer,
+        )
+
+    def begin_piece(self, m, k):
+        for dx in (1, 0):
+            self.core_copy(m, k, dx).start()
+
+    def x_piece(self, m, k):
+        self.core_copy(m, k, 1).wait_recv()
+        kept = self.unit(m, k, 0, 1)
+
+        def add(span):
+            value = self.core_in[m, k, 1, span, :].astype(F32) + kept[span, :].astype(F32)
+            self.core_in[m, k, 1, span, :] = value.astype(BF16)
+
+        by_rows(self.rows, add)
+        self.x_copy(m, k).start()
+
+    def z_piece(self, m, k):
+        self.x_copy(m, k).wait_recv()
+        self.core_copy(m, k, 0).wait_recv()
+        kept = self.unit(m, k, 0, 0)
+
+        def sum_of(span):
+            return (
+                self.x_in[m, k, span, :].astype(F32)
+                + self.core_in[m, k, 0, span, :].astype(F32)
+                + kept[span, :].astype(F32)
+            )
+
+        def away(span):
+            self.x_in[m, k, span, :] = sum_of(span).astype(BF16)
+
+        def here(span):
+            self.total[m, span, :] = sum_of(span)
+
+        pl.when(k != 0)(lambda: by_rows(self.rows, away))
+        pl.when(k == 0)(lambda: by_rows(self.rows, here))
+
+    def drain(self):
+        for m in range(self.micro):
+            for k in range(ZS):
+                for dx in range(XS):
+                    self.core_copy(m, k, dx).wait_send()
+                self.x_copy(m, k).wait_send()
+            for down in (0, 1):
+                for far in range(1, ZS):
+                    pl.when(self.beyond(down, far))(self.z_copy(m, down, far).wait_send)
+
+
+def piece_of(place, index):
+    turn = lax.rem(index, ZS)
+    inner = turn + lax.div(turn, 2) * (5 - 2 * turn)
+    last = lax.rem(ZS - turn, ZS)
+    z = place.z
+    return lax.div(index, ZS), jnp.where(z == 0, turn, jnp.where(z == ZS - 1, last, inner))
+
+
+def run_pieces(place, reduce, piece, between):
+    pieces = reduce.micro * ZS
+
+    def step(index, carry):
+        @pl.when(index < pieces)
+        def _():
+            m, k = piece_of(place, index)
+            piece(index, m, k)
+            reduce.begin_piece(m, k)
+
+        between(index)
+
+        @pl.when((index >= 1) & (index < pieces + 1))
+        def _():
+            reduce.x_piece(*piece_of(place, index - 1))
+
+        @pl.when(index >= 3)
+        def _():
+            reduce.z_piece(*piece_of(place, index - 3))
+
+        for m in range(reduce.micro - 1):
+            for far in range(1, ZS):
+                pl.when(index == (m + 1) * ZS + 2 + ZS - far)(functools.partial(reduce.chain, m, far))
+        return carry
+
+    lax.fori_loop(0, pieces + 3, step, 0)
+    for far in range(ZS - 1, 0, -1):
+        reduce.chain(reduce.micro - 1, far)
+
+
+def begin_gathers(gathers):
+    for m in range(gathers[0].micro):
+        for gather in gathers:
+            gather.send_own(m)
+        if m == 0:
+            for gather in gathers:
+                gather.z_round(1, 0)
+            for gather in gathers:
+                gather.x_round(0, 0)
+
+
+def gather_steps(gathers, index):
+    for m in range(gathers[0].micro):
+        for far in range(0 if m else 1, ZS):
+
+            @pl.when(index == (max(0, m * (ZS - 2) - 1) + far if m else far - 1))
+            def _(m=m, far=far):
+                for gather in gathers:
+                    if far + 1 < ZS:
+                        gather.z_round(far + 1, m)
+                for gather in gathers:
+                    gather.x_round(far, m)
+
+
+def wait_local(gather, m):
+    gather.local(m).wait()
+
+
+def by_lanes(count, width, body):
+    def step(index, carry):
+        body(pl.ds(pl.multiple_of(index * width, width), width))
+        return carry
+
+    lax.fori_loop(0, count, step, 0)
+
+
 class Spread:
     @staticmethod
     def scratch(pieces, depth):
@@ -840,6 +1002,18 @@
         for later in range(axis, self.depth):
             self.hop(later, index << (later - axis)).start()
 
+    def begin_slowly(self):
+        for piece in range(self.pieces):
+            self.local(piece).start()
+            self.z_copy(1, piece).start()
+
+    def slow_round(self, turn):
+        steps = (0, 1, 3, 2)
+        self.z_round(steps[turn])
+        if 0 < turn < ZS - 1:
+            for piece in range(self.pieces):
+                self.z_copy(steps[turn + 1], piece).start()
+
     def z_round(self, step):
         for piece in range(self.pieces):
             if step:
@@ -893,14 +1067,37 @@
     return upstream + scale * scaled - rows * (scale * scale * scale) * inner, grad * rows * scale
 
 
-def start_kernel(sizes, tokens, cotangent, gain, table, w_kv, w_query, w_out, w_down, *refs):
+def y_half(place, target, rows):
+    return target.at[pl.ds(pl.multiple_of(place.y * rows, rows), rows)]
+
+
+def gate_up_spread(place, source, kind, target, rows, refs):
+    width = target.shape[1]
+
+    def columns(z):
+        return source.at[0, :, pl.ds(pl.multiple_of((kind * ZS + z) * width, HDIM), width)]
+
+    def view(z, y, x, core):
+        return target.at[pl.ds(pl.multiple_of((z * YS + y) * rows, rows), rows)]
+
+    return Spread(place, lambda z: [columns(z)], lambda block: [block], view, 1, refs)
+
+
+def by_heads(width, body):
+    def step(head, carry):
+        body(lambda kind: pl.ds(pl.multiple_of(kind * width + head * HDIM, HDIM), HDIM))
+        return carry
+
+    lax.fori_loop(0, width // HDIM, step, 0)
+
+
+def start_kernel(sizes, tokens, gain, table, w_kv, w_query, w_out, w_gate, *refs):
     refs = list(refs)
-    normed_out, cotangent_out, table_out, qkv_weight, out_weight, down_weight = [refs.pop(0) for _ in range(6)]
-    wide, kv_rows, model_rows, out_rows, down_rows = sizes
+    normed_out, table_out, qkv_weight, out_weight, gate_weight = [refs.pop(0) for _ in range(5)]
+    wide, kv_rows, model_rows, out_rows = sizes
     place = Place()
     normed_own = refs.pop(0)
     normed = Gather(place, normed_own, normed_out, refs)
-    upstream = Gather(place, cotangent, cotangent_out, refs)
     tables = Gather(place, table, table_out, refs)
 
     def lanes(start):
@@ -926,14 +1123,8 @@
         place, lambda z: [w_query.at[0, :, lanes(z * wide)]], lambda block: [block], query_view, 1, refs
     )
 
-    def half(target, rows):
-        return target.at[pl.ds(pl.multiple_of(place.y * rows, rows), rows)]
-
-    shared = Share(
-        place,
-        [(w_out.at[0], half(out_weight, out_rows)), (w_down.at[0], half(down_weight, down_rows))],
-        refs,
-    )
+    shared = Share(place, [(w_out.at[0], y_half(place, out_weight, out_rows))], refs)
+    gate = gate_up_spread(place, w_gate, 0, gate_weight, model_rows, refs)
     place.enter(True)
     kv.begin()
     tables.send_own(0)
@@ -945,155 +1136,371 @@
         by_rows(tokens.shape[1], body)
         normed.send_own(m)
     query.begin()
-    shared.begin()
     kv.z_round(0)
     tables.z_round(1)
     kv.z_round(1)
     kv.z_round(3)
     normed.z_round(1)
-    for m in range(upstream.micro):
-        upstream.send_own(m)
     kv.z_round(2)
+    normed.x_round(0)
     for index in (0, 1, 3, 2):
         kv.hop_round(0, index)
-    normed.x_round(0)
     tables.z_round(2)
-    normed.z_round(2)
     for step in (0, 1, 3, 2):
         query.z_round(step)
+    normed.z_round(2)
+    gate.begin_slowly()
+    normed.x_round(1)
+    gate.slow_round(0)
+    normed.z_round(3)
     for index in (0, 2, 6, 4, 1, 3, 7, 5):
         kv.hop_round(1, index)
-    normed.z_round(3)
-    normed.x_round(1)
     tables.z_round(3)
+    gate.slow_round(1)
     for far in range(ZS):
         tables.x_round(far)
-    upstream.z_round(1)
     normed.x_round(2)
-    upstream.x_round(0)
-    upstream.z_round(2)
     normed.x_round(3)
-    upstream.x_round(1)
-    upstream.z_round(3)
-    upstream.x_round(2)
-    upstream.x_round(3)
+    gate.slow_round(2)
     for index in range(ZS << 2):
         kv.hop_round(2, index)
     for index in range(ZS):
         query.hop_round(0, index)
-    for part in (tables, normed, kv, query, shared, upstream):
+    shared.begin()
+    gate.slow_round(3)
+    for index in range(ZS):
+        gate.hop_round(0, index)
+    for part in (tables, normed, kv, query, shared, gate):
         part.drain()
 
 
-def first_kernel(sizes, part, tokens, gain, w_gate_up, gate_part, *refs):
+def attend_kernel(
+    sizes, normed, weight, out_weight, row_gate, cosine, sine, row_blocks, key_blocks, tokens, gain, w_up, w_down, *refs
+):
     refs = list(refs)
-    rows_out, weight, middle_out, own = [refs.pop(0) for _ in range(4)]
-    model_rows, hidden_width = sizes
+    normed_out, middle_out, turned_out, attended_out, up_weight, down_weight = [refs.pop(0) for _ in range(6)]
+    model_rows, down_rows = sizes
     place = Place()
-    reduce = Reduce(place, part, refs)
-    gather = Gather(place, own, rows_out, refs)
-
-    def view(z, y, column):
-        row = pl.multiple_of((z * YS + y) * model_rows, model_rows)
-        return weight.at[pl.ds(row, model_rows), pl.ds(column, hidden_width)]
-
-    shared = Share(place, [(gate_part.at[z], view(z, place.y, 0)) for z in range(ZS)], refs)
-    up = Spread(
-        place,
-        lambda z: [w_gate_up.at[0, :, pl.ds(pl.multiple_of((ZS + z) * hidden_width, HDIM), hidden_width)]],
-        lambda block: [block],
-        lambda z, y, x, core: view(z, y, hidden_width),
-        1,
-        refs,
-    )
+    reduce = PieceReduce(place, refs)
+    up = gate_up_spread(place, w_up, 1, up_weight, model_rows, refs)
+    shared = Share(place, [(w_down.at[0], y_half(place, down_weight, down_rows))], refs)
+    arrived, qkv, attended, load, store = [refs.pop(0) for _ in range(5)]
+    wide = out_weight.shape[0]
+    model = out_weight.shape[1]
+    tile = model // 2
+    pieces = reduce.micro * ZS
+
+    def load_of(index):
+        m, k = piece_of(place, index)
+        return pltpu.make_async_copy(normed.at[m * ZS + k], arrived, load)
+
+    def stores(sequence):
+        return [
+            pltpu.make_async_copy(qkv, turned_out.at[sequence], store.at[0]),
+            pltpu.make_async_copy(attended, attended_out.at[sequence], store.at[1]),
+        ]
+
+    def piece(index, m, k):
+        sequence = m * ZS + k
+
+        @pl.when(index > 0)
+        def _():
+            for copy in stores(0):
+                copy.wait()
+
+        load_of(index).wait()
+        for kind in range(3):
+            value = dot(arrived[...], weight[:, kind * wide : (kind + 1) * wide])
+            for head in range(wide // HDIM):
+                part = value[:, head * HDIM : (head + 1) * HDIM]
+                if kind < 2:
+                    part = turned(part, cosine[...], sine[...])
+                start = kind * wide + head * HDIM
+                qkv[:, start : start + HDIM] = part.astype(BF16)
+
+        @pl.when(index + 1 < pieces)
+        def _():
+            load_of(index + 1).start()
+
+        def head(span_of):
+            query, key, value = [qkv[:, span_of(kind)] for kind in range(3)]
+            probs = masked_probs(query, key, row_blocks[sequence], key_blocks[sequence]).astype(BF16)
+            attended[:, span_of(0)] = dot(probs, value).astype(BF16)
+
+        by_heads(wide, head)
+        for start in range(0, model, tile):
+            value = dot(attended[...], out_weight[:, start : start + tile]) * row_gate[sequence]
+            reduce.part[m, k, :, start : start + tile] = value.astype(BF16)
+        for copy in stores(sequence):
+            copy.start()
+
+    def between(index):
+        for turn, at in enumerate((1, 4, 7)):
+            pl.when(index == at)(functools.partial(up.slow_round, turn))
+
     place.enter(True)
-    reduce.begin()
-    up.begin()
+    load_of(0).start()
+    up.begin_slowly()
     shared.begin()
-    reduce.pass_x(0)
-    up.z_round(0)
-    reduce.pass_x(1)
-    reduce.sums(0)
-    up.z_round(1)
-    up.z_round(3)
-    reduce.sums(1)
-    up.z_round(2)
-    reduce.end_chain()
-    for m in range(gather.micro):
+    run_pieces(place, reduce, piece, between)
+    up.slow_round(3)
+    for m in range(reduce.micro):
         reduce.finish(m)
 
         def body(span, m=m):
             middle = tokens[m, span, :].astype(F32) + reduce.total[m, span, :]
             middle_out[m, span, :] = middle
-            own[m, span, :] = normed_rows(middle, gain[...]).astype(BF16)
+            normed_out[m, span, :] = normed_rows(middle, gain[...]).astype(BF16)
 
         by_rows(reduce.rows, body)
-        gather.send_own(m)
-    gather.run()
+    for copy in stores(0):
+        copy.wait()
     for index in range(ZS):
         up.hop_round(0, index)
-    for part in (gather, shared, up, reduce):
+    for part in (shared, up, reduce):
         part.drain()
 
 
-def second_kernel(part, middle, cotangent, gain, gate_grad, up_grad, down_grad, *refs):
+def attend_back_kernel(
+    rows, weight, out_weight, row_gate, cosine, sine, row_blocks, key_blocks, turned_qkv, tokens, middle_grad, gain, gate_grads, up_grads, *refs
+):
     refs = list(refs)
-    rows_out, grad_out, terms_out, gate_out, up_out, down_out, own = [refs.pop(0) for _ in range(7)]
+    input_out, terms_out, row_grad_out, qkv_grad_out, weight_grad_out, other_out, everyone = [
+        refs.pop(0) for _ in range(7)
+    ]
     place = Place()
-    reduce = Reduce(place, part, refs)
-    gather = Gather(place, own, rows_out, refs)
-    local, send, arrive, y_send, y_recv = [refs.pop(0) for _ in range(5)]
-    width = gate_grad.shape[2]
-    columns = gate_out.at[:, pl.ds(pl.multiple_of(place.z * width, HDIM), width)]
-    kept = pltpu.make_async_copy(gate_grad.at[place.z], columns, local)
-
-    def give(step):
+    gather = Gather(place, rows, everyone, refs)
+    reduce = PieceReduce(place, refs)
+    arrived, kept, row_grad, qkv_grad, load, store = [refs.pop(0) for _ in range(6)]
+    mine, theirs, mine_sem, y_send, y_recv, z_send, z_recv, z_local = [refs.pop(0) for _ in range(8)]
+    wide, model = out_weight.shape
+    tile = model // 2
+    width = mine.shape[2]
+
+    def stores(sequence):
+        return [
+            pltpu.make_async_copy(row_grad, row_grad_out.at[sequence], store.at[0]),
+            pltpu.make_async_copy(qkv_grad, qkv_grad_out.at[sequence], store.at[1]),
+        ]
+
+    def piece(index, m, k):
+        sequence = m * ZS + k
+        gather.piece_arrival(m, k)
+        pl.when(k == 0)(lambda: gather.local(m).wait())
+        loads = [
+            pltpu.make_async_copy(everyone.at[m, k, dc, dx], arrived.at[dc, dx], load.at[dc, dx])
+            for dc in range(CS)
+            for dx in range(XS)
+        ]
+        loads.append(pltpu.make_async_copy(turned_qkv.at[sequence], kept, load.at[CS, 0]))
+        for copy in loads:
+            copy.start()
+
+        @pl.when(index > 0)
+        def _():
+            for copy in stores(0):
+                copy.wait()
+
+        for copy in loads:
+            copy.wait()
+        length = kept.shape[0]
+        for start in range(0, model, tile):
+            value = arrived[:, :, :, start : start + tile].astype(F32).reshape(length, tile) * row_gate[sequence]
+            row_grad[:, start : start + tile] = value.astype(BF16)
+        qkv_grad[:, :wide] = dot_t(row_grad[...], out_weight[...]).astype(BF16)
+
+        def head(span_of):
+            query, key, value = [kept[:, span_of(kind)] for kind in range(3)]
+            grad = qkv_grad[:, span_of(0)]
+            probs = masked_probs(query, key, row_blocks[sequence], key_blocks[sequence])
+            prob_grad = dot_t(grad, value)
+            inner = jnp.sum(probs * prob_grad, axis=1, keepdims=True)
+            raw_grad = (probs * (prob_grad - inner) * HDIM ** (-0.5)).astype(BF16)
+            qkv_grad[:, span_of(0)] = turned(dot(raw_grad, key), cosine[...], -sine[...]).astype(BF16)
+            qkv_grad[:, span_of(1)] = turned(dot_l(raw_grad, query), cosine[...], -sine[...]).astype(BF16)
+            qkv_grad[:, span_of(2)] = dot_l(probs.astype(BF16), grad).astype(BF16)
+
+        by_heads(wide, head)
+        for start in range(0, model, tile):
+            value = dot_t(qkv_grad[...], weight[start : start + tile, :])
+            reduce.part[m, k, :, start : start + tile] = value.astype(BF16)
+        for copy in stores(sequence):
+            copy.start()
+
+    steps = (1, 3, 2, 0)
+
+    def z_of(turn):
+        return lax.rem(place.z + steps[turn], ZS)
+
+    def own_copy(turn):
+        return pltpu.make_async_copy(gate_grads.at[z_of(turn), place.y], mine.at[turn], mine_sem.at[turn])
+
+    def y_copy(part):
+        turn = part % ZS
+        grads, target = (up_grads, other_out.at[z_of(turn)]) if part >= ZS else (gate_grads, theirs.at[turn])
         return remote(
-            gate_grad.at[lax.rem(place.z + step, ZS)],
-            columns,
-            send.at[step],
-            arrive.at[step],
-            place.z_peers[step],
-        )
-
-    halves = [
-        remote(up_grad.at[:, 1 - place.y], up_out, y_send.at[0], y_recv.at[0], place.y_peer),
-        remote(down_grad.at[1 - place.y], down_out, y_send.at[1], y_recv.at[1], place.y_peer),
-    ]
+            grads.at[z_of(turn), 1 - place.y], target, y_send.at[part], y_recv.at[part], place.y_peer
+        )
+
+    columns = weight_grad_out.at[:, pl.ds(pl.multiple_of(place.z * width, HDIM), width)]
+
+    def z_copy(turn):
+        if steps[turn] == 0:
+            return pltpu.make_async_copy(theirs.at[turn], columns, z_local)
+        return remote(
+            theirs.at[turn], columns, z_send.at[steps[turn]], z_recv.at[steps[turn]], place.z_peers[steps[turn]]
+        )
+
+    def pass_grads(part):
+        y_copy(part).wait()
+        if part + 2 < 2 * ZS:
+            y_copy(part + 2).start()
+        if part >= ZS:
+            return
+        own_copy(part).wait()
+
+        def add(span):
+            value = mine[part, span, :].astype(F32) + theirs[part, span, :].astype(F32)
+            theirs[part, span, :] = value.astype(BF16)
+
+        by_rows(mine.shape[1], add)
+        z_copy(part).start()
+
+    def between(index):
+        gather_steps([gather], index)
+        for part, at in enumerate((2, 3, 5, 6, 8, 9)):
+            pl.when(index == at)(functools.partial(pass_grads, part))
+
     place.enter(True)
-    kept.start()
-    reduce.begin()
-    for copy in halves:
-        copy.start()
-    for step in (1, 3, 2):
-        give(step).start()
-    for m in range(reduce.micro):
-        reduce.pass_x(m)
-    for m in range(reduce.micro):
-        reduce.sums(m)
-    reduce.end_chain()
+    for turn in range(ZS):
+        own_copy(turn).start()
+    for part in range(2):
+        y_copy(part).start()
+    begin_gathers([gather])
+    run_pieces(place, reduce, piece, between)
+    for part in range(6, 2 * ZS):
+        pass_grads(part)
     terms_out[...] = jnp.zeros_like(terms_out)
     for m in range(gather.micro):
         reduce.finish(m)
 
         def body(span, m=m):
-            result, terms = norm_back(
+            result, found = norm_back(
+                reduce.total[m, span, :], tokens[m, span, :].astype(F32), middle_grad[m, span, :], gain[...]
+            )
+            input_out[m, span, :] = result.astype(BF16)
+            terms_out[...] += found
+
+        by_rows(reduce.rows, body)
+    for copy in stores(0):
+        copy.wait()
+    gather.drain(True)
+    reduce.drain()
+    for turn in range(ZS):
+        z_copy(turn).wait()
+
+
+def mlp_kernel(normed, gate_weight, up_weight, down, select, select_back, gates, middle, cotangent, gain, *refs):
+    refs = list(refs)
+    own_out, grad_out, terms_out, rows_out, up_grad_out, hidden_out, down_grad_out, result_out = [
+        refs.pop(0) for _ in range(8)
+    ]
+    everyone, upstreams = [refs.pop(0) for _ in range(2)]
+    place = Place()
+    gathers = [Gather(place, normed, everyone, refs), Gather(place, cotangent, upstreams, refs)]
+    reduce = PieceReduce(place, refs)
+    arrived, upstream, rows, down_grad, hidden, both_grad, result = [refs.pop(0) for _ in range(7)]
+    load, store = [refs.pop(0) for _ in range(2)]
+    width = down.shape[0]
+    model = middle.shape[2]
+    tile = model // 2
+
+    def stores(index):
+        pairs = (
+            (rows, rows_out),
+            (down_grad, down_grad_out),
+            (hidden, hidden_out),
+            (both_grad, up_grad_out),
+            (result, result_out),
+        )
+        return [
+            pltpu.make_async_copy(here, there.at[index], store.at[i]) for i, (here, there) in enumerate(pairs)
+        ]
+
+    def piece(index, m, k):
+        for gather in gathers:
+            gather.piece_arrival(m, k)
+            pl.when(k == 0)(functools.partial(wait_local, gather, m))
+        sequence = m * ZS + k
+        loads = [
+            pltpu.make_async_copy(source.at[m, k, dc, dx], target.at[dc, dx], load.at[i, dc, dx])
+            for i, (source, target) in enumerate(((everyone, arrived), (upstreams, upstream)))
+            for dc in range(CS)
+            for dx in range(XS)
+        ]
+        for copy in loads:
+            copy.start()
+
+        @pl.when(index > 0)
+        def _():
+            for copy in stores(0):
+                copy.wait()
+
+        for copy in loads:
+            copy.wait()
+        chosen, back, gate_of_row = select[sequence], select_back[sequence], gates[sequence]
+        length = select.shape[2]
+
+        def to_rows(span):
+            rows[:, span] = dot(chosen, arrived[:, :, :, span].reshape(length, tile)).astype(BF16)
+            down_grad[:, span] = (dot(chosen, upstream[:, :, :, span].reshape(length, tile)) * gate_of_row).astype(BF16)
+
+        by_lanes(model // tile, tile, to_rows)
+
+        half = width // (2 * HDIM) * HDIM
+        for start, stop in ((0, half), (half, width)):
+            gate = dot(rows[...], gate_weight[:, start:stop])
+            up = dot(rows[...], up_weight[:, start:stop])
+            hidden_grad = dot_t(down_grad[...], down[start:stop, :])
+            sigma = 0.5 * jnp.tanh(0.5 * gate) + 0.5
+            silu = gate * sigma
+            hidden[:, start:stop] = (silu * up).astype(BF16)
+            slope = sigma + silu * (1.0 - sigma)
+            both_grad[:, start:stop] = (hidden_grad * up * slope).astype(BF16)
+            both_grad[:, width + start : width + stop] = (hidden_grad * silu).astype(BF16)
+
+        def to_tokens(span):
+            row_grad = dot_t(both_grad[:, :width], gate_weight[span, :])
+            row_grad = (row_grad + dot_t(both_grad[:, width:], up_weight[span, :])).astype(BF16)
+            reduce.part[m, k, :, span] = dot(back, row_grad).astype(BF16)
+            value = (dot(hidden[...], down[:, span]) * gate_of_row).astype(BF16)
+            result[:, span] = dot(back, value).astype(BF16)
+
+        by_lanes(model // tile, tile, to_tokens)
+        for copy in stores(sequence):
+            copy.start()
+
+    place.enter(False)
+    begin_gathers(gathers)
+    run_pieces(place, reduce, piece, functools.partial(gather_steps, gathers))
+    terms_out[...] = jnp.zeros_like(terms_out)
+    for m in range(reduce.micro):
+        reduce.finish(m)
+
+        def body(span, m=m):
+            found, terms = norm_back(
                 reduce.total[m, span, :], middle[m, span, :], cotangent[m, span, :].astype(F32), gain[...]
             )
-            grad_out[m, span, :] = result
-            own[m, span, :] = result.astype(BF16)
+            grad_out[m, span, :] = found
+            own_out[m, span, :] = found.astype(BF16)
             terms_out[...] += terms
 
         by_rows(reduce.rows, body)
-        gather.send_own(m)
-    gather.run()
-    gather.drain()
+    for copy in stores(0):
+        copy.wait()
+    for gather in gathers:
+        gather.drain(True)
     reduce.drain()
-    kept.wait()
-    for copy in halves:
-        copy.wait()
-    for step in (1, 3, 2):
-        give(step).wait()
 
 
 class Halves:
@@ -1116,12 +1523,11 @@
         lax.fori_loop(0, self.other.shape[0], body, 0)
 
 
-def last_kernel(part, other, tokens, middle, middle_grad, gain, terms_in, query_grad, kv_grad, out_grad, *refs):
+def last_kernel(part, middle, first_terms, second_terms, query_grad, kv_grad, out_grad, *refs):
     refs = list(refs)
-    input_out, output, gains_out, query_out, kv_out, out_out = [refs.pop(0) for _ in range(6)]
+    output, gains_out, query_out, kv_out, out_out = [refs.pop(0) for _ in range(5)]
     place = Place()
-    first = Reduce(place, part, refs)
-    second = Reduce(place, other, refs)
+    reduce = Reduce(place, part, refs)
     query_own, query_in, kv_own, core_in, x_in, y_in = [refs.pop(0) for _ in range(6)]
     hop_send, hop_recv, hop_local, z_send, z_recv, z_local = [refs.pop(0) for _ in range(6)]
     terms, gain_in, gain_send, gain_recv = [refs.pop(0) for _ in range(4)]
@@ -1183,59 +1589,44 @@
             terms[...] += gain_in[number + i]
 
     place.enter(True)
-    first.begin()
     over_core.begin()
     query.begin()
-    over_out.start()
-    second.begin()
-    for m in range(first.micro):
-        first.pass_x(m)
+    reduce.begin()
+    terms[...] = jnp.zeros_like(terms)
+    terms[0:1, :] = jnp.sum(first_terms[...], axis=0, keepdims=True)
+    terms[1:2, :] = jnp.sum(second_terms[...], axis=0, keepdims=True)
     over_core.add()
     over_x.begin()
-    first.sums(0)
+    add_gains(0, [place.core_peer])
+    reduce.pass_x(0)
     query.add()
     for step in (1, 3, 2, 0):
         z_copy(step, 0).start()
-    for m in range(second.micro):
-        second.pass_x(m)
-    first.sums(1)
+    over_out.start()
+    add_gains(1, [place.x_peer])
     over_x.add()
     over_y.begin()
-    first.end_chain()
-    second.sums(0)
+    for m in range(1, reduce.micro):
+        reduce.pass_x(m)
+    add_gains(2, [place.y_peer])
+    reduce.sums(0)
     over_y.add()
     for step in (1, 3, 2, 0):
         for piece in (1, 2):
             z_copy(step, piece).start()
-    terms[...] = jnp.zeros_like(terms)
-    for m in range(first.micro):
-        first.finish(m)
-
-        def body(span, m=m):
-            result, found = norm_back(
-                first.total[m, span, :], tokens[m, span, :].astype(F32), middle_grad[m, span, :], gain[...]
-            )
-            input_out[m, span, :] = result.astype(BF16)
-            terms[0:1, :] += jnp.sum(found, axis=0, keepdims=True)
-
-        by_rows(first.rows, body)
-    terms[1:2, :] = jnp.sum(terms_in[...], axis=0, keepdims=True)
-    add_gains(0, [place.core_peer])
-    second.sums(1)
-    add_gains(1, [place.x_peer])
-    second.end_chain()
-    add_gains(2, [place.y_peer])
-    for m in range(second.micro):
-        second.finish(m)
-
-        def finish(span, m=m):
-            output[m, span, :] = (middle[m, span, :] + second.total[m, span, :]).astype(BF16)
-
-        by_rows(second.rows, finish)
     add_gains(3, place.z_peers[1:])
     gains_out[...] = terms[...]
-    first.drain()
-    second.drain()
+    for m in range(1, reduce.micro):
+        reduce.sums(m)
+    reduce.end_chain()
+    for m in range(reduce.micro):
+        reduce.finish(m)
+
+        def finish(span, m=m):
+            output[m, span, :] = (middle[m, span, :] + reduce.total[m, span, :]).astype(BF16)
+
+        by_rows(reduce.rows, finish)
+    reduce.drain()
     over_out.wait()
     for step in range(ZS):
         for piece in range(3):
@@ -1254,66 +1645,6 @@
         ),
         cost_estimate=pl.CostEstimate(flops=0, bytes_accessed=int(seconds * 3e12), transcendentals=0),
     )(*operands)
-
-
-def attend_kernel(qkv_ref, cos_ref, sin_ref, row_ref, key_ref, turned_ref, out_ref):
-    cosine, sine = cos_ref[...], sin_ref[...]
-    width = out_ref.shape[2]
-    for head in range(width // HDIM):
-        parts = []
-        for kind in range(3):
-            span = slice(kind * width + head * HDIM, kind * width + (head + 1) * HDIM)
-            value = qkv_ref[0, :, span]
-            if kind < 2:
-                value = turned(value, cosine, sine)
-            value = value.astype(BF16)
-            turned_ref[0, :, span] = value
-            parts.append(value)
-        query, key, value = parts
-        probs = masked_probs(query, key, row_ref[0], key_ref[0]).astype(BF16)
-        out_ref[0, :, head * HDIM : (head + 1) * HDIM] = dot(probs, value).astype(BF16)
-
-
-def attend_back_kernel(turned_ref, grad_ref, cos_ref, sin_ref, row_ref, key_ref, out_ref):
-    cosine, sine = cos_ref[...], -sin_ref[...]
-    width = grad_ref.shape[2]
-    for head in range(width // HDIM):
-        spans = [slice(kind * width + head * HDIM, kind * width + (head + 1) * HDIM) for kind in range(3)]
-        query, key, value = [turned_ref[0, :, span] for span in spans]
-        grad = grad_ref[0, :, spans[0]]
-        probs = masked_probs(query, key, row_ref[0], key_ref[0])
-        prob_grad = dot_t(grad, value)
-        inner = jnp.sum(probs * prob_grad, axis=1, keepdims=True)
-        raw_grad = (probs * (prob_grad - inner) * HDIM ** (-0.5)).astype(BF16)
-        results = [
-            turned(dot(raw_grad, key), cosine, sine),
-            turned(dot_l(raw_grad, query), cosine, sine),
-            dot_l(probs.astype(BF16), grad),
-        ]
-        for span, result in zip(spans, results):
-            out_ref[0, :, span] = result.astype(BF16)
-
-
-def per_sequence(kernel, operands, tables, out_widths, matmuls):
-    seqs, rows = operands[0].shape[:2]
-    own = [pl.BlockSpec((1,) + value.shape[1:], lambda k: (k, 0, 0)) for value in operands]
-    shared = [pl.BlockSpec(value.shape, lambda k: (0, 0)) for value in tables[:2]]
-    blocks = [pl.BlockSpec((1,) + value.shape[1:], lambda k: (k, 0, 0)) for value in tables[2:]]
-    width = out_widths[-1] if len(out_widths) > 1 else out_widths[0] // 3
-    moved = sum(value.size * value.dtype.itemsize for value in operands) + 2 * seqs * rows * sum(out_widths)
-    return pl.pallas_call(
-        kernel,
-        grid=(seqs,),
-        in_specs=own + shared + blocks,
-        out_specs=[pl.BlockSpec((1, rows, out), lambda k: (k, 0, 0)) for out in out_widths],
-        out_shape=[jax.ShapeDtypeStruct((seqs, rows, out), BF16) for out in out_widths],
-        compiler_params=pltpu.CompilerParams(vmem_limit_bytes=40 << 20),
-        cost_estimate=pl.CostEstimate(
-            flops=2 * matmuls * seqs * rows * rows * width,
-            bytes_accessed=moved,
-            transcendentals=seqs * rows * rows * width // HDIM,
-        ),
-    )(*operands, *tables)
 
 
 def fast_device(
@@ -1367,169 +1698,228 @@
     gathered = jax.ShapeDtypeStruct(everyone, BF16)
     terms = jax.ShapeDtypeStruct((STEP, model), F32)
     own_buffer = pltpu.VMEM(shape, BF16)
-    normed, cotangents, table, qkv_weight, out_weight, down_weight = connect(
-        functools.partial(
-            start_kernel, (wide, kv_rows, model_rows, w_out.shape[1], w_down.shape[1])
-        ),
-        [tokens, cotangent, first_gain, table, w_kv, w_query, w_out, w_down],
-        [VMEM, VMEM, VMEM, VMEM, ANY, ANY, ANY, ANY],
+    gate_weight = jax.ShapeDtypeStruct((model, hidden_width), BF16)
+    normed, table, qkv_weight, out_weight, gate_weight = connect(
+        functools.partial(start_kernel, (wide, kv_rows, model_rows, w_out.shape[1])),
+        [tokens, first_gain, table, w_kv, w_query, w_out, w_gate_up],
+        [VMEM, VMEM, VMEM, ANY, ANY, ANY, ANY],
         [
-            gathered,
             gathered,
             jax.ShapeDtypeStruct((1, ZS, CS, XS) + table.shape[1:], F32),
             jax.ShapeDtypeStruct((model, 3 * wide), BF16),
             jax.ShapeDtypeStruct((wide, model), BF16),
-            jax.ShapeDtypeStruct((hidden_width, model), BF16),
+            gate_weight,
         ],
-        [ANY] * 6,
+        [ANY] * 5,
         [own_buffer]
-        + Gather.scratch(micro)
         + Gather.scratch(micro)
         + Gather.scratch(1)
         + Spread.scratch(2, 3)
         + Spread.scratch(1, 1)
-        + Share.scratch(2),
+        + Share.scratch(1)
+        + Spread.scratch(1, 1),
         1,
-        140e-6,
-    )
-    cotangents = cotangents.reshape(seqs, SEQ, model)
-    normed = normed.reshape(-1, model)
-    gate_part = w_gate_up[0, :, : ZS * hidden_width]
-    gate_part, normed = lax.optimization_barrier((gate_part, normed))
-    gate_part = z_exchange(gate_part.reshape(model_rows, ZS, hidden_width).transpose(1, 0, 2))
+        130e-6,
+    )
 
     part = table[0, ..., : 9 * micro, :local].reshape(ZS, CS, XS, micro, 9, local)
     part = part.transpose(3, 0, 1, 2, 5, 4).reshape(seqs, SEQ, 9)
-    att_weight = jnp.sum(jnp.where(part[..., 0:2] == owner, part[..., 2:4], 0.0), axis=-1).reshape(-1, 1)
+    att_weight = jnp.sum(jnp.where(part[..., 0:2] == owner, part[..., 2:4], 0.0), axis=-1)[..., None]
     hit = jnp.any(part[..., 4:6] == owner, axis=-1)
     mlp_weight = jnp.sum(jnp.where(part[..., 4:6] == owner, part[..., 6:8], 0.0), axis=-1)
     seq_blocks = part[..., 8].astype(jnp.int32)
     tables = [cosine, sine, seq_blocks[:, :, None], seq_blocks[:, None, :]]
     before_mask = jnp.arange(SEQ)[:, None] < jnp.arange(SEQ)[None, :]
     before = dot(hit.astype(BF16), before_mask.astype(BF16)).astype(jnp.int32)
-    slots = jnp.arange(XS * CS * CAP)
+    slots = jnp.arange(XS * CS * CAP + -XS * CS * CAP % STEP)
     chosen = hit[:, None, :] & (before[:, None, :] == slots[None, :, None])
     row_gate = jnp.sum(jnp.where(chosen, mlp_weight[:, None, :], 0.0), axis=2)
     select = chosen.astype(BF16)
-
-    def to_rows(gathered):
-        return jnp.einsum("gru,gud->grd", select, gathered, preferred_element_type=F32)
-
-    def to_tokens(rows):
-        rows = rows.reshape(seqs, -1, model)
-        rows = jnp.einsum("gru,grd->gud", select, rows, preferred_element_type=F32).astype(BF16)
-        return rows.reshape(everyone)
-
-    qkv = dot(normed, qkv_weight).reshape(seqs, SEQ, 3 * wide)
-    turned_qkv, attended = per_sequence(attend_kernel, [qkv], tables, [3 * wide, wide], 2)
-    attended = attended.reshape(-1, wide)
-    result = (dot(attended, out_weight) * att_weight).astype(BF16).reshape(everyone)
-    normed_two, gate_up, middle = connect(
-        functools.partial(first_kernel, (model_rows, hidden_width)),
-        [result, tokens, second_gain, w_gate_up, gate_part],
-        [ANY, VMEM, VMEM, ANY, ANY],
-        [gathered, jax.ShapeDtypeStruct((model, 2 * hidden_width), BF16), tall],
-        [ANY, ANY, VMEM],
-        [own_buffer]
-        + Reduce.scratch(*shape)
+    slot_count = select.shape[1]
+
+    def kept(width, rows=SEQ):
+        return jax.ShapeDtypeStruct((seqs, rows, width), BF16)
+
+    normed_two, middle, turned_qkv, attended, up_weight, down_weight = connect(
+        functools.partial(attend_kernel, (model_rows, w_down.shape[1])),
+        [
+            normed.reshape(seqs, SEQ, model),
+            qkv_weight,
+            out_weight,
+            att_weight,
+            *tables,
+            tokens,
+            second_gain,
+            w_gate_up,
+            w_down,
+        ],
+        [ANY] + [VMEM] * 9 + [ANY] * 2,
+        [
+            short,
+            tall,
+            kept(3 * wide),
+            kept(wide),
+            jax.ShapeDtypeStruct(gate_weight.shape, BF16),
+            jax.ShapeDtypeStruct((hidden_width, model), BF16),
+        ],
+        [VMEM, VMEM] + [ANY] * 4,
+        PieceReduce.scratch(*shape)
+        + Spread.scratch(1, 1)
+        + Share.scratch(1)
+        + [
+            pltpu.VMEM((SEQ, model), BF16),
+            pltpu.VMEM((SEQ, 3 * wide), BF16),
+            pltpu.VMEM((SEQ, wide), BF16),
+            DMA,
+            DMA((2,)),
+        ],
+        2,
+        130e-6,
+    )
+
+    middle_rows, middle_grad, gain_second, rows_two, both_grad, hidden, down_grad, result_two, *_ = connect(
+        mlp_kernel,
+        [
+            normed_two,
+            gate_weight,
+            up_weight,
+            down_weight,
+            select,
+            select.transpose(0, 2, 1),
+            row_gate[:, :, None],
+            middle,
+            cotangent,
+            second_gain,
+        ],
+        [VMEM] * 10,
+        [
+            short,
+            tall,
+            terms,
+            kept(model, slot_count),
+            kept(2 * hidden_width, slot_count),
+            kept(hidden_width, slot_count),
+            kept(model, slot_count),
+            kept(model),
+            gathered,
+            gathered,
+        ],
+        [VMEM, VMEM, VMEM] + [ANY] * 7,
+        Gather.scratch(micro)
         + Gather.scratch(micro)
-        + Share.scratch(ZS)
-        + Spread.scratch(1, 1),
-        2,
+        + PieceReduce.scratch(*shape)
+        + [
+            pltpu.VMEM((CS, XS, local, model), BF16),
+            pltpu.VMEM((CS, XS, local, model), BF16),
+            pltpu.VMEM((slot_count, model), BF16),
+            pltpu.VMEM((slot_count, model), BF16),
+            pltpu.VMEM((slot_count, hidden_width), BF16),
+            pltpu.VMEM((slot_count, 2 * hidden_width), BF16),
+            pltpu.VMEM((SEQ, model), BF16),
+            DMA((2, CS, XS)),
+            DMA((5,)),
+        ],
+        5,
         150e-6,
     )
-    rows_two = to_rows(normed_two.reshape(seqs, SEQ, model)).astype(BF16).reshape(-1, model)
-    down_grad = (to_rows(cotangents) * row_gate[:, :, None]).astype(BF16).reshape(-1, model)
-    both = dot(rows_two, gate_up)
-    gate, up = both[:, :hidden_width], both[:, hidden_width:]
-    sigma = 1.0 / (1.0 + jnp.exp(-gate))
-    hidden = (gate * sigma * up).astype(BF16)
-    hidden_grad = dot_t(down_grad, down_weight)
-    slope = sigma * (1.0 + gate * (1.0 - sigma))
-    both_grad = jnp.concatenate(
-        [hidden_grad * up * slope, hidden_grad * gate * sigma], axis=1
-    ).astype(BF16)
-    row_grad = to_tokens(dot_t(both_grad, gate_up).astype(BF16))
-    result_two = to_tokens((dot(hidden, down_weight) * row_gate.reshape(-1, 1)).astype(BF16))
-
-    def halved(value, other):
-        return (take(value, y, 1).astype(F32) + other.astype(F32)).astype(BF16)
+    rows_two, both_grad, hidden, down_grad = [
+        value.reshape(-1, value.shape[2]) for value in (rows_two, both_grad, hidden, down_grad)
+    ]
+    result_two = result_two.reshape(everyone)
 
     def by_y(value):
         return value.astype(BF16).reshape(ZS, YS, model_rows, hidden_width)
 
     gate_grad = by_y(dot_l(rows_two, both_grad[:, :hidden_width]))
-    gate_grad = halved(gate_grad, y_move(take(gate_grad, 1 - y, 1)))
     up_grad = by_y(dot_l(rows_two, both_grad[:, hidden_width:]))
     grad_down = dot_l(hidden, down_grad).reshape(YS, -1, model)
-    middle_grads, middle_grad, gain_second, gate_grad, up_other, down_other = connect(
-        second_kernel,
-        [row_grad, middle, cotangent, second_gain, gate_grad, up_grad, grad_down.astype(BF16)],
-        [ANY, VMEM, VMEM, VMEM, ANY, ANY, ANY],
+    down_other = y_move(take(grad_down, 1 - y, 0).astype(BF16))
+    input_grad, gain_first, result_grad, qkv_grad, gate_grad, up_other, _ = connect(
+        attend_back_kernel,
         [
-            gathered,
-            tall,
+            middle_rows,
+            qkv_weight,
+            out_weight,
+            att_weight,
+            *tables,
+            turned_qkv,
+            tokens,
+            middle_grad,
+            first_gain,
+            gate_grad,
+            up_grad,
+        ],
+        [VMEM] * 8 + [ANY] + [VMEM] * 3 + [ANY] * 2,
+        [
+            short,
             terms,
+            kept(model),
+            kept(3 * wide),
             jax.ShapeDtypeStruct((model_rows, ZS * hidden_width), BF16),
             jax.ShapeDtypeStruct((ZS, model_rows, hidden_width), BF16),
-            jax.ShapeDtypeStruct(w_down.shape[1:], BF16),
+            gathered,
         ],
-        [ANY, VMEM, VMEM, ANY, ANY, ANY],
-        [own_buffer]
-        + Reduce.scratch(*shape)
-        + Gather.scratch(micro)
-        + [DMA, DMA((ZS,)), DMA((ZS,)), DMA((2,)), DMA((2,))],
+        [VMEM, VMEM] + [ANY] * 5,
+        Gather.scratch(micro)
+        + PieceReduce.scratch(*shape)
+        + [
+            pltpu.VMEM((CS, XS, local, model), BF16),
+            pltpu.VMEM((SEQ, 3 * wide), BF16),
+            pltpu.VMEM((SEQ, model), BF16),
+            pltpu.VMEM((SEQ, 3 * wide), BF16),
+            DMA((CS + 1, XS)),
+            DMA((2,)),
+            pltpu.VMEM((ZS, model_rows, hidden_width), BF16),
+            pltpu.VMEM((ZS, model_rows, hidden_width), BF16),
+            DMA((ZS,)),
+            DMA((2 * ZS,)),
+            DMA((2 * ZS,)),
+            DMA((ZS,)),
+            DMA((ZS,)),
+            DMA,
+        ],
         3,
-        130e-6,
-    )
-    up_grad = z_exchange(halved(up_grad, up_other))
-    grad_down = (take(grad_down, y, 0) + down_other.astype(F32))[None]
-    result_grad = (middle_grads.reshape(-1, model).astype(F32) * att_weight).astype(BF16)
-    attended_grad = dot_t(result_grad, out_weight).astype(BF16).reshape(seqs, SEQ, wide)
-    qkv_grad = per_sequence(attend_back_kernel, [turned_qkv, attended_grad], tables, [3 * wide], 5)[0]
-    qkv_grad = qkv_grad.reshape(-1, 3 * wide)
-    normed_part = dot_t(qkv_grad, qkv_weight).astype(BF16).reshape(everyone)
+        150e-6,
+    )
+    up_grad = (take(up_grad, y, 1).astype(F32) + up_other.astype(F32)).astype(BF16)
+    up_grad = z_exchange(up_grad)
+    result_grad, qkv_grad, attended, normed = [
+        value.reshape(-1, value.shape[-1]) for value in (result_grad, qkv_grad, attended, normed)
+    ]
     grad_out = dot_l(attended, result_grad).reshape(YS, -1, model)
     query_grad = dot_l(normed, qkv_grad[:, :wide]).astype(BF16).reshape(ZS, YS, model_rows, wide)
     kv_grad = dot_l(normed, qkv_grad[:, wide:]).astype(BF16).reshape(-1, CS, kv_rows, 2 * wide)
-    normed_part, up_grad = lax.optimization_barrier((normed_part, up_grad))
-    input_grad, output, gains, query_grad, kv_grad, out_other = connect(
+    output, gains, query_grad, kv_grad, out_other = connect(
         last_kernel,
         [
-            normed_part,
             result_two,
-            tokens,
             middle,
-            middle_grad,
-            first_gain,
+            gain_first,
             gain_second,
             query_grad,
             kv_grad,
             grad_out.astype(BF16),
         ],
-        [ANY, ANY, VMEM, VMEM, VMEM, VMEM, VMEM, ANY, ANY, ANY],
+        [ANY, VMEM, VMEM, VMEM] + [ANY] * 3,
         [
-            short,
             short,
             jax.ShapeDtypeStruct((8, model), F32),
             jax.ShapeDtypeStruct((model_rows, ZS * wide), BF16),
             jax.ShapeDtypeStruct((kv_rows, 2 * ZS * wide), BF16),
             jax.ShapeDtypeStruct(w_out.shape[1:], BF16),
         ],
-        [VMEM, VMEM, VMEM, ANY, ANY, ANY],
+        [VMEM, VMEM] + [ANY] * 3,
         Reduce.scratch(*shape)
-        + Reduce.scratch(*shape)
         + [pltpu.VMEM((ZS, model_rows, wide), BF16) for _ in range(2)]
         + [pltpu.VMEM((ZS * YS * XS, kv_rows, 2 * wide), BF16) for _ in range(2)]
         + [pltpu.VMEM((ZS * YS, kv_rows, 2 * wide), BF16), pltpu.VMEM((ZS, kv_rows, 2 * wide), BF16)]
-        + [DMA((5,)), DMA((5,)), DMA((2,)), DMA((ZS, 3)), DMA((ZS, 3)), DMA((3,))]
+        + [DMA((6,)), DMA((6,)), DMA((2,)), DMA((ZS, 3)), DMA((ZS, 3)), DMA((3,))]
         + [pltpu.VMEM((8, model), F32), pltpu.VMEM((6, 8, model), F32), DMA((6,)), DMA((6,))],
         4,
-        130e-6,
+        90e-6,
     )
     devices = ZS * YS * XS * CS
     gains = take(gains[:2].reshape(2, devices, model // devices), group * XS * CS + owner, 1)
-    gate_up_grad = [gate_grad.astype(F32)] + [up_grad[z].astype(F32) for z in range(ZS)]
     return (
         output,
         input_grad,
@@ -1538,8 +1928,8 @@
         kv_grad.astype(F32),
         query_grad.astype(F32)[None],
         (take(grad_out, y, 0) + out_other.astype(F32))[None],
-        jnp.concatenate(gate_up_grad, axis=1)[None],
-        grad_down,
+        jnp.concatenate([gate_grad.astype(F32)] + [up_grad[z].astype(F32) for z in range(ZS)], axis=1)[None],
+        (take(grad_down, y, 0) + down_other.astype(F32))[None],
     )
 
 

time: 1120 us -> 1050 us (0.938)
  matrix products: 269 us -> 88.4 us
  Pallas kernels: 728 us -> 873 us
  waiting for transfers between devices: 21.8 us -> 0.01 us
    pallas_call x4 -> x5, Pallas kernels: 672 us -> 873 us  [connect(): pl.pallas_call(kernel, in_specs=spaces, out_specs=out_spaces, out_shape=o...]
    dot_general x8 -> x0, matrix products: 110 us -> none  [the longest x4 75.7 us: dot_t(): lax.dot_general(left, right, (((1,), (1,)), ((), ())), preferred_element_...]
    dot_general x5 -> x1, matrix products: 74.2 us -> 0.12 us  [dot(): return jnp.dot(left, right, preferred_element_type=F32)]
    pallas_call x2 -> x0, Pallas kernels: 56.5 us -> none  [per_sequence(): pl.pallas_call(kernel, grid=(seqs,), in_specs=own + shared + blocks, out_...]
    all_to_all x2 -> x1, waiting for transfers between devices: 21.8 us -> 0.01 us  [z_exchange(): lax.all_to_all(value, 'group', split_axis=0, concat_axis=0, tiled=True, a...]
  transfers between devices with their start and end apart: 3 -> 2, of which waited for: 1 -> 0; matrix products, arithmetic and copies ran while one was open for 15% -> 10% of each run, Pallas kernels for 2% -> 29%
where the time goes in v3:
time: 1050 us; the launch traced here: 1040 us
  Pallas kernels  873 us (83%)
  matrix products  88.4 us (8%)
  other arithmetic  37.4 us (4%)
  local copies, waits for them, and re-layouts  34.7 us (3%)
    pallas_call x5, Pallas kernels, connect(): pl.pallas_call(kernel, in_specs=spaces, out_specs=out_spaces, out_shape=o...  873 us
    dot_general x6, matrix products, dot_l(): lax.dot_general(left, right, (((0,), (0,)), ((), ())), preferred_element_...  88.3 us
  transfers between devices with their start and end apart: 2, of which 0 were waited for; matrix products, arithmetic and copies ran while one was open for 10% of the time, Pallas kernels for 29%

profile of v3, /device:TPU:0, one launch (start us, length us, event | category | flops | bytes accessed | tf_op | source)
XLA Modules:
  0.0 1041.9 jit_solution(3687989723212108277)
XLA Ops:
  0.6 0.7 fusion.39
  1.4 0.7 fusion.41
  2.1 0.7 fusion.40
  3.0 0.7 slice_bitcast_fusion.4
  3.9 0.6 pad_bitcast_fusion.table
  4.5 181.1 %shard_map.205 = (bf16[2,4,2,2,80,2048]{5,4,3,2,1,0:T(8,128)(2,1)}, f32[1,4,2,2,24,128]{5,4,3,2,1,0:T(8,128)}, bf16[2048,1536]{1,0:T(8,128)(2,1)}, bf16[512,2048]{1,0:T(8,128)(2,1)}, bf16[2048,1408]{1,0:T(8,128)(2,1)}) custom-call(bf16[2,80,2048]{2,1,0:T(8,128)(2,1)} %tokens.5, f32[1,2048]{1,0:T(1,128)} %bitcast.145, f32[1,24,128]{2,1,0:T(8,128)} %pad_bitcast_fusion.table, ...), custom_call_target="tpu_custom_call" | custom-call | bytes 390000000 | tf_op jit(solution)/shard_map/pallas_call | solution.py:1637
  185.6 1.0 copy.28
  186.7 0.2 reshape.205
  187.1 0.6 fusion.37
  187.8 2.2 fusion.12.select_back
  190.0 1.6 fusion.14.select
  191.6 0.6 select_reduce_fusion
  192.2 1.2 copy.32.gates
  193.7 0.7 fusion.20
  194.3 0.8 pad_maximum_fusion.cosine
  195.1 1.5 copy.30.row_gate
  196.6 1.5 copy.31.row_blocks
  198.1 0.8 pad_maximum_fusion.1.sine
  198.9 151.6 %shard_map.206 = (bf16[2,80,2048]{2,1,0:T(8,128)(2,1)}, f32[2,80,2048]{2,1,0:T(8,128)}, bf16[8,320,1536]{2,1,0:T(8,128)(2,1)}, bf16[8,320,512]{2,1,0:T(8,128)(2,...) custom-call(bf16[8,320,2048]{2,1,0:T(8,128)(2,1)} %bitcast.129, bf16[2048,1536]{1,0:T(8,128)(2,1)} %get-tuple-element.40.weight, ...), custom_call_target="tpu_custom_call" | custom-call | bytes 390000000 | tf_op jit(solution)/shard_map/pallas_call | solution.py:1637
  350.5 237.5 %shard_map.207 = (bf16[2,80,2048]{2,1,0:T(8,128)(2,1)}, f32[2,80,2048]{2,1,0:T(8,128)}, f32[16,2048]{1,0:T(8,128)}, bf16[8,208,2048]{2,1,0:T(8,128)(2,1)}, bf16[...) custom-call(bf16[2,80,2048]{2,1,0:T(8,128)(2,1)} %get-tuple-element., ...), custom_call_target="tpu_custom_call" | custom-call | bytes 450000000 | tf_op jit(solution)/shard_map/pallas_call | solution.py:1637
  588.0 7.5 copy.36
  595.4 16.7 %fusion.43 = f32[2,704,2048]{2,1,0:T(8,128)} fusion(bf16[2,704,1664]{2,1,0:T(8,128)(2,1)} %bitcast.134, bf16[1664,2048,1]{1,0,2:T(8,128)(2,1)} %bitcast.156), kind=kOutput, calls=%fused_computation.86 | convolution fusion | flops 9596567552 | bytes 23035904 | tf_op jit(solution)/shard_map/dot_general | solution.py:455
  612.1 4.8 fusion.9
  617.0 2.5 collective-permute-start
  619.5 16.9 %convolution_convert_fusion = bf16[2048,1408]{1,0:T(8,128)(2,1)} fusion(bf16[1664,2048]{1,0:T(8,128)(2,1)} %bitcast.154, bf16[1664,2816]{1,0:T(8,128)(2,1)} %bitcast.148), kind=kOutput, calls=%fused_computation | convolution fusion | flops 9599451136 | bytes 17268736 | tf_op jit(solution)/shard_map/dot_general | solution.py:455
  636.4 15.6 %convolution_convert_fusion.1 = bf16[2048,1408]{1,0:T(8,128)(2,1)} fusion(bf16[1664,2048]{1,0:T(8,128)(2,1)} %bitcast.155, bf16[1664,2816]{1,0:T(8,128)(2,1)S(1)} %bitcast.151), kind=kOutput, calls=%fused_computation.1 | convolution fusion | flops 9599451136 | bytes 17268736 | tf_op jit(solution)/shard_map/dot_general | solution.py:455
  651.9 161.1 %shard_map.208 = (bf16[2,80,2048]{2,1,0:T(8,128)(2,1)}, f32[16,2048]{1,0:T(8,128)}, bf16[8,320,2048]{2,1,0:T(8,128)(2,1)}, bf16[8,320,1536]{2,1,0:T(8,128)(2,1)}...) custom-call(bf16[2,80,2048]{2,1,0:T(8,128)(2,1)} %get-tuple-element.49.rows, ...), custom_call_target="tpu_custom_call" | custom-call | bytes 450000000 | tf_op jit(solution)/shard_map/pallas_call | solution.py:1637
  813.0 5.0 fusion
  818.0 4.9 all-to-all-start
  823.0 16.8 %fusion.6 = bf16[2048,1024]{1,0:T(8,128)(2,1)} fusion(bf16[2560,2048]{1,0:T(8,128)(2,1)} %bitcast.130, bf16[2560,1536]{1,0:T(8,128)(2,1)} %bitcast.152), kind=kOutput, calls=%fused_computation.12 | convolution fusion | flops 10739515392 | bytes 19922944 | tf_op jit(solution)/shard_map/dot_general | solution.py:455
  839.8 11.6 %convolution_convert_fusion.2 = bf16[2048,512]{1,0:T(8,128)(2,1)} fusion(bf16[2560,2048]{1,0:T(8,128)(2,1)} %bitcast.131, bf16[2560,1536]{1,0:T(8,128)(2,1)} %bitcast.153), kind=kOutput, calls=%fused_computation.13 | convolution fusion | flops 5369757696 | bytes 15204352 | tf_op jit(solution)/shard_map/dot_general | solution.py:455
  851.4 4.4 copy.35
  855.8 10.7 %fusion.42 = (bf16[2,256,2048]{2,1,0:T(8,128)(2,1)}, f32[2,256,2048]{2,1,0:T(8,128)}) fusion(bf16[2,256,2560]{2,1,0:T(8,128)(2,1)} %bitcast.137, bf16[2560,2048,1]{1,0,2:T(8,128)(2,1)} %bitcast.147), kind=kOutput, calls=%fused_computation.85 | convolution fusion | flops 5369757696 | bytes 19398656 | tf_op jit(solution)/shard_map/dot_general | solution.py:455
  866.5 141.7 %shard_map.209 = (bf16[2,80,2048]{2,1,0:T(8,128)(2,1)}, f32[8,2048]{1,0:T(8,128)}, bf16[256,2048]{1,0:T(8,128)(2,1)}, bf16[64,4096]{1,0:T(8,128)(2,1)}, bf16[256,2048]{1,0:T(8,128)(2,1)}) custom-call(bf16[2,4,2,2,80,2048]{5,4,3,2,1,0:T(8,128)(2,1)} %bitcast.128, f32[2,80,2048]{2,1,0:T(8,128)} %get-tuple-element.47.middle, ...), custom_call_target="tpu_custom_call" | custom-call | bytes 270000000 | tf_op jit(solution)/shard_map/pallas_call | solution.py:1637
  1008.2 2.1 convert_element_type.180
  1010.3 0.8 slice.104
  1011.3 0.5 fusion.35
  1011.8 3.0 bitcast_convert_fusion.1
  1014.8 3.6 fusion.15
  1018.4 1.8 constant_dynamic-update-slice_fusion
  1020.2 7.3 fusion.1
  1027.6 1.0 fusion.19
  1028.6 0.9 fusion.18
  1029.5 1.0 fusion.17
  1030.5 1.0 fusion.16
  1031.5 8.5 bitcast_convert_fusion
  1040.0 0.8 copy.43
  1040.8 0.8 copy.44
  (29 shorter events, 1.1 us)
Async XLA Ops:
  612.1 24.2 %slice-start = ((s8[9371648]{0:T(1024)(128)(4,1)}), s8[983040]{0:T(1024)(128)(4,1)S(1)}, s32[]{:S(2)}) async-start(s8[9371648]{0:T(1024)(128)(4,1)} %bitcast.149), calls=%async_computation.1 | async-start | bytes 1966080
  617.0 403.3 %collective-permute-start = (bf16[704,2048]{1,0:T(8,128)(2,1)}, bf16[704,2048]{1,0:T(8,128)(2,1)}, u32[]{:S(2)}, u32[]{:S(2)}) collective-permute-start(bf16[704,2048]{1,0:T(8,128)(2,1)} %fusion.9), channel_id=1, source_target_pairs={{0,4},{4,0},{8,12},{12,8},{16,20},{20,16},{24,28},{28,24},{1,5},{5... | collective-permute-start | bytes 8650760 | tf_op jit(solution)/shard_map/ppermute | solution.py:394
  619.5 16.9 %slice-start.1 = ((s8[9371648]{0:T(1024)(128)(4,1)}), s8[4194304]{0:T(1024)(128)(4,1)S(1)}, s32[]{:S(2)}) async-start(s8[9371648]{0:T(1024)(128)(4,1)} %bitcast.149), calls=%async_computation.2 | async-start | bytes 8388608
  619.5 16.9 %slice-start.2 = ((s8[9371648]{0:T(1024)(128)(4,1)}), s8[4194304]{0:T(1024)(128)(4,1)S(1)}, s32[]{:S(2)}) async-start(s8[9371648]{0:T(1024)(128)(4,1)} %bitcast.149), calls=%async_computation.3 | async-start | bytes 8388608
  818.0 209.5 %all-to-all-start = ((bf16[4,256,1408]{2,1,0:T(8,128)(2,1)}), bf16[4,256,1408]{2,1,0:T(8,128)(2,1)S(1)}, u32[]{:S(2)}, u32[]{:S(2)}) async-start(bf16[4,256,1408]{2,1,0:T(8,128)(2,1)} %fusion), calls=%async_computation | async-start | bytes 5767168 | tf_op jit(solution)/shard_map/all_to_all | solution.py:415
  1011.3 7.2 copy-start
  1031.5 8.5 copy-start.2
  1031.5 9.4 copy-start.1

commit v4 on v3

--- a/solution.py
+++ b/solution.py
@@ -377,6 +377,8 @@
 
 ZS, YS, XS, CS = 4, 2, 2, 2
 SEQ = 320
+MICRO = 2
+KINDS = 9
 F32 = jnp.float32
 BF16 = jnp.bfloat16
 
@@ -641,13 +643,8 @@
     def sums(self, m):
         for turn, k in enumerate(ORDER):
             self.z_unit(m, k)
-            if m and turn < 2:
-                self.chain(m - 1, 2 - turn)
-        self.chain(m, ZS - 1)
-
-    def end_chain(self):
-        for far in range(ZS - 2, 0, -1):
-            self.chain(self.micro - 1, far)
+            if turn:
+                self.chain(m, ZS - turn)
 
     def run(self):
         self.begin()
@@ -655,7 +652,6 @@
             self.pass_x(m)
         for m in range(self.micro):
             self.sums(m)
-        self.end_chain()
 
     def drain(self):
         for m in range(self.micro):
@@ -754,6 +750,11 @@
         for dx in range(XS):
             self.over_core(m, self.own.at[m], k, dx).wait_recv()
 
+    def arrivals(self, m=0):
+        for k in range(ZS):
+            self.piece_arrival(m, k)
+        self.local(m).wait()
+
     def z_round(self, far, chosen=None):
         for m in range(self.micro) if chosen is None else [chosen]:
             self.z_arrival(m, far)
@@ -780,9 +781,7 @@
         for m in range(self.micro):
             own = self.own.at[m]
             if not waited:
-                for k in range(ZS):
-                    self.piece_arrival(m, k)
-                self.local(m).wait()
+                self.arrivals(m)
             pl.when(z < ZS - 1)(lambda: self.up(m, own, ZS - 1).wait_send())
             pl.when(z > 0)(lambda: self.down(m, own, 1).wait_send())
             for far in range(1, ZS - 1):
@@ -878,7 +877,7 @@
                     pl.when(self.beyond(down, far))(self.z_copy(m, down, far).wait_send)
 
 
-def piece_of(place, index):
+def piece_of(place, index, micro):
     turn = lax.rem(index, ZS)
     inner = turn + lax.div(turn, 2) * (5 - 2 * turn)
     last = lax.rem(ZS - turn, ZS)
@@ -892,7 +891,7 @@
     def step(index, carry):
         @pl.when(index < pieces)
         def _():
-            m, k = piece_of(place, index)
+            m, k = piece_of(place, index, reduce.micro)
             piece(index, m, k)
             reduce.begin_piece(m, k)
 
@@ -900,20 +899,19 @@
 
         @pl.when((index >= 1) & (index < pieces + 1))
         def _():
-            reduce.x_piece(*piece_of(place, index - 1))
-
-        @pl.when(index >= 3)
+            reduce.x_piece(*piece_of(place, index - 1, reduce.micro))
+
+        @pl.when((index >= 3) & (index < pieces + 3))
         def _():
-            reduce.z_piece(*piece_of(place, index - 3))
-
-        for m in range(reduce.micro - 1):
+            reduce.z_piece(*piece_of(place, index - 3, reduce.micro))
+
+        for m in range(reduce.micro):
+            first = (m + 1) * ZS + 2
             for far in range(1, ZS):
-                pl.when(index == (m + 1) * ZS + 2 + ZS - far)(functools.partial(reduce.chain, m, far))
+                pl.when(index == first + ZS - 1 - far)(functools.partial(reduce.chain, m, far))
         return carry
 
-    lax.fori_loop(0, pieces + 3, step, 0)
-    for far in range(ZS - 1, 0, -1):
-        reduce.chain(reduce.micro - 1, far)
+    lax.fori_loop(0, pieces + 5, step, 0)
 
 
 def begin_gathers(gathers):
@@ -1071,18 +1069,6 @@
     return target.at[pl.ds(pl.multiple_of(place.y * rows, rows), rows)]
 
 
-def gate_up_spread(place, source, kind, target, rows, refs):
-    width = target.shape[1]
-
-    def columns(z):
-        return source.at[0, :, pl.ds(pl.multiple_of((kind * ZS + z) * width, HDIM), width)]
-
-    def view(z, y, x, core):
-        return target.at[pl.ds(pl.multiple_of((z * YS + y) * rows, rows), rows)]
-
-    return Spread(place, lambda z: [columns(z)], lambda block: [block], view, 1, refs)
-
-
 def by_heads(width, body):
     def step(head, carry):
         body(lambda kind: pl.ds(pl.multiple_of(kind * width + head * HDIM, HDIM), HDIM))
@@ -1091,47 +1077,168 @@
     lax.fori_loop(0, width // HDIM, step, 0)
 
 
-def start_kernel(sizes, tokens, gain, table, w_kv, w_query, w_out, w_gate, *refs):
+def columns_of(marks, place, m, k):
+    local, lanes = marks.shape[3:]
+    length = CS * XS * local
+    block = marks[k].reshape(length, lanes)
+    across = jnp.transpose(block)
+
+    def pick(kind, source, axis):
+        value = None
+        for index in range(MICRO):
+            at = index * KINDS + kind
+            part = source[:, at : at + 1] if axis else source[at : at + 1, :]
+            value = part if value is None else jnp.where(m == index, part, value)
+        return value
+
+    owner = place.owner.astype(F32)
+    gates = [jnp.where(pick(kind, block, 1) == owner, pick(kind + 2, block, 1), 0.0) for kind in range(2)]
+    return gates[0] + gates[1], pick(KINDS - 1, block, 1), pick(KINDS - 1, across, 0)
+
+
+def attention_kernel(
+    sizes,
+    tokens,
+    cotangent,
+    first_gain,
+    second_gain,
+    table,
+    cosine,
+    sine,
+    w_kv,
+    w_query,
+    w_out,
+    w_gate_up,
+    w_down,
+    *refs,
+):
     refs = list(refs)
-    normed_out, table_out, qkv_weight, out_weight, gate_weight = [refs.pop(0) for _ in range(5)]
-    wide, kv_rows, model_rows, out_rows = sizes
+    normed_out, middle_out, everyone, cotangent_out, table_out, turned_out, attended_out = [
+        refs.pop(0) for _ in range(7)
+    ]
+    qkv_weight, out_weight, gate_up_weight, down_weight = [refs.pop(0) for _ in range(4)]
+    wide, kv_rows, model_rows, out_rows, down_rows = sizes
     place = Place()
-    normed_own = refs.pop(0)
-    normed = Gather(place, normed_own, normed_out, refs)
+    own = refs.pop(0)
+    normed = Gather(place, own, everyone, refs)
+    upstream = Gather(place, cotangent, cotangent_out, refs)
     tables = Gather(place, table, table_out, refs)
-
-    def lanes(start):
-        return pl.ds(pl.multiple_of(start, HDIM), wide)
+    reduce = PieceReduce(place, refs)
+
+    def lanes(start, width):
+        return pl.ds(pl.multiple_of(start, HDIM), width)
 
     def kv_view(z, y, x, core):
         row = ((z * YS + y) * (XS * CS) + x * CS + core) * kv_rows
         return qkv_weight.at[pl.ds(pl.multiple_of(row, kv_rows), kv_rows), pl.ds(wide, 2 * wide)]
 
-    def query_view(z, y, x, core):
-        row = (z * YS + y) * model_rows
-        return qkv_weight.at[pl.ds(pl.multiple_of(row, model_rows), model_rows), pl.ds(0, wide)]
+    def rows_of(z, y):
+        return pl.ds(pl.multiple_of((z * YS + y) * model_rows, model_rows), model_rows)
 
     kv = Spread(
         place,
-        lambda z: [w_kv.at[:, lanes(z * wide)], w_kv.at[:, lanes((ZS + z) * wide)]],
-        lambda block: [block.at[:, pl.ds(0, wide)], block.at[:, pl.ds(wide, wide)]],
+        lambda z: [w_kv.at[:, lanes((kind * ZS + z) * wide, wide)] for kind in range(2)],
+        lambda block: [block.at[:, pl.ds(kind * wide, wide)] for kind in range(2)],
         kv_view,
         3,
         refs,
     )
     query = Spread(
-        place, lambda z: [w_query.at[0, :, lanes(z * wide)]], lambda block: [block], query_view, 1, refs
-    )
-
+        place,
+        lambda z: [w_query.at[0, :, lanes(z * wide, wide)]],
+        lambda block: [block],
+        lambda z, y, x, core: qkv_weight.at[rows_of(z, y), pl.ds(0, wide)],
+        1,
+        refs,
+    )
+    hidden_width = gate_up_weight.shape[2]
+    gate_up = Spread(
+        place,
+        lambda z: [w_gate_up.at[0, :, lanes((kind * ZS + z) * hidden_width, hidden_width)] for kind in range(2)],
+        lambda block: [block.at[kind] for kind in range(2)],
+        lambda z, y, x, core: gate_up_weight.at[:, rows_of(z, y)],
+        1,
+        refs,
+    )
     shared = Share(place, [(w_out.at[0], y_half(place, out_weight, out_rows))], refs)
-    gate = gate_up_spread(place, w_gate, 0, gate_weight, model_rows, refs)
+    down = Share(place, [(w_down.at[0], y_half(place, down_weight, down_rows))], refs)
+    arrived, qkv, attended, marks, weight, out_here, load, store, late_load = [refs.pop(0) for _ in range(9)]
+    model = tokens.shape[2]
+    tile = model // 2
+    late_loads = [
+        pltpu.make_async_copy(qkv_weight, weight, late_load.at[0]),
+        pltpu.make_async_copy(out_weight, out_here, late_load.at[1]),
+        pltpu.make_async_copy(table_out.at[0], marks, late_load.at[2]),
+    ]
+
+    def stores(sequence):
+        return [
+            pltpu.make_async_copy(qkv, turned_out.at[sequence], store.at[0]),
+            pltpu.make_async_copy(attended, attended_out.at[sequence], store.at[1]),
+        ]
+
+    def piece(index, m, k):
+        sequence = m * ZS + k
+        normed.piece_arrival(m, k)
+        pl.when(k == 0)(functools.partial(wait_local, normed, m))
+        loads = [
+            pltpu.make_async_copy(everyone.at[m, k, dc, dx], arrived.at[dc, dx], load.at[dc, dx])
+            for dc in range(CS)
+            for dx in range(XS)
+        ]
+        for copy in loads:
+            copy.start()
+
+        @pl.when(index == 0)
+        def _():
+            for copy in late_loads:
+                copy.wait()
+
+        @pl.when(index > 0)
+        def _():
+            for copy in stores(0):
+                copy.wait()
+
+        row_gate, row_block, key_block = columns_of(marks, place, m, k)
+        for copy in loads:
+            copy.wait()
+        length = qkv.shape[0]
+        for kind in range(3):
+            value = dot(arrived[...].reshape(length, model), weight[:, kind * wide : (kind + 1) * wide])
+            for head in range(wide // HDIM):
+                part = value[:, head * HDIM : (head + 1) * HDIM]
+                if kind < 2:
+                    part = turned(part, cosine[...], sine[...])
+                start = kind * wide + head * HDIM
+                qkv[:, start : start + HDIM] = part.astype(BF16)
+
+        def head(span_of):
+            query, key, value = [qkv[:, span_of(kind)] for kind in range(3)]
+            probs = masked_probs(query, key, row_block, key_block).astype(BF16)
+            attended[:, span_of(0)] = dot(probs, value).astype(BF16)
+
+        by_heads(wide, head)
+        for start in range(0, model, tile):
+            value = dot(attended[...], out_here[:, start : start + tile]) * row_gate
+            reduce.part[m, k, :, start : start + tile] = value.astype(BF16)
+        for copy in stores(sequence):
+            copy.start()
+
+    def between(index):
+        for far in range(1, ZS):
+            pl.when(index == far - 1)(functools.partial(upstream.z_round, far))
+            pl.when(index == far)(functools.partial(upstream.x_round, far - 1))
+        pl.when(index == ZS)(functools.partial(upstream.x_round, ZS - 1))
+        pl.when(index == 4)(functools.partial(gate_up.slow_round, 2))
+
     place.enter(True)
+    shared.begin()
     kv.begin()
     tables.send_own(0)
     for m in range(normed.micro):
 
         def body(span, m=m):
-            normed_own[m, span, :] = normed_rows(tokens[m, span, :].astype(F32), gain[...]).astype(BF16)
+            own[m, span, :] = normed_rows(tokens[m, span, :].astype(F32), first_gain[...]).astype(BF16)
 
         by_rows(tokens.shape[1], body)
         normed.send_own(m)
@@ -1142,137 +1249,74 @@
     kv.z_round(3)
     normed.z_round(1)
     kv.z_round(2)
-    normed.x_round(0)
     for index in (0, 1, 3, 2):
         kv.hop_round(0, index)
+    normed.x_round(0)
+    gate_up.begin_slowly()
+    gate_up.slow_round(0)
     tables.z_round(2)
+    normed.z_round(2)
+    normed.x_round(1)
     for step in (0, 1, 3, 2):
         query.z_round(step)
-    normed.z_round(2)
-    gate.begin_slowly()
-    normed.x_round(1)
-    gate.slow_round(0)
-    normed.z_round(3)
     for index in (0, 2, 6, 4, 1, 3, 7, 5):
         kv.hop_round(1, index)
+    normed.z_round(3)
     tables.z_round(3)
-    gate.slow_round(1)
     for far in range(ZS):
         tables.x_round(far)
     normed.x_round(2)
     normed.x_round(3)
-    gate.slow_round(2)
+    for m in range(upstream.micro):
+        upstream.send_own(m)
     for index in range(ZS << 2):
         kv.hop_round(2, index)
     for index in range(ZS):
         query.hop_round(0, index)
-    shared.begin()
-    gate.slow_round(3)
-    for index in range(ZS):
-        gate.hop_round(0, index)
-    for part in (tables, normed, kv, query, shared, gate):
-        part.drain()
-
-
-def attend_kernel(
-    sizes, normed, weight, out_weight, row_gate, cosine, sine, row_blocks, key_blocks, tokens, gain, w_up, w_down, *refs
-):
-    refs = list(refs)
-    normed_out, middle_out, turned_out, attended_out, up_weight, down_weight = [refs.pop(0) for _ in range(6)]
-    model_rows, down_rows = sizes
-    place = Place()
-    reduce = PieceReduce(place, refs)
-    up = gate_up_spread(place, w_up, 1, up_weight, model_rows, refs)
-    shared = Share(place, [(w_down.at[0], y_half(place, down_weight, down_rows))], refs)
-    arrived, qkv, attended, load, store = [refs.pop(0) for _ in range(5)]
-    wide = out_weight.shape[0]
-    model = out_weight.shape[1]
-    tile = model // 2
-    pieces = reduce.micro * ZS
-
-    def load_of(index):
-        m, k = piece_of(place, index)
-        return pltpu.make_async_copy(normed.at[m * ZS + k], arrived, load)
-
-    def stores(sequence):
-        return [
-            pltpu.make_async_copy(qkv, turned_out.at[sequence], store.at[0]),
-            pltpu.make_async_copy(attended, attended_out.at[sequence], store.at[1]),
-        ]
-
-    def piece(index, m, k):
-        sequence = m * ZS + k
-
-        @pl.when(index > 0)
-        def _():
-            for copy in stores(0):
-                copy.wait()
-
-        load_of(index).wait()
-        for kind in range(3):
-            value = dot(arrived[...], weight[:, kind * wide : (kind + 1) * wide])
-            for head in range(wide // HDIM):
-                part = value[:, head * HDIM : (head + 1) * HDIM]
-                if kind < 2:
-                    part = turned(part, cosine[...], sine[...])
-                start = kind * wide + head * HDIM
-                qkv[:, start : start + HDIM] = part.astype(BF16)
-
-        @pl.when(index + 1 < pieces)
-        def _():
-            load_of(index + 1).start()
-
-        def head(span_of):
-            query, key, value = [qkv[:, span_of(kind)] for kind in range(3)]
-            probs = masked_probs(query, key, row_blocks[sequence], key_blocks[sequence]).astype(BF16)
-            attended[:, span_of(0)] = dot(probs, value).astype(BF16)
-
-        by_heads(wide, head)
-        for start in range(0, model, tile):
-            value = dot(attended[...], out_weight[:, start : start + tile]) * row_gate[sequence]
-            reduce.part[m, k, :, start : start + tile] = value.astype(BF16)
-        for copy in stores(sequence):
-            copy.start()
-
-    def between(index):
-        for turn, at in enumerate((1, 4, 7)):
-            pl.when(index == at)(functools.partial(up.slow_round, turn))
-
-    place.enter(True)
-    load_of(0).start()
-    up.begin_slowly()
-    shared.begin()
+    shared.drain()
+    tables.arrivals()
+    for copy in late_loads:
+        copy.start()
+    down.begin()
+    gate_up.slow_round(1)
     run_pieces(place, reduce, piece, between)
-    up.slow_round(3)
     for m in range(reduce.micro):
         reduce.finish(m)
 
         def body(span, m=m):
             middle = tokens[m, span, :].astype(F32) + reduce.total[m, span, :]
             middle_out[m, span, :] = middle
-            normed_out[m, span, :] = normed_rows(middle, gain[...]).astype(BF16)
+            normed_out[m, span, :] = normed_rows(middle, second_gain[...]).astype(BF16)
 
         by_rows(reduce.rows, body)
     for copy in stores(0):
         copy.wait()
+    gate_up.slow_round(3)
     for index in range(ZS):
-        up.hop_round(0, index)
-    for part in (shared, up, reduce):
+        gate_up.hop_round(0, index)
+    for gather in (tables, normed):
+        gather.drain(True)
+    for part in (upstream, kv, query, gate_up, down, reduce):
         part.drain()
 
 
 def attend_back_kernel(
-    rows, weight, out_weight, row_gate, cosine, sine, row_blocks, key_blocks, turned_qkv, tokens, middle_grad, gain, gate_grads, up_grads, *refs
+    rows, weight_in, out_in, marks, cosine, sine, turned_qkv, tokens, middle_grad, gain, gate_grads, up_grads, *refs
 ):
     refs = list(refs)
-    input_out, terms_out, row_grad_out, qkv_grad_out, weight_grad_out, other_out, everyone = [
+    input_out, terms_out, row_grad_out, qkv_grad_out, weight_grad_out, sums_out, everyone = [
         refs.pop(0) for _ in range(7)
     ]
     place = Place()
     gather = Gather(place, rows, everyone, refs)
     reduce = PieceReduce(place, refs)
     arrived, kept, row_grad, qkv_grad, load, store = [refs.pop(0) for _ in range(6)]
-    mine, theirs, mine_sem, y_send, y_recv, z_send, z_recv, z_local = [refs.pop(0) for _ in range(8)]
+    mine, theirs, mine_sem, y_send, y_recv, z_send, z_recv, sum_local = [refs.pop(0) for _ in range(8)]
+    weight, out_weight, weight_load = [refs.pop(0) for _ in range(3)]
+    weight_loads = [
+        pltpu.make_async_copy(weight_in, weight, weight_load.at[0]),
+        pltpu.make_async_copy(out_in, out_weight, weight_load.at[1]),
+    ]
     wide, model = out_weight.shape
     tile = model // 2
     width = mine.shape[2]
@@ -1296,6 +1340,11 @@
         for copy in loads:
             copy.start()
 
+        @pl.when(index == 0)
+        def _():
+            for copy in weight_loads:
+                copy.wait()
+
         @pl.when(index > 0)
         def _():
             for copy in stores(0):
@@ -1304,15 +1353,16 @@
         for copy in loads:
             copy.wait()
         length = kept.shape[0]
+        row_gate, row_block, key_block = columns_of(marks, place, m, k)
         for start in range(0, model, tile):
-            value = arrived[:, :, :, start : start + tile].astype(F32).reshape(length, tile) * row_gate[sequence]
+            value = arrived[:, :, :, start : start + tile].astype(F32).reshape(length, tile) * row_gate
             row_grad[:, start : start + tile] = value.astype(BF16)
         qkv_grad[:, :wide] = dot_t(row_grad[...], out_weight[...]).astype(BF16)
 
         def head(span_of):
             query, key, value = [kept[:, span_of(kind)] for kind in range(3)]
             grad = qkv_grad[:, span_of(0)]
-            probs = masked_probs(query, key, row_blocks[sequence], key_blocks[sequence])
+            probs = masked_probs(query, key, row_block, key_block)
             prob_grad = dot_t(grad, value)
             inner = jnp.sum(probs * prob_grad, axis=1, keepdims=True)
             raw_grad = (probs * (prob_grad - inner) * HDIM ** (-0.5)).astype(BF16)
@@ -1328,35 +1378,41 @@
             copy.start()
 
     steps = (1, 3, 2, 0)
+    sources = (gate_grads, up_grads)
 
     def z_of(turn):
         return lax.rem(place.z + steps[turn], ZS)
 
-    def own_copy(turn):
-        return pltpu.make_async_copy(gate_grads.at[z_of(turn), place.y], mine.at[turn], mine_sem.at[turn])
+    def own_copy(part):
+        kind, turn = divmod(part, ZS)
+        return pltpu.make_async_copy(sources[kind].at[z_of(turn), place.y], mine.at[part], mine_sem.at[part])
 
     def y_copy(part):
-        turn = part % ZS
-        grads, target = (up_grads, other_out.at[z_of(turn)]) if part >= ZS else (gate_grads, theirs.at[turn])
+        kind, turn = divmod(part, ZS)
         return remote(
-            grads.at[z_of(turn), 1 - place.y], target, y_send.at[part], y_recv.at[part], place.y_peer
+            sources[kind].at[z_of(turn), 1 - place.y],
+            theirs.at[part],
+            y_send.at[part],
+            y_recv.at[part],
+            place.y_peer,
         )
 
     columns = weight_grad_out.at[:, pl.ds(pl.multiple_of(place.z * width, HDIM), width)]
 
-    def z_copy(turn):
+    def sum_copy(part):
+        kind, turn = divmod(part, ZS)
+        if kind:
+            return pltpu.make_async_copy(theirs.at[part], sums_out.at[z_of(turn)], sum_local.at[part])
         if steps[turn] == 0:
-            return pltpu.make_async_copy(theirs.at[turn], columns, z_local)
+            return pltpu.make_async_copy(theirs.at[part], columns, sum_local.at[part])
         return remote(
-            theirs.at[turn], columns, z_send.at[steps[turn]], z_recv.at[steps[turn]], place.z_peers[steps[turn]]
+            theirs.at[part], columns, z_send.at[steps[turn]], z_recv.at[steps[turn]], place.z_peers[steps[turn]]
         )
 
     def pass_grads(part):
         y_copy(part).wait()
         if part + 2 < 2 * ZS:
             y_copy(part + 2).start()
-        if part >= ZS:
-            return
         own_copy(part).wait()
 
         def add(span):
@@ -1364,16 +1420,18 @@
             theirs[part, span, :] = value.astype(BF16)
 
         by_rows(mine.shape[1], add)
-        z_copy(part).start()
+        sum_copy(part).start()
 
     def between(index):
         gather_steps([gather], index)
         for part, at in enumerate((2, 3, 5, 6, 8, 9)):
             pl.when(index == at)(functools.partial(pass_grads, part))
 
+    for copy in weight_loads:
+        copy.start()
+    for part in range(2 * ZS):
+        own_copy(part).start()
     place.enter(True)
-    for turn in range(ZS):
-        own_copy(turn).start()
     for part in range(2):
         y_copy(part).start()
     begin_gathers([gather])
@@ -1396,24 +1454,32 @@
         copy.wait()
     gather.drain(True)
     reduce.drain()
-    for turn in range(ZS):
-        z_copy(turn).wait()
-
-
-def mlp_kernel(normed, gate_weight, up_weight, down, select, select_back, gates, middle, cotangent, gain, *refs):
+    for part in range(2 * ZS):
+        sum_copy(part).wait()
+
+
+def mlp_kernel(
+    normed, gate_up_part, down_part, select, select_back, gates, cotangents, middle, cotangent, gain, *refs
+):
     refs = list(refs)
     own_out, grad_out, terms_out, rows_out, up_grad_out, hidden_out, down_grad_out, result_out = [
         refs.pop(0) for _ in range(8)
     ]
-    everyone, upstreams = [refs.pop(0) for _ in range(2)]
+    everyone = refs.pop(0)
     place = Place()
-    gathers = [Gather(place, normed, everyone, refs), Gather(place, cotangent, upstreams, refs)]
+    gathers = [Gather(place, normed, everyone, refs)]
     reduce = PieceReduce(place, refs)
     arrived, upstream, rows, down_grad, hidden, both_grad, result = [refs.pop(0) for _ in range(7)]
-    load, store = [refs.pop(0) for _ in range(2)]
+    gate_weight, up_weight, down, load, store, weight_load = [refs.pop(0) for _ in range(6)]
     width = down.shape[0]
     model = middle.shape[2]
     tile = model // 2
+    weight_loads = [
+        pltpu.make_async_copy(source, target, weight_load.at[i])
+        for i, (source, target) in enumerate(
+            ((gate_up_part.at[0], gate_weight), (gate_up_part.at[1], up_weight), (down_part, down))
+        )
+    ]
 
     def stores(index):
         pairs = (
@@ -1434,12 +1500,17 @@
         sequence = m * ZS + k
         loads = [
             pltpu.make_async_copy(source.at[m, k, dc, dx], target.at[dc, dx], load.at[i, dc, dx])
-            for i, (source, target) in enumerate(((everyone, arrived), (upstreams, upstream)))
+            for i, (source, target) in enumerate(((everyone, arrived), (cotangents, upstream)))
             for dc in range(CS)
             for dx in range(XS)
         ]
         for copy in loads:
             copy.start()
+
+        @pl.when(index == 0)
+        def _():
+            for copy in weight_loads:
+                copy.wait()
 
         @pl.when(index > 0)
         def _():
@@ -1480,6 +1551,8 @@
         for copy in stores(sequence):
             copy.start()
 
+    for copy in weight_loads:
+        copy.start()
     place.enter(False)
     begin_gathers(gathers)
     run_pieces(place, reduce, piece, functools.partial(gather_steps, gathers))
@@ -1504,16 +1577,14 @@
 
 
 class Halves:
-    def __init__(self, own, other, copies):
-        self.own, self.other, self.copies = own, other, copies
+    def __init__(self, own, other, copy):
+        self.own, self.other, self.copy = own, other, copy
 
     def begin(self):
-        for copy in self.copies:
-            copy.start()
+        self.copy.start()
 
     def add(self):
-        for copy in self.copies:
-            copy.wait()
+        self.copy.wait()
 
         def body(index, carry):
             value = self.own[index].astype(F32) + self.other[index].astype(F32)
@@ -1523,40 +1594,34 @@
         lax.fori_loop(0, self.other.shape[0], body, 0)
 
 
-def last_kernel(part, middle, first_terms, second_terms, query_grad, kv_grad, out_grad, *refs):
+def last_kernel(part, middle, first_terms, second_terms, rows, grads, attended, row_grads, up_grad, *refs):
     refs = list(refs)
-    output, gains_out, query_out, kv_out, out_out = [refs.pop(0) for _ in range(5)]
+    output, gains_out, query_out, kv_out, out_out, up_out = [refs.pop(0) for _ in range(6)]
     place = Place()
     reduce = Reduce(place, part, refs)
-    query_own, query_in, kv_own, core_in, x_in, y_in = [refs.pop(0) for _ in range(6)]
-    hop_send, hop_recv, hop_local, z_send, z_recv, z_local = [refs.pop(0) for _ in range(6)]
+    tall, long, load = [refs.pop(0) for _ in range(3)]
+    query_all, query_in, kv_all, core_in, x_in, y_in, out_own, out_send, out_in = [refs.pop(0) for _ in range(9)]
+    hop_send, hop_recv, z_send, z_recv, z_local = [refs.pop(0) for _ in range(5)]
     terms, gain_in, gain_send, gain_recv = [refs.pop(0) for _ in range(4)]
+    up_send, up_recv, up_local = [refs.pop(0) for _ in range(3)]
     wide, kv_rows = query_out.shape[1] // ZS, kv_out.shape[0]
+    model = tall.shape[1]
+    tile = model // ZS
 
     def swap(number, source, target, peer):
         return remote(source, target, hop_send.at[number], hop_recv.at[number], peer)
 
     query = Halves(
-        query_own,
-        query_in,
-        [
-            pltpu.make_async_copy(query_grad.at[:, place.y], query_own, hop_local.at[0]),
-            swap(0, query_grad.at[:, 1 - place.y], query_in, place.y_peer),
-        ],
+        query_all.at[:, place.y], query_in, swap(0, query_all.at[:, 1 - place.y], query_in, place.y_peer)
     )
     over_core = Halves(
-        kv_own,
-        core_in,
-        [
-            pltpu.make_async_copy(kv_grad.at[:, place.core], kv_own, hop_local.at[1]),
-            swap(1, kv_grad.at[:, 1 - place.core], core_in, place.core_peer),
-        ],
+        kv_all.at[:, place.core], core_in, swap(1, kv_all.at[:, 1 - place.core], core_in, place.core_peer)
     )
     by_x = core_in.reshape(ZS * YS, XS, kv_rows, 2 * wide)
-    over_x = Halves(by_x.at[:, place.x], x_in, [swap(2, by_x.at[:, 1 - place.x], x_in, place.x_peer)])
+    over_x = Halves(by_x.at[:, place.x], x_in, swap(2, by_x.at[:, 1 - place.x], x_in, place.x_peer))
     by_y = x_in.reshape(ZS, YS, kv_rows, 2 * wide)
-    over_y = Halves(by_y.at[:, place.y], y_in, [swap(3, by_y.at[:, 1 - place.y], y_in, place.y_peer)])
-    over_out = swap(4, out_grad.at[1 - place.y], out_out, place.y_peer)
+    over_y = Halves(by_y.at[:, place.y], y_in, swap(3, by_y.at[:, 1 - place.y], y_in, place.y_peer))
+    over_out = swap(4, out_send, out_in, place.y_peer)
 
     def lanes(start):
         return pl.ds(pl.multiple_of(start, HDIM), wide)
@@ -1576,49 +1641,104 @@
             return pltpu.make_async_copy(source, target, z_local.at[piece])
         return remote(source, target, z_send.at[step, piece], z_recv.at[step, piece], place.z_peers[step])
 
-    def add_gains(number, peers):
-        copies = [
-            remote(terms, gain_in.at[number + i], gain_send.at[number + i], gain_recv.at[number + i], peer)
-            for i, peer in enumerate(peers)
+    hops = [[place.core_peer], [place.x_peer], [place.y_peer], place.z_peers[1:]]
+
+    def gain_copies(hop):
+        return [
+            remote(terms, gain_in.at[hop + i], gain_send.at[hop + i], gain_recv.at[hop + i], peer)
+            for i, peer in enumerate(hops[hop])
         ]
-        for copy in copies:
+
+    def send_gains(hop):
+        for copy in gain_copies(hop):
             copy.start()
+
+    def add_gains(hop):
+        copies = gain_copies(hop)
         for copy in copies:
             copy.wait()
-        for i in range(len(peers)):
-            terms[...] += gain_in[number + i]
-
+        for i in range(len(copies)):
+            terms[...] += gain_in[hop + i]
+        if hop + 1 < len(hops):
+            send_gains(hop + 1)
+
+    width = up_grad.shape[2]
+    columns = up_out.at[:, pl.ds(pl.multiple_of(place.z * width, HDIM), width)]
+    up_copies = [pltpu.make_async_copy(up_grad.at[place.z], columns, up_local)]
+    for step in (1, 3, 2):
+        source = up_grad.at[lax.rem(place.z + step, ZS)]
+        up_copies.append(remote(source, columns, up_send.at[step], up_recv.at[step], place.z_peers[step]))
+    loads = [pltpu.make_async_copy(rows, tall, load.at[0]), pltpu.make_async_copy(grads, long, load.at[1])]
+    later_loads = [
+        pltpu.make_async_copy(row_grads, tall, load.at[2]),
+        pltpu.make_async_copy(attended, long.at[:, pl.ds(0, wide)], load.at[3]),
+    ]
+
+    def small_grads(z):
+        span = slice(z * tile, (z + 1) * tile)
+        value = dot_l(tall[:, span], long[:, :wide]).astype(BF16)
+        query_all[z] = value.reshape(query_all.shape[1:])
+        blocks = kv_all.shape[0] // ZS
+        for kind in range(2):
+            value = dot_l(tall[:, span], long[:, (kind + 1) * wide : (kind + 2) * wide]).astype(BF16)
+            kv_all[z * blocks : (z + 1) * blocks, :, :, kind * wide : (kind + 1) * wide] = value.reshape(
+                (blocks,) + kv_all.shape[1:3] + (wide,)
+            )
+
+    def out_grads():
+        out_rows = out_own.shape[0]
+        for start in range(0, model, model // 2):
+            span = slice(start, start + model // 2)
+            value = dot_l(long[:, :wide], tall[:, span])
+            first, second = value[:out_rows], value[out_rows:]
+            out_own[:, span] = jnp.where(place.y == 0, first, second)
+            out_send[:, span] = jnp.where(place.y == 0, second, first).astype(BF16)
+
+    for copy in loads:
+        copy.start()
     place.enter(True)
-    over_core.begin()
-    query.begin()
     reduce.begin()
+    for copy in up_copies:
+        copy.start()
     terms[...] = jnp.zeros_like(terms)
     terms[0:1, :] = jnp.sum(first_terms[...], axis=0, keepdims=True)
     terms[1:2, :] = jnp.sum(second_terms[...], axis=0, keepdims=True)
+    send_gains(0)
+    for copy in loads:
+        copy.wait()
+    small_grads(0)
+    reduce.pass_x(0)
+    for z in range(1, ZS):
+        small_grads(z)
+    for copy in later_loads:
+        copy.start()
+    over_core.begin()
+    query.begin()
+    add_gains(0)
     over_core.add()
     over_x.begin()
-    add_gains(0, [place.core_peer])
-    reduce.pass_x(0)
+    for m in range(1, reduce.micro):
+        reduce.pass_x(m)
+    add_gains(1)
+    for copy in later_loads:
+        copy.wait()
+    out_grads()
+    over_out.start()
+    reduce.sums(0)
+    over_x.add()
+    over_y.begin()
     query.add()
     for step in (1, 3, 2, 0):
         z_copy(step, 0).start()
-    over_out.start()
-    add_gains(1, [place.x_peer])
-    over_x.add()
-    over_y.begin()
+    add_gains(2)
     for m in range(1, reduce.micro):
-        reduce.pass_x(m)
-    add_gains(2, [place.y_peer])
-    reduce.sums(0)
+        reduce.sums(m)
     over_y.add()
     for step in (1, 3, 2, 0):
         for piece in (1, 2):
             z_copy(step, piece).start()
-    add_gains(3, place.z_peers[1:])
+    add_gains(3)
     gains_out[...] = terms[...]
-    for m in range(1, reduce.micro):
-        reduce.sums(m)
-    reduce.end_chain()
     for m in range(reduce.micro):
         reduce.finish(m)
 
@@ -1626,11 +1746,121 @@
             output[m, span, :] = (middle[m, span, :] + reduce.total[m, span, :]).astype(BF16)
 
         by_rows(reduce.rows, finish)
+    over_out.wait()
+
+    def add_out(span):
+        out_out[span, :] = out_own[span, :] + out_in[span, :].astype(F32)
+
+    by_rows(out_own.shape[0], add_out)
     reduce.drain()
-    over_out.wait()
+    for copy in up_copies:
+        copy.wait()
     for step in range(ZS):
         for piece in range(3):
             z_copy(step, piece).wait()
+
+
+def gate_up_grads_kernel(rows, both_grad, gate_out, up_out):
+    value = dot_l(rows[...], both_grad[...]).astype(BF16)
+    width = both_grad.shape[1] // 2
+    gate_out[0] = value[:, :width].reshape(gate_out.shape[1:])
+    up_out[0] = value[:, width:].reshape(up_out.shape[1:])
+
+
+def gate_up_grads(rows, both_grad, model_rows):
+    count, model = rows.shape
+    width = both_grad.shape[1] // 2
+    block = pl.BlockSpec((1, YS, model_rows, width), lambda z: (z, 0, 0, 0))
+    return pl.pallas_call(
+        gate_up_grads_kernel,
+        grid=(ZS,),
+        in_specs=[
+            pl.BlockSpec((count, model // ZS), lambda z: (0, z)),
+            pl.BlockSpec((count, 2 * width), lambda z: (0, 0)),
+        ],
+        out_specs=[block, block],
+        out_shape=[jax.ShapeDtypeStruct((ZS, YS, model_rows, width), BF16)] * 2,
+        compiler_params=pltpu.CompilerParams(vmem_limit_bytes=60 << 20),
+        cost_estimate=pl.CostEstimate(
+            flops=4 * count * model * width, bytes_accessed=12 * model * width, transcendentals=0
+        ),
+    )(rows, both_grad)
+
+
+def down_grads_kernel(hidden, down_grad, down_out, small_out):
+    value = dot_l(hidden[...], down_grad[...])
+    down_out[...] = value
+    small_out[...] = value.astype(BF16)
+
+
+def down_grads(hidden, down_grad):
+    count, model = down_grad.shape
+    width = hidden.shape[1]
+    tile = model // ZS
+    return pl.pallas_call(
+        down_grads_kernel,
+        grid=(ZS,),
+        in_specs=[
+            pl.BlockSpec((count, width), lambda z: (0, 0)),
+            pl.BlockSpec((count, tile), lambda z: (0, z)),
+        ],
+        out_specs=[pl.BlockSpec((width, tile), lambda z: (0, z))] * 2,
+        out_shape=[jax.ShapeDtypeStruct((width, model), F32), jax.ShapeDtypeStruct((width, model), BF16)],
+        compiler_params=pltpu.CompilerParams(vmem_limit_bytes=60 << 20),
+        cost_estimate=pl.CostEstimate(
+            flops=2 * count * model * width, bytes_accessed=10 * model * width, transcendentals=0
+        ),
+    )(hidden, down_grad)
+
+
+def widen_kernel(first, second, own, other, kv, query, weight_out, down_out, kv_out, query_out):
+    step = pl.program_id(0)
+    pl.when(step < ZS)(lambda: weight_out.__setitem__(..., first[...].astype(F32)))
+    pl.when(step >= ZS)(lambda: weight_out.__setitem__(..., second[...].astype(F32)))
+    down_out[...] = own[0] + other[...].astype(F32)
+    kv_out[...] = kv[...].astype(F32)
+    query_out[...] = query[...].astype(F32)
+
+
+def widen(first, second, own, other, kv, query, y):
+    steps = 2 * ZS
+    rows, width = first.shape[0], first.shape[1] // ZS
+    down_rows, model = other.shape
+    down_step = down_rows // ZS
+
+    def block(*dims):
+        return pl.BlockSpec(dims, lambda i, y: (i // 2,) + (0,) * (len(dims) - 1))
+
+    small = [(value.shape[0] // ZS, value.shape[1]) for value in (kv, query)]
+    return pl.pallas_call(
+        lambda y, *refs: widen_kernel(*refs),
+        grid_spec=pltpu.PrefetchScalarGridSpec(
+            num_scalar_prefetch=1,
+            grid=(steps,),
+            in_specs=[
+                pl.BlockSpec((rows, width), lambda i, y: (0, jnp.minimum(i, ZS - 1))),
+                pl.BlockSpec((rows, width), lambda i, y: (0, jnp.maximum(i - ZS, 0))),
+                pl.BlockSpec((1, down_step, model), lambda i, y: (y[0], i // 2, 0)),
+                block(down_step, model),
+                block(*small[0]),
+                block(*small[1]),
+            ],
+            out_specs=[
+                pl.BlockSpec((rows, width), lambda i, y: (0, i)),
+                block(down_step, model),
+                block(*small[0]),
+                block(*small[1]),
+            ],
+        ),
+        out_shape=[
+            jax.ShapeDtypeStruct((rows, steps * width), F32),
+            jax.ShapeDtypeStruct(other.shape, F32),
+            jax.ShapeDtypeStruct(kv.shape, F32),
+            jax.ShapeDtypeStruct(query.shape, F32),
+        ],
+        compiler_params=pltpu.CompilerParams(vmem_limit_bytes=60 << 20),
+        cost_estimate=pl.CostEstimate(flops=0, bytes_accessed=12 * rows * steps * width, transcendentals=0),
+    )(jnp.full((1,), y, jnp.int32), first, second, own, other, kv, query)
 
 
 def connect(kernel, operands, spaces, out_shapes, out_spaces, scratch, number, seconds):
@@ -1677,10 +1907,10 @@
 
     lines = []
     for m in range(micro):
-        lines += [own_rows(att_routes[m]).T, att_gates[m].T, own_rows(mlp_routes[m]).T, mlp_gates[m].T]
-        lines += [own_rows(blocks[m, 0][:, None]).T]
-    table = jnp.concatenate(lines, axis=0)
-    table = jnp.pad(table, ((0, -table.shape[0] % 8), (0, -local % HDIM)))[None]
+        lines += [own_rows(att_routes[m]), att_gates[m], own_rows(mlp_routes[m]), mlp_gates[m]]
+        lines += [own_rows(blocks[m, 0][:, None])]
+    table = jnp.concatenate(lines, axis=1)
+    table = jnp.pad(table, ((0, 0), (0, -table.shape[1] % HDIM)))[None]
 
     positions = (
         (x ^ jnp.arange(XS)[None, :, None]) * CS + (core ^ jnp.arange(CS)[:, None, None])
@@ -1698,37 +1928,86 @@
     gathered = jax.ShapeDtypeStruct(everyone, BF16)
     terms = jax.ShapeDtypeStruct((STEP, model), F32)
     own_buffer = pltpu.VMEM(shape, BF16)
-    gate_weight = jax.ShapeDtypeStruct((model, hidden_width), BF16)
-    normed, table, qkv_weight, out_weight, gate_weight = connect(
-        functools.partial(start_kernel, (wide, kv_rows, model_rows, w_out.shape[1])),
-        [tokens, first_gain, table, w_kv, w_query, w_out, w_gate_up],
-        [VMEM, VMEM, VMEM, ANY, ANY, ANY, ANY],
+
+    def kept(width, rows=SEQ):
+        return jax.ShapeDtypeStruct((seqs, rows, width), BF16)
+
+    def weight(*dims):
+        return jax.ShapeDtypeStruct(dims, BF16)
+
+    marks = (ZS, CS, XS) + table.shape[1:]
+    (
+        normed_two,
+        middle,
+        normed,
+        cotangents,
+        table,
+        turned_qkv,
+        attended,
+        qkv_weight,
+        out_weight,
+        gate_up_weight,
+        down_weight,
+    ) = connect(
+        functools.partial(attention_kernel, (wide, kv_rows, model_rows, w_out.shape[1], w_down.shape[1])),
         [
+            tokens,
+            cotangent,
+            first_gain,
+            second_gain,
+            table,
+            cosine,
+            sine,
+            w_kv,
+            w_query,
+            w_out,
+            w_gate_up,
+            w_down,
+        ],
+        [VMEM] * 7 + [ANY] * 5,
+        [
+            short,
+            tall,
             gathered,
-            jax.ShapeDtypeStruct((1, ZS, CS, XS) + table.shape[1:], F32),
-            jax.ShapeDtypeStruct((model, 3 * wide), BF16),
-            jax.ShapeDtypeStruct((wide, model), BF16),
-            gate_weight,
+            gathered,
+            jax.ShapeDtypeStruct((1,) + marks, F32),
+            kept(3 * wide),
+            kept(wide),
+            weight(model, 3 * wide),
+            weight(wide, model),
+            weight(2, model, hidden_width),
+            weight(hidden_width, model),
         ],
-        [ANY] * 5,
+        [VMEM, VMEM] + [ANY] * 9,
         [own_buffer]
         + Gather.scratch(micro)
+        + Gather.scratch(micro)
         + Gather.scratch(1)
+        + PieceReduce.scratch(*shape)
         + Spread.scratch(2, 3)
         + Spread.scratch(1, 1)
+        + Spread.scratch(2, 1)
         + Share.scratch(1)
-        + Spread.scratch(1, 1),
+        + Share.scratch(1)
+        + [
+            pltpu.VMEM((CS, XS, local, model), BF16),
+            pltpu.VMEM((SEQ, 3 * wide), BF16),
+            pltpu.VMEM((SEQ, wide), BF16),
+            pltpu.VMEM(marks, F32),
+            pltpu.VMEM((model, 3 * wide), BF16),
+            pltpu.VMEM((wide, model), BF16),
+            DMA((CS, XS)),
+            DMA((2,)),
+            DMA((3,)),
+        ],
         1,
-        130e-6,
-    )
-
-    part = table[0, ..., : 9 * micro, :local].reshape(ZS, CS, XS, micro, 9, local)
-    part = part.transpose(3, 0, 1, 2, 5, 4).reshape(seqs, SEQ, 9)
-    att_weight = jnp.sum(jnp.where(part[..., 0:2] == owner, part[..., 2:4], 0.0), axis=-1)[..., None]
+        250e-6,
+    )
+    table = table[0]
+    part = table[..., : KINDS * micro].reshape(ZS, SEQ, micro, KINDS).transpose(2, 0, 1, 3)
+    part = part.reshape(seqs, SEQ, KINDS)
     hit = jnp.any(part[..., 4:6] == owner, axis=-1)
     mlp_weight = jnp.sum(jnp.where(part[..., 4:6] == owner, part[..., 6:8], 0.0), axis=-1)
-    seq_blocks = part[..., 8].astype(jnp.int32)
-    tables = [cosine, sine, seq_blocks[:, :, None], seq_blocks[:, None, :]]
     before_mask = jnp.arange(SEQ)[:, None] < jnp.arange(SEQ)[None, :]
     before = dot(hit.astype(BF16), before_mask.astype(BF16)).astype(jnp.int32)
     slots = jnp.arange(XS * CS * CAP + -XS * CS * CAP % STEP)
@@ -1736,62 +2015,21 @@
     row_gate = jnp.sum(jnp.where(chosen, mlp_weight[:, None, :], 0.0), axis=2)
     select = chosen.astype(BF16)
     slot_count = select.shape[1]
-
-    def kept(width, rows=SEQ):
-        return jax.ShapeDtypeStruct((seqs, rows, width), BF16)
-
-    normed_two, middle, turned_qkv, attended, up_weight, down_weight = connect(
-        functools.partial(attend_kernel, (model_rows, w_down.shape[1])),
-        [
-            normed.reshape(seqs, SEQ, model),
-            qkv_weight,
-            out_weight,
-            att_weight,
-            *tables,
-            tokens,
-            second_gain,
-            w_gate_up,
-            w_down,
-        ],
-        [ANY] + [VMEM] * 9 + [ANY] * 2,
-        [
-            short,
-            tall,
-            kept(3 * wide),
-            kept(wide),
-            jax.ShapeDtypeStruct(gate_weight.shape, BF16),
-            jax.ShapeDtypeStruct((hidden_width, model), BF16),
-        ],
-        [VMEM, VMEM] + [ANY] * 4,
-        PieceReduce.scratch(*shape)
-        + Spread.scratch(1, 1)
-        + Share.scratch(1)
-        + [
-            pltpu.VMEM((SEQ, model), BF16),
-            pltpu.VMEM((SEQ, 3 * wide), BF16),
-            pltpu.VMEM((SEQ, wide), BF16),
-            DMA,
-            DMA((2,)),
-        ],
-        2,
-        130e-6,
-    )
-
     middle_rows, middle_grad, gain_second, rows_two, both_grad, hidden, down_grad, result_two, *_ = connect(
         mlp_kernel,
         [
             normed_two,
-            gate_weight,
-            up_weight,
+            gate_up_weight,
             down_weight,
             select,
             select.transpose(0, 2, 1),
             row_gate[:, :, None],
+            cotangents,
             middle,
             cotangent,
             second_gain,
         ],
-        [VMEM] * 10,
+        [VMEM] + [ANY] * 2 + [VMEM] * 3 + [ANY] + [VMEM] * 3,
         [
             short,
             tall,
@@ -1802,11 +2040,9 @@
             kept(model, slot_count),
             kept(model),
             gathered,
-            gathered,
         ],
-        [VMEM, VMEM, VMEM] + [ANY] * 7,
+        [VMEM, VMEM, VMEM] + [ANY] * 6,
         Gather.scratch(micro)
-        + Gather.scratch(micro)
         + PieceReduce.scratch(*shape)
         + [
             pltpu.VMEM((CS, XS, local, model), BF16),
@@ -1816,8 +2052,12 @@
             pltpu.VMEM((slot_count, hidden_width), BF16),
             pltpu.VMEM((slot_count, 2 * hidden_width), BF16),
             pltpu.VMEM((SEQ, model), BF16),
+            pltpu.VMEM((model, hidden_width), BF16),
+            pltpu.VMEM((model, hidden_width), BF16),
+            pltpu.VMEM((hidden_width, model), BF16),
             DMA((2, CS, XS)),
             DMA((5,)),
+            DMA((3,)),
         ],
         5,
         150e-6,
@@ -1827,21 +2067,20 @@
     ]
     result_two = result_two.reshape(everyone)
 
-    def by_y(value):
-        return value.astype(BF16).reshape(ZS, YS, model_rows, hidden_width)
-
-    gate_grad = by_y(dot_l(rows_two, both_grad[:, :hidden_width]))
-    up_grad = by_y(dot_l(rows_two, both_grad[:, hidden_width:]))
-    grad_down = dot_l(hidden, down_grad).reshape(YS, -1, model)
-    down_other = y_move(take(grad_down, 1 - y, 0).astype(BF16))
-    input_grad, gain_first, result_grad, qkv_grad, gate_grad, up_other, _ = connect(
+    grad_down, down_small = [value.reshape(YS, -1, model) for value in down_grads(hidden, down_grad)]
+    down_small = take(down_small, 1 - y, 0)
+    rows_two, down_small = lax.optimization_barrier((rows_two, down_small))
+    down_small = y_move(down_small)
+    gate_grad, up_grad = gate_up_grads(rows_two, both_grad, model_rows)
+    input_grad, gain_first, result_grad, qkv_grad, gate_grad, up_grad, _ = connect(
         attend_back_kernel,
         [
             middle_rows,
             qkv_weight,
             out_weight,
-            att_weight,
-            *tables,
+            table,
+            cosine,
+            sine,
             turned_qkv,
             tokens,
             middle_grad,
@@ -1849,7 +2088,7 @@
             gate_grad,
             up_grad,
         ],
-        [VMEM] * 8 + [ANY] + [VMEM] * 3 + [ANY] * 2,
+        [VMEM] + [ANY] * 2 + [VMEM] * 3 + [ANY] + [VMEM] * 3 + [ANY] * 2,
         [
             short,
             terms,
@@ -1869,67 +2108,76 @@
             pltpu.VMEM((SEQ, 3 * wide), BF16),
             DMA((CS + 1, XS)),
             DMA((2,)),
-            pltpu.VMEM((ZS, model_rows, hidden_width), BF16),
-            pltpu.VMEM((ZS, model_rows, hidden_width), BF16),
-            DMA((ZS,)),
+            pltpu.VMEM((2 * ZS, model_rows, hidden_width), BF16),
+            pltpu.VMEM((2 * ZS, model_rows, hidden_width), BF16),
+            DMA((2 * ZS,)),
             DMA((2 * ZS,)),
             DMA((2 * ZS,)),
             DMA((ZS,)),
             DMA((ZS,)),
-            DMA,
+            DMA((2 * ZS,)),
+            pltpu.VMEM((model, 3 * wide), BF16),
+            pltpu.VMEM((wide, model), BF16),
+            DMA((2,)),
         ],
         3,
         150e-6,
     )
-    up_grad = (take(up_grad, y, 1).astype(F32) + up_other.astype(F32)).astype(BF16)
-    up_grad = z_exchange(up_grad)
-    result_grad, qkv_grad, attended, normed = [
-        value.reshape(-1, value.shape[-1]) for value in (result_grad, qkv_grad, attended, normed)
-    ]
-    grad_out = dot_l(attended, result_grad).reshape(YS, -1, model)
-    query_grad = dot_l(normed, qkv_grad[:, :wide]).astype(BF16).reshape(ZS, YS, model_rows, wide)
-    kv_grad = dot_l(normed, qkv_grad[:, wide:]).astype(BF16).reshape(-1, CS, kv_rows, 2 * wide)
-    output, gains, query_grad, kv_grad, out_other = connect(
+    rows = seqs * SEQ
+    output, gains, query_grad, kv_grad, grad_out, up_grad = connect(
         last_kernel,
         [
             result_two,
             middle,
             gain_first,
             gain_second,
-            query_grad,
-            kv_grad,
-            grad_out.astype(BF16),
+            normed.reshape(rows, model),
+            qkv_grad.reshape(rows, 3 * wide),
+            attended.reshape(rows, wide),
+            result_grad.reshape(rows, model),
+            up_grad,
         ],
-        [ANY, VMEM, VMEM, VMEM] + [ANY] * 3,
+        [ANY, VMEM, VMEM, VMEM] + [ANY] * 5,
         [
             short,
             jax.ShapeDtypeStruct((8, model), F32),
             jax.ShapeDtypeStruct((model_rows, ZS * wide), BF16),
             jax.ShapeDtypeStruct((kv_rows, 2 * ZS * wide), BF16),
-            jax.ShapeDtypeStruct(w_out.shape[1:], BF16),
+            jax.ShapeDtypeStruct(w_out.shape[1:], F32),
+            weight(model_rows, ZS * hidden_width),
         ],
-        [VMEM, VMEM] + [ANY] * 3,
+        [VMEM, VMEM, ANY, ANY, VMEM, ANY],
         Reduce.scratch(*shape)
-        + [pltpu.VMEM((ZS, model_rows, wide), BF16) for _ in range(2)]
-        + [pltpu.VMEM((ZS * YS * XS, kv_rows, 2 * wide), BF16) for _ in range(2)]
-        + [pltpu.VMEM((ZS * YS, kv_rows, 2 * wide), BF16), pltpu.VMEM((ZS, kv_rows, 2 * wide), BF16)]
-        + [DMA((6,)), DMA((6,)), DMA((2,)), DMA((ZS, 3)), DMA((ZS, 3)), DMA((3,))]
-        + [pltpu.VMEM((8, model), F32), pltpu.VMEM((6, 8, model), F32), DMA((6,)), DMA((6,))],
+        + [pltpu.VMEM((rows, model), BF16), pltpu.VMEM((rows, 3 * wide), BF16), DMA((4,))]
+        + [pltpu.VMEM((ZS, YS, model_rows, wide), BF16), pltpu.VMEM((ZS, model_rows, wide), BF16)]
+        + [
+            pltpu.VMEM((ZS * YS * XS, CS, kv_rows, 2 * wide), BF16),
+            pltpu.VMEM((ZS * YS * XS, kv_rows, 2 * wide), BF16),
+            pltpu.VMEM((ZS * YS, kv_rows, 2 * wide), BF16),
+            pltpu.VMEM((ZS, kv_rows, 2 * wide), BF16),
+        ]
+        + [pltpu.VMEM(w_out.shape[1:], kind) for kind in (F32, BF16, BF16)]
+        + [DMA((5,)), DMA((5,)), DMA((ZS, 3)), DMA((ZS, 3)), DMA((3,))]
+        + [pltpu.VMEM((8, model), F32), pltpu.VMEM((6, 8, model), F32), DMA((6,)), DMA((6,))]
+        + [DMA((ZS,)), DMA((ZS,)), DMA],
         4,
-        90e-6,
+        100e-6,
     )
     devices = ZS * YS * XS * CS
     gains = take(gains[:2].reshape(2, devices, model // devices), group * XS * CS + owner, 1)
+    grad_gate_up, grad_down, kv_grad, query_grad = widen(
+        gate_grad, up_grad, grad_down, down_small, kv_grad, query_grad, y
+    )
     return (
         output,
         input_grad,
         gains[0],
         gains[1],
-        kv_grad.astype(F32),
-        query_grad.astype(F32)[None],
-        (take(grad_out, y, 0) + out_other.astype(F32))[None],
-        jnp.concatenate([gate_grad.astype(F32)] + [up_grad[z].astype(F32) for z in range(ZS)], axis=1)[None],
-        (take(grad_down, y, 0) + down_other.astype(F32))[None],
+        kv_grad,
+        query_grad[None],
+        grad_out[None],
+        grad_gate_up[None],
+        grad_down[None],
     )
 
 

time: 1050 us -> 923 us (0.88)
  matrix products: 88.4 us -> 0.12 us
  other arithmetic: 37.4 us -> 7.03 us
  Pallas kernels: 873 us -> 891 us
  local copies, waits for them, and re-layouts: 34.7 us -> 17.9 us
    dot_general x6 -> x0, matrix products: 88.3 us -> none  [dot_l(): lax.dot_general(left, right, (((0,), (0,)), ((), ())), preferred_element_...]
    pallas_call x0 -> x3, Pallas kernels: none -> 59.6 us  [the longest x1 27 us: gate_up_grads(): pl.pallas_call(gate_up_grads_kernel, grid=(ZS,), in_specs=[pl.BlockSpec((...]
    pallas_call x5 -> x4, Pallas kernels: 873 us -> 831 us  [connect(): pl.pallas_call(kernel, in_specs=spaces, out_specs=out_spaces, out_shape=o...]
    broadcast_in_dim x4 -> x0, other arithmetic: 22.5 us -> none  [the longest x1 8.53 us: fast_device(): jnp.concatenate([gate_grad.astype(F32)] + [up_grad[z].astype(F32) for z i...]
    dot_general x2 -> x0, local copies, waits for them, and re-layouts: 11.9 us -> none  [dot_l(): lax.dot_general(left, right, (((0,), (0,)), ((), ())), preferred_element_...]
  transfers between devices with their start and end apart: 2 -> 1, of which waited for: 0 -> 0; matrix products, arithmetic and copies ran while one was open for 10% -> 0% of each run, Pallas kernels for 29% -> 35%
where the time goes in v4:
time: 923 us; the launch traced here: 918 us
  Pallas kernels  891 us (97%)
  local copies, waits for them, and re-layouts  17.9 us (2%)
    pallas_call x4, Pallas kernels, connect(): pl.pallas_call(kernel, in_specs=spaces, out_specs=out_spaces, out_shape=o...  831 us
    pallas_call x1, Pallas kernels, gate_up_grads(): pl.pallas_call(gate_up_grads_kernel, grid=(ZS,), in_specs=[pl.BlockSpec((...  27 us
  transfers between devices with their start and end apart: 1, of which 0 were waited for; matrix products, arithmetic and copies ran while one was open for 0% of the time, Pallas kernels for 35%

profile of v4, /device:TPU:0, one launch (start us, length us, event | category | flops | bytes accessed | tf_op | source)
XLA Modules:
  0.0 917.5 jit_solution(1577300793074082551)
XLA Ops:
  0.7 0.1 add_multiply_fusion
  0.8 0.1 add_convert_fusion
  0.8 0.1 convert_element_type.91
  0.9 0.7 fusion.4
  1.6 0.8 pad_maximum_fusion.cosine
  2.4 0.7 fusion.20
  3.1 0.7 fusion.22
  3.8 0.7 fusion.21
  4.5 0.1 fusion.9
  4.6 0.1 fusion.15
  4.6 0.1 fusion.7
  4.7 0.7 slice_bitcast_fusion
  5.4 0.1 concatenate.9
  5.6 0.1 copy.46
  5.7 0.6 pad_bitcast_fusion.table
  6.3 0.8 pad_maximum_fusion.1.sine
  7.1 351.5 %shard_map.205 = (bf16[2,80,2048]{2,1,0:T(8,128)(2,1)}, f32[2,80,2048]{2,1,0:T(8,128)}, bf16[2,4,2,2,80,2048]{5,4,3,2,1,0:T(8,128)(2,1)}, bf16[2,4,2,2,80,2048]{...) custom-call(bf16[2,80,2048]{2,1,0:T(8,128)(2,1)} %tokens.3, ...), custom_call_target="tpu_custom_call" | custom-call | bytes 750000000 | tf_op jit(solution)/shard_map/pallas_call | solution.py:1867
  358.6 1.4 copy.47
  360.0 0.2 reshape.170
  360.3 0.1 convolution_convert_fusion
  360.4 2.2 fusion.1.select_back
  362.6 1.6 fusion.3.select
  364.2 0.6 select_reduce_fusion
  364.8 1.2 copy.49.gates
  366.1 183.2 %shard_map.206 = (bf16[2,80,2048]{2,1,0:T(8,128)(2,1)}, f32[2,80,2048]{2,1,0:T(8,128)}, f32[16,2048]{1,0:T(8,128)}, bf16[8,208,2048]{2,1,0:T(8,128)(2,1)}, bf16[...) custom-call(bf16[2,80,2048]{2,1,0:T(8,128)(2,1)} %get-tuple-element., ...), custom_call_target="tpu_custom_call" | custom-call | bytes 450000000 | tf_op jit(solution)/shard_map/pallas_call | solution.py:1867
  549.2 16.2 %shard_map.207 = (f32[1408,2048]{1,0:T(8,128)}, bf16[1408,2048]{1,0:T(8,128)(2,1)}) custom-call(bf16[1664,1408]{1,0:T(8,128)(2,1)} %bitcast.76, bf16[1664,2048]{1,0:T(8,128)(2,1)} %bitcast.74), custom_call_target="tpu_custom_call" | custom-call | flops 9596567552 | bytes 28835840 | tf_op jit(solution)/shard_map/pallas_call | solution.py:1800
  565.5 3.9 dynamic-slice_bitcast_fusion
  569.4 0.5 collective-permute-start
  569.9 27.0 %shard_map.208 = (bf16[4,2,256,1408]{3,2,1,0:T(8,128)(2,1)}, bf16[4,2,256,1408]{3,2,1,0:T(8,128)(2,1)}) custom-call(bf16[1664,2048]{1,0:T(8,128)(2,1)} %bitcast.73, bf16[1664,2816]{1,0:T(8,128)(2,1)} %bitcast.72), custom_call_target="tpu_custom_call" | custom-call | flops 19193135104 | bytes 34603008 | tf_op jit(solution)/shard_map/pallas_call | solution.py:1774
  596.9 159.6 %shard_map.209 = (bf16[2,80,2048]{2,1,0:T(8,128)(2,1)}, f32[16,2048]{1,0:T(8,128)}, bf16[8,320,2048]{2,1,0:T(8,128)(2,1)}, bf16[8,320,1536]{2,1,0:T(8,128)(2,1)}...) custom-call(bf16[2,80,2048]{2,1,0:T(8,128)(2,1)} %get-tuple-element.57.rows, ...), custom_call_target="tpu_custom_call" | custom-call | bytes 450000000 | tf_op jit(solution)/shard_map/pallas_call | solution.py:1867
  756.6 137.1 %shard_map.210 = (bf16[2,80,2048]{2,1,0:T(8,128)(2,1)}, f32[8,2048]{1,0:T(8,128)}, bf16[256,2048]{1,0:T(8,128)(2,1)}, bf16[64,4096]{1,0:T(8,128)(2,1)}, f32[256,2048]{1,0:T(8,128)}, /*index=5*/bf16[256,5632]{1,0:T(8,128)(2,1)}) custom-call(bf16[2,4,2,2,80,2048]{5,4,3,2,1,0:T(8,128)(2,1)} %bitcast.57, f32[2,80,2048]{2,1,0:T(8,128)} %get-tuple-element.55.middle, ...), custom_call_target="tpu_custom_call" | custom-call | bytes 300000000 | tf_op jit(solution)/shard_map/pallas_call | solution.py:1867
  893.7 0.8 slice.64
  894.6 0.1 reshape.182
  894.6 0.5 fusion.18
  895.2 0.0 collective-permute-done.refs_3_
  895.2 0.0 copy-start
  895.2 1.6 copy-done
  896.7 0.0 copy-start.2
  896.7 16.3 %shard_map.211 = (f32[256,11264]{1,0:T(8,128)}, f32[704,2048]{1,0:T(8,128)}, f32[64,4096]{1,0:T(8,128)}, f32[256,2048]{1,0:T(8,128)}) custom-call(s32[1]{0:T(128)} %bitcast.29.y, bf16[256,5632]{1,0:T(8,128)(2,1)} %get-tuple-element.80.refs_0_, bf16[256,5632]{1,0:T(8,128)(2,1)} %get-tuple-element.81.refs_1_, f32[2,704,2048]{2,1,0:T(8,128)} %bitcast.55, ...), custom_call_target="tpu_custom_call" | custom-call | bytes 34603008 | tf_op jit(solution)/shard_map/pallas_call | solution.py:1835
  913.0 0.0 copy-start.1
  913.0 2.1 copy.53
  915.2 0.0 copy-done.2
  915.2 0.8 copy.54
  916.0 0.0 copy-done.1
  916.0 1.3 copy.55
  (6 shorter events, 0.1 us)
Async XLA Ops:
  569.4 325.8 %collective-permute-start = (bf16[704,2048]{1,0:T(8,128)(2,1)}, bf16[704,2048]{1,0:T(8,128)(2,1)S(1)}, u32[]{:S(2)}, u32[]{:S(2)}) collective-permute-start(bf16[704,2048]{1,0:T(8,128)(2,1)} %dynamic-slice_bitcast_fusion), channel_id=1, source_target_pairs={{0,4},{4,0},{8,12},{12,8},{16,20},{20,16},{24,28},{28,24},{1,5},{5... | collective-permute-start | bytes 8650760 | tf_op jit(solution)/shard_map/ppermute | solution.py:396
  895.2 1.6 copy-start
  896.7 18.4 %copy-start.2 = (bf16[2,80,2048]{2,1,0:T(8,128)(2,1)S(1)}, bf16[2,80,2048]{2,1,0:T(8,128)(2,1)}, u32[]{:S(2)}) copy-start(bf16[2,80,2048]{2,1,0:T(8,128)(2,1)} %get-tuple-element.128) | copy-start | bytes 1966084
  913.0 3.0 copy-start.1

commit v5 on v4

--- a/solution.py
+++ b/solution.py
@@ -1000,17 +1000,9 @@
         for later in range(axis, self.depth):
             self.hop(later, index << (later - axis)).start()
 
-    def begin_slowly(self):
+    def send(self, step):
         for piece in range(self.pieces):
-            self.local(piece).start()
-            self.z_copy(1, piece).start()
-
-    def slow_round(self, turn):
-        steps = (0, 1, 3, 2)
-        self.z_round(steps[turn])
-        if 0 < turn < ZS - 1:
-            for piece in range(self.pieces):
-                self.z_copy(steps[turn + 1], piece).start()
+            (self.z_copy(step, piece) if step else self.local(piece)).start()
 
     def z_round(self, step):
         for piece in range(self.pieces):
@@ -1225,11 +1217,23 @@
             copy.start()
 
     def between(index):
-        for far in range(1, ZS):
-            pl.when(index == far - 1)(functools.partial(upstream.z_round, far))
-            pl.when(index == far)(functools.partial(upstream.x_round, far - 1))
-        pl.when(index == ZS)(functools.partial(upstream.x_round, ZS - 1))
-        pl.when(index == 4)(functools.partial(gate_up.slow_round, 2))
+        due = {
+            2: [lambda: gate_up.z_round(1)],
+            3: [lambda: gate_up.z_round(3)],
+            4: [lambda: upstream.send_own(0)],
+            5: [lambda: gate_up.z_round(2), lambda: upstream.send_own(1)],
+            6: [lambda: upstream.z_round(1)],
+            7: [lambda: upstream.x_round(0), lambda: upstream.z_round(2)],
+            8: [lambda: upstream.x_round(1), lambda: upstream.z_round(3)],
+            9: [lambda: upstream.x_round(2)],
+            10: [lambda: upstream.x_round(3)],
+        }
+        for at, tasks in due.items():
+
+            @pl.when(index == at)
+            def _(tasks=tasks):
+                for task in tasks:
+                    task()
 
     place.enter(True)
     shared.begin()
@@ -1252,8 +1256,9 @@
     for index in (0, 1, 3, 2):
         kv.hop_round(0, index)
     normed.x_round(0)
-    gate_up.begin_slowly()
-    gate_up.slow_round(0)
+    for step in (0, 1, 3, 2):
+        gate_up.send(step)
+    gate_up.z_round(0)
     tables.z_round(2)
     normed.z_round(2)
     normed.x_round(1)
@@ -1267,8 +1272,6 @@
         tables.x_round(far)
     normed.x_round(2)
     normed.x_round(3)
-    for m in range(upstream.micro):
-        upstream.send_own(m)
     for index in range(ZS << 2):
         kv.hop_round(2, index)
     for index in range(ZS):
@@ -1278,7 +1281,6 @@
     for copy in late_loads:
         copy.start()
     down.begin()
-    gate_up.slow_round(1)
     run_pieces(place, reduce, piece, between)
     for m in range(reduce.micro):
         reduce.finish(m)
@@ -1291,7 +1293,6 @@
         by_rows(reduce.rows, body)
     for copy in stores(0):
         copy.wait()
-    gate_up.slow_round(3)
     for index in range(ZS):
         gate_up.hop_round(0, index)
     for gather in (tables, normed):
@@ -1474,6 +1475,7 @@
     width = down.shape[0]
     model = middle.shape[2]
     tile = model // 2
+    pieces = reduce.micro * ZS
     weight_loads = [
         pltpu.make_async_copy(source, target, weight_load.at[i])
         for i, (source, target) in enumerate(
@@ -1481,16 +1483,23 @@
         )
     ]
 
-    def stores(index):
-        pairs = (
-            (rows, rows_out),
-            (down_grad, down_grad_out),
-            (hidden, hidden_out),
-            (both_grad, up_grad_out),
-            (result, result_out),
-        )
+    kept = (
+        (rows, rows_out),
+        (down_grad, down_grad_out),
+        (hidden, hidden_out),
+        (both_grad, up_grad_out),
+        (result, result_out),
+    )
+
+    def store_of(number, sequence):
+        here, there = kept[number]
+        return pltpu.make_async_copy(here, there.at[sequence], store.at[number])
+
+    def loads_of(number, source, target, m, k):
         return [
-            pltpu.make_async_copy(here, there.at[index], store.at[i]) for i, (here, there) in enumerate(pairs)
+            pltpu.make_async_copy(source.at[m, k, dc, dx], target.at[dc, dx], load.at[number, dc, dx])
+            for dc in range(CS)
+            for dx in range(XS)
         ]
 
     def piece(index, m, k):
@@ -1498,26 +1507,29 @@
             gather.piece_arrival(m, k)
             pl.when(k == 0)(functools.partial(wait_local, gather, m))
         sequence = m * ZS + k
-        loads = [
-            pltpu.make_async_copy(source.at[m, k, dc, dx], target.at[dc, dx], load.at[i, dc, dx])
-            for i, (source, target) in enumerate(((everyone, arrived), (cotangents, upstream)))
-            for dc in range(CS)
-            for dx in range(XS)
-        ]
+        loads = loads_of(0, everyone, arrived, m, k)
         for copy in loads:
             copy.start()
 
+        def stored(*numbers):
+            @pl.when(index > 0)
+            def _():
+                for number in numbers:
+                    store_of(number, 0).wait()
+
+        def store_out(*numbers):
+            for number in numbers:
+                store_of(number, sequence).start()
+
         @pl.when(index == 0)
         def _():
+            for copy in loads_of(1, cotangents, upstream, m, k):
+                copy.start()
             for copy in weight_loads:
                 copy.wait()
 
-        @pl.when(index > 0)
-        def _():
-            for copy in stores(0):
-                copy.wait()
-
-        for copy in loads:
+        stored(0, 1)
+        for copy in loads + loads_of(1, cotangents, upstream, m, k):
             copy.wait()
         chosen, back, gate_of_row = select[sequence], select_back[sequence], gates[sequence]
         length = select.shape[2]
@@ -1527,6 +1539,14 @@
             down_grad[:, span] = (dot(chosen, upstream[:, :, :, span].reshape(length, tile)) * gate_of_row).astype(BF16)
 
         by_lanes(model // tile, tile, to_rows)
+        store_out(0, 1)
+
+        @pl.when(index + 1 < pieces)
+        def _():
+            for copy in loads_of(1, cotangents, upstream, *piece_of(place, index + 1, reduce.micro)):
+                copy.start()
+
+        stored(2, 3)
 
         half = width // (2 * HDIM) * HDIM
         for start, stop in ((0, half), (half, width)):
@@ -1540,6 +1560,9 @@
             both_grad[:, start:stop] = (hidden_grad * up * slope).astype(BF16)
             both_grad[:, width + start : width + stop] = (hidden_grad * silu).astype(BF16)
 
+        store_out(2, 3)
+        stored(4)
+
         def to_tokens(span):
             row_grad = dot_t(both_grad[:, :width], gate_weight[span, :])
             row_grad = (row_grad + dot_t(both_grad[:, width:], up_weight[span, :])).astype(BF16)
@@ -1548,8 +1571,7 @@
             result[:, span] = dot(back, value).astype(BF16)
 
         by_lanes(model // tile, tile, to_tokens)
-        for copy in stores(sequence):
-            copy.start()
+        store_out(4)
 
     for copy in weight_loads:
         copy.start()
@@ -1569,8 +1591,8 @@
             terms_out[...] += terms
 
         by_rows(reduce.rows, body)
-    for copy in stores(0):
-        copy.wait()
+    for number in range(len(kept)):
+        store_of(number, 0).wait()
     for gather in gathers:
         gather.drain(True)
     reduce.drain()

time: 923 us -> 883 us (0.957)
  Pallas kernels: 891 us -> 850 us
    pallas_call x4, Pallas kernels: 831 us -> 790 us  [connect(): pl.pallas_call(kernel, in_specs=spaces, out_specs=out_spaces, out_shape=o...]
  transfers between devices with their start and end apart: 1 -> 1, of which waited for: 0 -> 0; matrix products, arithmetic and copies ran while one was open for 0% -> 0% of each run, Pallas kernels for 35% -> 37%
where the time goes in v5:
time: 883 us; the launch traced here: 877 us
  Pallas kernels  850 us (96%)
  local copies, waits for them, and re-layouts  17.9 us (2%)
    pallas_call x4, Pallas kernels, connect(): pl.pallas_call(kernel, in_specs=spaces, out_specs=out_spaces, out_shape=o...  790 us
    pallas_call x1, Pallas kernels, gate_up_grads(): pl.pallas_call(gate_up_grads_kernel, grid=(ZS,), in_specs=[pl.BlockSpec((...  27 us
  transfers between devices with their start and end apart: 1, of which 0 were waited for; matrix products, arithmetic and copies ran while one was open for 0% of the time, Pallas kernels for 37%

profile of v5, /device:TPU:0, one launch (start us, length us, event | category | flops | bytes accessed | tf_op | source)
XLA Modules:
  0.0 877.4 jit_solution(704091311339004767)
XLA Ops:
  0.7 0.1 add_multiply_fusion
  0.8 0.1 add_convert_fusion
  0.8 0.1 convert_element_type.91
  0.9 0.7 fusion.4
  1.6 0.8 pad_maximum_fusion.cosine
  2.4 0.7 fusion.20
  3.1 0.7 fusion.22
  3.8 0.7 fusion.21
  4.5 0.1 fusion.9
  4.6 0.1 fusion.15
  4.6 0.1 fusion.7
  4.7 0.7 slice_bitcast_fusion
  5.4 0.1 concatenate.9
  5.6 0.1 copy.46
  5.7 0.6 pad_bitcast_fusion.table
  6.3 0.8 pad_maximum_fusion.1.sine
  7.1 317.1 %shard_map.205 = (bf16[2,80,2048]{2,1,0:T(8,128)(2,1)}, f32[2,80,2048]{2,1,0:T(8,128)}, bf16[2,4,2,2,80,2048]{5,4,3,2,1,0:T(8,128)(2,1)}, bf16[2,4,2,2,80,2048]{...) custom-call(bf16[2,80,2048]{2,1,0:T(8,128)(2,1)} %tokens.3, ...), custom_call_target="tpu_custom_call" | custom-call | bytes 750000000 | tf_op jit(solution)/shard_map/pallas_call | solution.py:1889
  324.2 1.4 copy.47
  325.6 0.2 reshape.170
  325.9 0.1 convolution_convert_fusion
  326.1 2.2 fusion.1.select_back
  328.3 1.6 fusion.3.select
  329.8 0.6 select_reduce_fusion
  330.5 1.2 copy.49.gates
  331.7 178.7 %shard_map.206 = (bf16[2,80,2048]{2,1,0:T(8,128)(2,1)}, f32[2,80,2048]{2,1,0:T(8,128)}, f32[16,2048]{1,0:T(8,128)}, bf16[8,208,2048]{2,1,0:T(8,128)(2,1)}, bf16[...) custom-call(bf16[2,80,2048]{2,1,0:T(8,128)(2,1)} %get-tuple-element., ...), custom_call_target="tpu_custom_call" | custom-call | bytes 450000000 | tf_op jit(solution)/shard_map/pallas_call | solution.py:1889
  510.4 16.2 %shard_map.207 = (f32[1408,2048]{1,0:T(8,128)}, bf16[1408,2048]{1,0:T(8,128)(2,1)}) custom-call(bf16[1664,1408]{1,0:T(8,128)(2,1)} %bitcast.76, bf16[1664,2048]{1,0:T(8,128)(2,1)} %bitcast.74), custom_call_target="tpu_custom_call" | custom-call | flops 9596567552 | bytes 28835840 | tf_op jit(solution)/shard_map/pallas_call | solution.py:1822
  526.6 3.9 dynamic-slice_bitcast_fusion
  530.5 1.6 collective-permute-start
  532.1 27.0 %shard_map.208 = (bf16[4,2,256,1408]{3,2,1,0:T(8,128)(2,1)}, bf16[4,2,256,1408]{3,2,1,0:T(8,128)(2,1)}) custom-call(bf16[1664,2048]{1,0:T(8,128)(2,1)} %bitcast.73, bf16[1664,2816]{1,0:T(8,128)(2,1)} %bitcast.72), custom_call_target="tpu_custom_call" | custom-call | flops 19193135104 | bytes 34603008 | tf_op jit(solution)/shard_map/pallas_call | solution.py:1796
  559.2 157.2 %shard_map.209 = (bf16[2,80,2048]{2,1,0:T(8,128)(2,1)}, f32[16,2048]{1,0:T(8,128)}, bf16[8,320,2048]{2,1,0:T(8,128)(2,1)}, bf16[8,320,1536]{2,1,0:T(8,128)(2,1)}...) custom-call(bf16[2,80,2048]{2,1,0:T(8,128)(2,1)} %get-tuple-element.57.rows, ...), custom_call_target="tpu_custom_call" | custom-call | bytes 450000000 | tf_op jit(solution)/shard_map/pallas_call | solution.py:1889
  716.3 137.2 %shard_map.210 = (bf16[2,80,2048]{2,1,0:T(8,128)(2,1)}, f32[8,2048]{1,0:T(8,128)}, bf16[256,2048]{1,0:T(8,128)(2,1)}, bf16[64,4096]{1,0:T(8,128)(2,1)}, f32[256,2048]{1,0:T(8,128)}, /*index=5*/bf16[256,5632]{1,0:T(8,128)(2,1)}) custom-call(bf16[2,4,2,2,80,2048]{5,4,3,2,1,0:T(8,128)(2,1)} %bitcast.57, f32[2,80,2048]{2,1,0:T(8,128)} %get-tuple-element.55.middle, ...), custom_call_target="tpu_custom_call" | custom-call | bytes 300000000 | tf_op jit(solution)/shard_map/pallas_call | solution.py:1889
  853.6 0.8 slice.64
  854.4 0.1 reshape.182
  854.5 0.5 fusion.18
  855.0 0.0 collective-permute-done.refs_3_
  855.0 0.0 copy-start
  855.0 1.6 copy-done
  856.6 0.0 copy-start.2
  856.6 16.3 %shard_map.211 = (f32[256,11264]{1,0:T(8,128)}, f32[704,2048]{1,0:T(8,128)}, f32[64,4096]{1,0:T(8,128)}, f32[256,2048]{1,0:T(8,128)}) custom-call(s32[1]{0:T(128)} %bitcast.29.y, bf16[256,5632]{1,0:T(8,128)(2,1)} %get-tuple-element.80.refs_0_, bf16[256,5632]{1,0:T(8,128)(2,1)} %get-tuple-element.81.refs_1_, f32[2,704,2048]{2,1,0:T(8,128)} %bitcast.55, ...), custom_call_target="tpu_custom_call" | custom-call | bytes 34603008 | tf_op jit(solution)/shard_map/pallas_call | solution.py:1857
  872.9 0.0 copy-start.1
  872.9 2.1 copy.53
  875.0 0.0 copy-done.2
  875.0 0.8 copy.54
  875.9 0.0 copy-done.1
  875.9 1.3 copy.55
  (6 shorter events, 0.1 us)
Async XLA Ops:
  530.5 324.5 %collective-permute-start = (bf16[704,2048]{1,0:T(8,128)(2,1)}, bf16[704,2048]{1,0:T(8,128)(2,1)S(1)}, u32[]{:S(2)}, u32[]{:S(2)}) collective-permute-start(bf16[704,2048]{1,0:T(8,128)(2,1)} %dynamic-slice_bitcast_fusion), channel_id=1, source_target_pairs={{0,4},{4,0},{8,12},{12,8},{16,20},{20,16},{24,28},{28,24},{1,5},{5... | collective-permute-start | bytes 8650760 | tf_op jit(solution)/shard_map/ppermute | solution.py:396
  855.0 1.6 copy-start
  856.6 18.4 %copy-start.2 = (bf16[2,80,2048]{2,1,0:T(8,128)(2,1)S(1)}, bf16[2,80,2048]{2,1,0:T(8,128)(2,1)}, u32[]{:S(2)}) copy-start(bf16[2,80,2048]{2,1,0:T(8,128)(2,1)} %get-tuple-element.128) | copy-start | bytes 1966084
  872.9 3.0 copy-start.1

commit v6 on v5

--- a/solution.py
+++ b/solution.py
@@ -877,21 +877,23 @@
                     pl.when(self.beyond(down, far))(self.z_copy(m, down, far).wait_send)
 
 
-def piece_of(place, index, micro):
+def piece_of(place, index, outward=False):
     turn = lax.rem(index, ZS)
+    if outward:
+        turn = ZS - 1 - turn
     inner = turn + lax.div(turn, 2) * (5 - 2 * turn)
     last = lax.rem(ZS - turn, ZS)
     z = place.z
     return lax.div(index, ZS), jnp.where(z == 0, turn, jnp.where(z == ZS - 1, last, inner))
 
 
-def run_pieces(place, reduce, piece, between):
+def run_pieces(place, reduce, piece, between, outward=False):
     pieces = reduce.micro * ZS
 
     def step(index, carry):
         @pl.when(index < pieces)
         def _():
-            m, k = piece_of(place, index, reduce.micro)
+            m, k = piece_of(place, index, outward)
             piece(index, m, k)
             reduce.begin_piece(m, k)
 
@@ -899,14 +901,14 @@
 
         @pl.when((index >= 1) & (index < pieces + 1))
         def _():
-            reduce.x_piece(*piece_of(place, index - 1, reduce.micro))
+            reduce.x_piece(*piece_of(place, index - 1, outward))
 
         @pl.when((index >= 3) & (index < pieces + 3))
         def _():
-            reduce.z_piece(*piece_of(place, index - 3, reduce.micro))
+            reduce.z_piece(*piece_of(place, index - 3, outward))
 
         for m in range(reduce.micro):
-            first = (m + 1) * ZS + 2
+            first = m * ZS + 3 if outward else (m + 1) * ZS + 2
             for far in range(1, ZS):
                 pl.when(index == first + ZS - 1 - far)(functools.partial(reduce.chain, m, far))
         return carry
@@ -1256,7 +1258,7 @@
     for index in (0, 1, 3, 2):
         kv.hop_round(0, index)
     normed.x_round(0)
-    for step in (0, 1, 3, 2):
+    for step in (0, 1, 3):
         gate_up.send(step)
     gate_up.z_round(0)
     tables.z_round(2)
@@ -1280,8 +1282,9 @@
     tables.arrivals()
     for copy in late_loads:
         copy.start()
+    gate_up.send(2)
     down.begin()
-    run_pieces(place, reduce, piece, between)
+    run_pieces(place, reduce, piece, between, True)
     for m in range(reduce.micro):
         reduce.finish(m)
 
@@ -1543,7 +1546,7 @@
 
         @pl.when(index + 1 < pieces)
         def _():
-            for copy in loads_of(1, cotangents, upstream, *piece_of(place, index + 1, reduce.micro)):
+            for copy in loads_of(1, cotangents, upstream, *piece_of(place, index + 1)):
                 copy.start()
 
         stored(2, 3)
@@ -1835,19 +1838,20 @@
     )(hidden, down_grad)
 
 
-def widen_kernel(first, second, own, other, kv, query, weight_out, down_out, kv_out, query_out):
+def widen_kernel(first, second, own, other_first, other_last, kv, query, weight_out, down_out, kv_out, query_out):
     step = pl.program_id(0)
     pl.when(step < ZS)(lambda: weight_out.__setitem__(..., first[...].astype(F32)))
     pl.when(step >= ZS)(lambda: weight_out.__setitem__(..., second[...].astype(F32)))
-    down_out[...] = own[0] + other[...].astype(F32)
+    pl.when(step < ZS)(lambda: down_out.__setitem__(..., own[0] + other_first[...].astype(F32)))
+    pl.when(step >= ZS)(lambda: down_out.__setitem__(..., own[0] + other_last[...].astype(F32)))
     kv_out[...] = kv[...].astype(F32)
     query_out[...] = query[...].astype(F32)
 
 
-def widen(first, second, own, other, kv, query, y):
+def widen(first, second, own, other_first, other_last, kv, query, y):
     steps = 2 * ZS
     rows, width = first.shape[0], first.shape[1] // ZS
-    down_rows, model = other.shape
+    _, down_rows, model = own.shape
     down_step = down_rows // ZS
 
     def block(*dims):
@@ -1863,7 +1867,8 @@
                 pl.BlockSpec((rows, width), lambda i, y: (0, jnp.minimum(i, ZS - 1))),
                 pl.BlockSpec((rows, width), lambda i, y: (0, jnp.maximum(i - ZS, 0))),
                 pl.BlockSpec((1, down_step, model), lambda i, y: (y[0], i // 2, 0)),
-                block(down_step, model),
+                pl.BlockSpec((down_step, model), lambda i, y: (jnp.minimum(i // 2, ZS // 2 - 1), 0)),
+                pl.BlockSpec((down_step, model), lambda i, y: (jnp.maximum(i // 2 - ZS // 2, 0), 0)),
                 block(*small[0]),
                 block(*small[1]),
             ],
@@ -1876,13 +1881,13 @@
         ),
         out_shape=[
             jax.ShapeDtypeStruct((rows, steps * width), F32),
-            jax.ShapeDtypeStruct(other.shape, F32),
+            jax.ShapeDtypeStruct((down_rows, model), F32),
             jax.ShapeDtypeStruct(kv.shape, F32),
             jax.ShapeDtypeStruct(query.shape, F32),
         ],
         compiler_params=pltpu.CompilerParams(vmem_limit_bytes=60 << 20),
         cost_estimate=pl.CostEstimate(flops=0, bytes_accessed=12 * rows * steps * width, transcendentals=0),
-    )(jnp.full((1,), y, jnp.int32), first, second, own, other, kv, query)
+    )(jnp.full((1,), y, jnp.int32), first, second, own, other_first, other_last, kv, query)
 
 
 def connect(kernel, operands, spaces, out_shapes, out_spaces, scratch, number, seconds):
@@ -2091,8 +2096,10 @@
 
     grad_down, down_small = [value.reshape(YS, -1, model) for value in down_grads(hidden, down_grad)]
     down_small = take(down_small, 1 - y, 0)
-    rows_two, down_small = lax.optimization_barrier((rows_two, down_small))
-    down_small = y_move(down_small)
+    half = down_small.shape[0] // 2
+    down_first, down_last = down_small[:half], down_small[half:]
+    rows_two, down_first, down_last = lax.optimization_barrier((rows_two, down_first, down_last))
+    down_first = y_move(down_first)
     gate_grad, up_grad = gate_up_grads(rows_two, both_grad, model_rows)
     input_grad, gain_first, result_grad, qkv_grad, gate_grad, up_grad, _ = connect(
         attend_back_kernel,
@@ -2145,6 +2152,8 @@
         3,
         150e-6,
     )
+    down_last, input_grad = lax.optimization_barrier((down_last, input_grad))
+    down_last = y_move(down_last)
     rows = seqs * SEQ
     output, gains, query_grad, kv_grad, grad_out, up_grad = connect(
         last_kernel,
@@ -2188,7 +2197,7 @@
     devices = ZS * YS * XS * CS
     gains = take(gains[:2].reshape(2, devices, model // devices), group * XS * CS + owner, 1)
     grad_gate_up, grad_down, kv_grad, query_grad = widen(
-        gate_grad, up_grad, grad_down, down_small, kv_grad, query_grad, y
+        gate_grad, up_grad, grad_down, down_first, down_last, kv_grad, query_grad, y
     )
     return (
         output,

time: 883 us -> 875 us (level)
  transfers between devices with their start and end apart: 1 -> 2, of which waited for: 0 -> 0; matrix products, arithmetic and copies ran while one was open for 0% -> 0% of each run, Pallas kernels for 37% -> 16%
where the time goes in v6:
time: 875 us; the launch traced here: 867 us
  Pallas kernels  844 us (96%)
  local copies, waits for them, and re-layouts  13.3 us (2%)
    pallas_call x4, Pallas kernels, connect(): pl.pallas_call(kernel, in_specs=spaces, out_specs=out_spaces, out_shape=o...  784 us
    pallas_call x1, Pallas kernels, gate_up_grads(): pl.pallas_call(gate_up_grads_kernel, grid=(ZS,), in_specs=[pl.BlockSpec((...  27.1 us
  transfers between devices with their start and end apart: 2, of which 0 were waited for; matrix products, arithmetic and copies ran while one was open for 0% of the time, Pallas kernels for 16%

profile of v6, /device:TPU:0, one launch (start us, length us, event | category | flops | bytes accessed | tf_op | source)
XLA Modules:
  0.0 867.1 jit_solution(10871506516926435110)
XLA Ops:
  0.7 0.1 add_multiply_fusion
  0.8 0.1 add_convert_fusion
  0.8 0.1 convert_element_type.91
  0.9 0.7 fusion.4
  1.6 0.8 pad_maximum_fusion.cosine
  2.4 0.7 fusion.20
  3.1 0.7 fusion.22
  3.8 0.7 fusion.21
  4.5 0.1 fusion.9
  4.6 0.1 fusion.15
  4.6 0.1 fusion.7
  4.7 0.7 slice_bitcast_fusion
  5.4 0.1 concatenate.9
  5.6 0.1 copy.46
  5.7 0.6 pad_bitcast_fusion.table
  6.3 0.8 pad_maximum_fusion.1.sine
  7.1 316.2 %shard_map.205 = (bf16[2,80,2048]{2,1,0:T(8,128)(2,1)}, f32[2,80,2048]{2,1,0:T(8,128)}, bf16[2,4,2,2,80,2048]{5,4,3,2,1,0:T(8,128)(2,1)}, bf16[2,4,2,2,80,2048]{...) custom-call(bf16[2,80,2048]{2,1,0:T(8,128)(2,1)} %tokens.3, ...), custom_call_target="tpu_custom_call" | custom-call | bytes 750000000 | tf_op jit(solution)/shard_map/pallas_call | solution.py:1894
  323.3 1.4 copy.47
  324.7 0.2 reshape.172
  325.0 0.1 convolution_convert_fusion
  325.1 2.2 fusion.1.select_back
  327.3 1.6 fusion.3.select
  328.9 0.6 select_reduce_fusion
  329.5 1.2 copy.49.gates
  330.8 175.4 %shard_map.206 = (bf16[2,80,2048]{2,1,0:T(8,128)(2,1)}, f32[2,80,2048]{2,1,0:T(8,128)}, f32[16,2048]{1,0:T(8,128)}, bf16[8,208,2048]{2,1,0:T(8,128)(2,1)}, bf16[...) custom-call(bf16[2,80,2048]{2,1,0:T(8,128)(2,1)} %get-tuple-element., ...), custom_call_target="tpu_custom_call" | custom-call | bytes 450000000 | tf_op jit(solution)/shard_map/pallas_call | solution.py:1894
  506.1 16.2 %shard_map.207 = (f32[1408,2048]{1,0:T(8,128)}, bf16[1408,2048]{1,0:T(8,128)(2,1)}) custom-call(bf16[1664,1408]{1,0:T(8,128)(2,1)} %bitcast.78, bf16[1664,2048]{1,0:T(8,128)(2,1)} %bitcast.76), custom_call_target="tpu_custom_call" | custom-call | flops 9596567552 | bytes 28835840 | tf_op jit(solution)/shard_map/pallas_call | solution.py:1825
  522.4 2.0 dynamic-slice_bitcast_fusion
  524.4 27.1 %shard_map.208 = (bf16[4,2,256,1408]{3,2,1,0:T(8,128)(2,1)}, bf16[4,2,256,1408]{3,2,1,0:T(8,128)(2,1)}) custom-call(bf16[1664,2048]{1,0:T(8,128)(2,1)} %bitcast.75, bf16[1664,2816]{1,0:T(8,128)(2,1)} %bitcast.74), custom_call_target="tpu_custom_call" | custom-call | flops 19193135104 | bytes 34603008 | tf_op jit(solution)/shard_map/pallas_call | solution.py:1799
  551.4 155.5 %shard_map.209 = (bf16[2,80,2048]{2,1,0:T(8,128)(2,1)}, f32[16,2048]{1,0:T(8,128)}, bf16[8,320,2048]{2,1,0:T(8,128)(2,1)}, bf16[8,320,1536]{2,1,0:T(8,128)(2,1)}...) custom-call(bf16[2,80,2048]{2,1,0:T(8,128)(2,1)} %get-tuple-element.60.rows, ...), custom_call_target="tpu_custom_call" | custom-call | bytes 450000000 | tf_op jit(solution)/shard_map/pallas_call | solution.py:1894
  707.0 1.5 collective-permute-start.1
  708.5 0.6 collective-permute-start
  709.1 137.0 %shard_map.210 = (bf16[2,80,2048]{2,1,0:T(8,128)(2,1)}, f32[8,2048]{1,0:T(8,128)}, bf16[256,2048]{1,0:T(8,128)(2,1)}, bf16[64,4096]{1,0:T(8,128)(2,1)}, f32[256,2048]{1,0:T(8,128)}, /*index=5*/bf16[256,5632]{1,0:T(8,128)(2,1)}) custom-call(bf16[2,4,2,2,80,2048]{5,4,3,2,1,0:T(8,128)(2,1)} %bitcast.59, f32[2,80,2048]{2,1,0:T(8,128)} %get-tuple-element.58.middle, ...), custom_call_target="tpu_custom_call" | custom-call | bytes 300000000 | tf_op jit(solution)/shard_map/pallas_call | solution.py:1894
  846.1 0.8 slice.80
  847.0 0.1 reshape.184
  847.0 0.5 fusion.18
  847.6 0.0 collective-permute-done.1.refs_4_
  847.6 0.0 collective-permute-done.refs_3_
  847.6 0.0 copy-start.2
  847.6 0.0 copy-start.1
  847.6 16.1 %shard_map.211 = (f32[256,11264]{1,0:T(8,128)}, f32[704,2048]{1,0:T(8,128)}, f32[64,4096]{1,0:T(8,128)}, f32[256,2048]{1,0:T(8,128)}) custom-call(s32[1]{0:T(128)} %bitcast.30.y, bf16[256,5632]{1,0:T(8,128)(2,1)} %get-tuple-element.85.refs_0_, bf16[256,5632]{1,0:T(8,128)(2,1)} %get-tuple-element.86.refs_1_, f32[2,704,2048]{2,1,0:T(8,128)} %bitcast.57, ...), custom_call_target="tpu_custom_call" | custom-call | bytes 34603008 | tf_op jit(solution)/shard_map/pallas_call | solution.py:1861
  863.7 0.0 copy-start
  863.7 0.0 copy-done.2
  863.7 0.8 copy.53
  864.6 0.0 copy-done.1
  864.6 0.8 copy.54
  865.4 0.1 copy-done
  865.5 1.3 copy.55
  (6 shorter events, 0.1 us)
Async XLA Ops:
  707.0 140.6 %collective-permute-start.1 = (bf16[352,2048]{1,0:T(8,128)(2,1)S(1)}, bf16[352,2048]{1,0:T(8,128)(2,1)}, u32[]{:S(2)}, u32[]{:S(2)}) collective-permute-start(bf16[352,2048]{1,0:T(8,128)(2,1)S(1)} %get-tuple-element.89), channel_id=1, source_target_pairs={{0,4},{4,0},{8,12},{12,8},{16,20},{20,16},{24,28},{28,24},{1,5},{5... | collective-permute-start | bytes 4325384 | tf_op jit(solution)/shard_map/ppermute | solution.py:396
  708.5 139.0 %collective-permute-start = (bf16[352,2048]{1,0:T(8,128)(2,1)S(1)}, bf16[352,2048]{1,0:T(8,128)(2,1)}, u32[]{:S(2)}, u32[]{:S(2)}) collective-permute-start(bf16[352,2048]{1,0:T(8,128)(2,1)S(1)} %get-tuple-element.88), channel_id=1, source_target_pairs={{0,4},{4,0},{8,12},{12,8},{16,20},{20,16},{24,28},{28,24},{1,5},{5... | collective-permute-start | bytes 4325384 | tf_op jit(solution)/shard_map/ppermute | solution.py:396
  847.6 16.2 %copy-start.2 = (bf16[2,80,2048]{2,1,0:T(8,128)(2,1)S(1)}, bf16[2,80,2048]{2,1,0:T(8,128)(2,1)}, u32[]{:S(2)}) copy-start(bf16[2,80,2048]{2,1,0:T(8,128)(2,1)} %get-tuple-element.135) | copy-start | bytes 1966084
  847.6 17.0 %copy-start.1 = (bf16[2,80,2048]{2,1,0:T(8,128)(2,1)S(1)}, bf16[2,80,2048]{2,1,0:T(8,128)(2,1)}, u32[]{:S(2)}) copy-start(bf16[2,80,2048]{2,1,0:T(8,128)(2,1)} %get-tuple-element.136) | copy-start | bytes 1966084
  863.7 1.8 copy-start

commit v7 on v6

--- a/solution.py
+++ b/solution.py
@@ -1415,8 +1415,8 @@
 
     def pass_grads(part):
         y_copy(part).wait()
-        if part + 2 < 2 * ZS:
-            y_copy(part + 2).start()
+        if part + 4 < 2 * ZS:
+            y_copy(part + 4).start()
         own_copy(part).wait()
 
         def add(span):
@@ -1436,7 +1436,7 @@
     for part in range(2 * ZS):
         own_copy(part).start()
     place.enter(True)
-    for part in range(2):
+    for part in range(4):
         y_copy(part).start()
     begin_gathers([gather])
     run_pieces(place, reduce, piece, between)

time: 875 us -> 873 us (level)
  no operation moved by 1% of the time
where the time goes in v7:
time: 873 us; the launch traced here: 868 us
  Pallas kernels  844 us (97%)
  local copies, waits for them, and re-layouts  13.3 us (2%)
    pallas_call x4, Pallas kernels, connect(): pl.pallas_call(kernel, in_specs=spaces, out_specs=out_spaces, out_shape=o...  785 us
    pallas_call x1, Pallas kernels, gate_up_grads(): pl.pallas_call(gate_up_grads_kernel, grid=(ZS,), in_specs=[pl.BlockSpec((...  27.1 us
  transfers between devices with their start and end apart: 2, of which 0 were waited for; matrix products, arithmetic and copies ran while one was open for 0% of the time, Pallas kernels for 16%

profile of v7, /device:TPU:0, one launch (start us, length us, event | category | flops | bytes accessed | tf_op | source)
XLA Modules:
  0.0 868.0 jit_solution(4028327130802414415)
XLA Ops:
  0.7 0.1 add_multiply_fusion
  0.8 0.1 add_convert_fusion
  0.8 0.1 convert_element_type.91
  0.9 0.7 fusion.4
  1.6 0.8 pad_maximum_fusion.cosine
  2.4 0.7 fusion.20
  3.1 0.7 fusion.22
  3.8 0.7 fusion.21
  4.5 0.1 fusion.9
  4.6 0.1 fusion.15
  4.6 0.1 fusion.7
  4.7 0.7 slice_bitcast_fusion
  5.4 0.1 concatenate.9
  5.6 0.1 copy.46
  5.7 0.6 pad_bitcast_fusion.table
  6.3 0.8 pad_maximum_fusion.1.sine
  7.1 316.2 %shard_map.205 = (bf16[2,80,2048]{2,1,0:T(8,128)(2,1)}, f32[2,80,2048]{2,1,0:T(8,128)}, bf16[2,4,2,2,80,2048]{5,4,3,2,1,0:T(8,128)(2,1)}, bf16[2,4,2,2,80,2048]{...) custom-call(bf16[2,80,2048]{2,1,0:T(8,128)(2,1)} %tokens.3, ...), custom_call_target="tpu_custom_call" | custom-call | bytes 750000000 | tf_op jit(solution)/shard_map/pallas_call | solution.py:1894
  323.3 1.4 copy.47
  324.7 0.2 reshape.172
  325.0 0.1 convolution_convert_fusion
  325.1 2.2 fusion.1.select_back
  327.3 1.6 fusion.3.select
  328.9 0.6 select_reduce_fusion
  329.5 1.2 copy.49.gates
  330.8 175.4 %shard_map.206 = (bf16[2,80,2048]{2,1,0:T(8,128)(2,1)}, f32[2,80,2048]{2,1,0:T(8,128)}, f32[16,2048]{1,0:T(8,128)}, bf16[8,208,2048]{2,1,0:T(8,128)(2,1)}, bf16[...) custom-call(bf16[2,80,2048]{2,1,0:T(8,128)(2,1)} %get-tuple-element., ...), custom_call_target="tpu_custom_call" | custom-call | bytes 450000000 | tf_op jit(solution)/shard_map/pallas_call | solution.py:1894
  506.1 16.2 %shard_map.207 = (f32[1408,2048]{1,0:T(8,128)}, bf16[1408,2048]{1,0:T(8,128)(2,1)}) custom-call(bf16[1664,1408]{1,0:T(8,128)(2,1)} %bitcast.78, bf16[1664,2048]{1,0:T(8,128)(2,1)} %bitcast.76), custom_call_target="tpu_custom_call" | custom-call | flops 9596567552 | bytes 28835840 | tf_op jit(solution)/shard_map/pallas_call | solution.py:1825
  522.4 2.0 dynamic-slice_bitcast_fusion
  524.4 27.1 %shard_map.208 = (bf16[4,2,256,1408]{3,2,1,0:T(8,128)(2,1)}, bf16[4,2,256,1408]{3,2,1,0:T(8,128)(2,1)}) custom-call(bf16[1664,2048]{1,0:T(8,128)(2,1)} %bitcast.75, bf16[1664,2816]{1,0:T(8,128)(2,1)} %bitcast.74), custom_call_target="tpu_custom_call" | custom-call | flops 19193135104 | bytes 34603008 | tf_op jit(solution)/shard_map/pallas_call | solution.py:1799
  551.4 154.1 %shard_map.209 = (bf16[2,80,2048]{2,1,0:T(8,128)(2,1)}, f32[16,2048]{1,0:T(8,128)}, bf16[8,320,2048]{2,1,0:T(8,128)(2,1)}, bf16[8,320,1536]{2,1,0:T(8,128)(2,1)}...) custom-call(bf16[2,80,2048]{2,1,0:T(8,128)(2,1)} %get-tuple-element.60.rows, ...), custom_call_target="tpu_custom_call" | custom-call | bytes 450000000 | tf_op jit(solution)/shard_map/pallas_call | solution.py:1894
  705.6 0.7 collective-permute-start.1
  706.2 1.4 collective-permute-start
  707.6 139.4 %shard_map.210 = (bf16[2,80,2048]{2,1,0:T(8,128)(2,1)}, f32[8,2048]{1,0:T(8,128)}, bf16[256,2048]{1,0:T(8,128)(2,1)}, bf16[64,4096]{1,0:T(8,128)(2,1)}, f32[256,2048]{1,0:T(8,128)}, /*index=5*/bf16[256,5632]{1,0:T(8,128)(2,1)}) custom-call(bf16[2,4,2,2,80,2048]{5,4,3,2,1,0:T(8,128)(2,1)} %bitcast.59, f32[2,80,2048]{2,1,0:T(8,128)} %get-tuple-element.58.middle, ...), custom_call_target="tpu_custom_call" | custom-call | bytes 300000000 | tf_op jit(solution)/shard_map/pallas_call | solution.py:1894
  847.0 0.8 slice.80
  847.9 0.1 reshape.184
  848.0 0.5 fusion.18
  848.5 0.0 collective-permute-done.1.refs_4_
  848.5 0.0 collective-permute-done.refs_3_
  848.5 0.0 copy-start.2
  848.5 0.0 copy-start.1
  848.5 16.1 %shard_map.211 = (f32[256,11264]{1,0:T(8,128)}, f32[704,2048]{1,0:T(8,128)}, f32[64,4096]{1,0:T(8,128)}, f32[256,2048]{1,0:T(8,128)}) custom-call(s32[1]{0:T(128)} %bitcast.30.y, bf16[256,5632]{1,0:T(8,128)(2,1)} %get-tuple-element.85.refs_0_, bf16[256,5632]{1,0:T(8,128)(2,1)} %get-tuple-element.86.refs_1_, f32[2,704,2048]{2,1,0:T(8,128)} %bitcast.57, ...), custom_call_target="tpu_custom_call" | custom-call | bytes 34603008 | tf_op jit(solution)/shard_map/pallas_call | solution.py:1861
  864.6 0.0 copy-start
  864.6 0.0 copy-done.2
  864.6 0.8 copy.53
  865.5 0.0 copy-done.1
  865.5 0.8 copy.54
  866.3 0.1 copy-done
  866.5 1.3 copy.55
  (6 shorter events, 0.1 us)
Async XLA Ops:
  705.6 142.9 %collective-permute-start.1 = (bf16[352,2048]{1,0:T(8,128)(2,1)S(1)}, bf16[352,2048]{1,0:T(8,128)(2,1)}, u32[]{:S(2)}, u32[]{:S(2)}) collective-permute-start(bf16[352,2048]{1,0:T(8,128)(2,1)S(1)} %get-tuple-element.89), channel_id=1, source_target_pairs={{0,4},{4,0},{8,12},{12,8},{16,20},{20,16},{24,28},{28,24},{1,5},{5... | collective-permute-start | bytes 4325384 | tf_op jit(solution)/shard_map/ppermute | solution.py:396
  706.2 142.3 %collective-permute-start = (bf16[352,2048]{1,0:T(8,128)(2,1)S(1)}, bf16[352,2048]{1,0:T(8,128)(2,1)}, u32[]{:S(2)}, u32[]{:S(2)}) collective-permute-start(bf16[352,2048]{1,0:T(8,128)(2,1)S(1)} %get-tuple-element.88), channel_id=1, source_target_pairs={{0,4},{4,0},{8,12},{12,8},{16,20},{20,16},{24,28},{28,24},{1,5},{5... | collective-permute-start | bytes 4325384 | tf_op jit(solution)/shard_map/ppermute | solution.py:396
  848.5 16.2 %copy-start.2 = (bf16[2,80,2048]{2,1,0:T(8,128)(2,1)S(1)}, bf16[2,80,2048]{2,1,0:T(8,128)(2,1)}, u32[]{:S(2)}) copy-start(bf16[2,80,2048]{2,1,0:T(8,128)(2,1)} %get-tuple-element.135) | copy-start | bytes 1966084
  848.5 17.0 %copy-start.1 = (bf16[2,80,2048]{2,1,0:T(8,128)(2,1)S(1)}, bf16[2,80,2048]{2,1,0:T(8,128)(2,1)}, u32[]{:S(2)}) copy-start(bf16[2,80,2048]{2,1,0:T(8,128)(2,1)} %get-tuple-element.136) | copy-start | bytes 1966084
  864.6 1.8 copy-start
